TPU v7x, 32 devices: a whole 2x2x4 slice. The times are simulated.
32 devices in a mesh: replica: 2 (over y), shard: 16 (over z, x, core).
Axes of the slice: x: 2, y: 2, z: 4, core: 2. Of those that a mesh axis runs over, the one named last changes fastest.
Arguments:
- tokens: bfloat16 [320, 197, 384], P(('replica', 'shard')), may hold values from -6 to 6
- norm1_gain: bfloat16 [2, 384], P(None, 'shard'), may hold values from 0.5 to 1.5
- norm1_shift: bfloat16 [2, 384], P(None, 'shard'), may hold values from -3 to 3
- qkv_weight: bfloat16 [2, 384, 1152], P(None, 'shard'), may hold values from -0.3125 to 0.3125
- query_bias: bfloat16 [2, 384], P(None, 'shard'), may hold values from -3 to 3
- value_bias: bfloat16 [2, 384], P(None, 'shard'), may hold values from -3 to 3
- proj_weight: bfloat16 [2, 384, 384], P(None, 'shard'), may hold values from -1.25 to 1.25
- proj_bias: bfloat16 [2, 384], P(None, 'shard'), may hold values from -3 to 3
- norm2_gain: bfloat16 [2, 384], P(None, 'shard'), may hold values from 0.5 to 1.5
- norm2_shift: bfloat16 [2, 384], P(None, 'shard'), may hold values from -3 to 3
- fc1_weight: bfloat16 [2, 384, 1536], P(None, 'shard'), may hold values from -0.3125 to 0.3125
- fc1_bias: bfloat16 [2, 1536], P(None, 'shard'), may hold values from -3 to 3
- fc2_weight: bfloat16 [2, 1536, 384], P(None, 'shard'), may hold values from -0.15625 to 0.15625
- fc2_bias: bfloat16 [2, 384], P(None, 'shard'), may hold values from -3 to 3
- cotangent: bfloat16 [320, 197, 384], P(('replica', 'shard')), may hold values from -6 to 6
Outputs:
- layer_one: float32 [320, 197, 384], P(('replica', 'shard'))
- layer_two: float32 [320, 197, 384], P(('replica', 'shard'))
- tokens_grad: float32 [320, 197, 384], P(('replica', 'shard'))
- norm1_gain_grad: float32 [2, 384], P(None, 'shard')
- norm1_shift_grad: float32 [2, 384], P(None, 'shard')
- qkv_weight_grad: float32 [2, 384, 1152], P(None, 'shard')
- query_bias_grad: float32 [2, 384], P(None, 'shard')
- value_bias_grad: float32 [2, 384], P(None, 'shard')
- proj_weight_grad: float32 [2, 384, 384], P(None, 'shard')
- proj_bias_grad: float32 [2, 384], P(None, 'shard')
- norm2_gain_grad: float32 [2, 384], P(None, 'shard')
- norm2_shift_grad: float32 [2, 384], P(None, 'shard')
- fc1_weight_grad: float32 [2, 384, 1536], P(None, 'shard')
- fc1_bias_grad: float32 [2, 1536], P(None, 'shard')
- fc2_weight_grad: float32 [2, 1536, 384], P(None, 'shard')
- fc2_bias_grad: float32 [2, 384], P(None, 'shard')
All inputs are finite; a program needn't handle non-finite values.
Results may differ from a plain program's by a relative error of at most 0.02.
Values may be sent and summed in bfloat16 or wider, within the bound.
No kernel may reach another device: no remote copies, remote signals or barrier semaphores. Data moves between devices by JAX's collectives and lax.ppermute only.
A program may use at most 256 MiB of HBM per device.

v0:
```python
import jax
import jax.numpy as jnp
from jax import lax
from jax.sharding import PartitionSpec as P

HEADS = 6


EPS = 1e-06


def layer_norm(values, gain_row, shift_row):
    average = jnp.mean(values, -1, keepdims=True)
    centred = values - average
    spread = jnp.mean(centred * centred, -1, keepdims=True)
    return centred * lax.rsqrt(spread + EPS) * gain_row + shift_row


def gelu_exact(values):
    return jax.nn.gelu(values, approximate=False)


def matmul(left, right):
    return jnp.dot(left, right, preferred_element_type=jnp.float32)


def left_product(left, right):
    return jnp.einsum("nf,nd->fd", left, right, preferred_element_type=jnp.float32)


def right_product(left, right):
    return jnp.einsum("nd,fd->nf", left, right, preferred_element_type=jnp.float32)


def split_heads(mixed):
    images, length, triple = mixed.shape
    width = triple // 3
    head_dim = width // HEADS
    query_heads = mixed[..., :width].reshape(images, length, HEADS, head_dim)
    key_heads = mixed[..., width : 2 * width].reshape(images, length, HEADS, head_dim)
    value_heads = mixed[..., 2 * width :].reshape(images, length, HEADS, head_dim)
    return (query_heads, key_heads, value_heads)


def attend(mixed):
    images, length, triple = mixed.shape
    query_heads, key_heads, value_heads = split_heads(mixed)
    factor = query_heads.shape[-1] ** (-0.5)
    scores = (
        jnp.einsum("bqhd,bkhd->bhqk", query_heads, key_heads, preferred_element_type=jnp.float32)
        * factor
    )
    largest = jnp.max(scores, -1, keepdims=True)
    expo = jnp.exp(scores - largest)
    total = jnp.sum(expo, -1, keepdims=True)
    probs = expo / total
    attended = jnp.einsum(
        "bhqk,bkhd->bqhd",
        probs.astype(jnp.bfloat16),
        value_heads,
        preferred_element_type=jnp.float32,
    )
    return (
        attended.reshape(images, length, triple // 3).astype(jnp.bfloat16),
        largest + jnp.log(total),
    )


def attend_back(mixed, log_total, grad_out):
    images, length, triple = mixed.shape
    width = triple // 3
    query_heads, key_heads, value_heads = split_heads(mixed)
    head_dim = query_heads.shape[-1]
    factor = head_dim ** (-0.5)
    scores = (
        jnp.einsum("bqhd,bkhd->bhqk", query_heads, key_heads, preferred_element_type=jnp.float32)
        * factor
    )
    probs = jnp.exp(scores - log_total)
    grad_heads = grad_out.reshape(images, length, HEADS, head_dim)
    grad_value = jnp.einsum(
        "bhqk,bqhd->bkhd",
        probs.astype(jnp.bfloat16),
        grad_heads,
        preferred_element_type=jnp.float32,
    )
    grad_probs = jnp.einsum(
        "bqhd,bkhd->bhqk", grad_heads, value_heads, preferred_element_type=jnp.float32
    )
    inner = jnp.sum(probs * grad_probs, -1, keepdims=True)
    grad_scores = (probs * (grad_probs - inner)).astype(jnp.bfloat16)
    grad_query = (
        jnp.einsum("bhqk,bkhd->bqhd", grad_scores, key_heads, preferred_element_type=jnp.float32)
        * factor
    )
    grad_key = (
        jnp.einsum("bhqk,bqhd->bkhd", grad_scores, query_heads, preferred_element_type=jnp.float32)
        * factor
    )
    return jnp.concatenate(
        [
            grad_query.reshape(images * length, width),
            grad_key.reshape(images * length, width),
            grad_value.reshape(images * length, width),
        ],
        -1,
    )


def forward_layer(inputs, weights):
    (
        gain_one,
        shift_one,
        w_qkv,
        bias_query,
        bias_value,
        w_proj,
        bias_proj,
        gain_two,
        shift_two,
        w_up,
        bias_up,
        w_down,
        bias_down,
    ) = weights
    images, length, width = inputs.shape
    flat_in = inputs.reshape(images * length, width)
    normed = layer_norm(
        flat_in, gain_one.astype(jnp.float32), shift_one.astype(jnp.float32)
    ).astype(jnp.bfloat16)
    qkv_bias = jnp.concatenate(
        [
            bias_query.astype(jnp.float32),
            jnp.zeros((width,), jnp.float32),
            bias_value.astype(jnp.float32),
        ]
    )
    mixed = (
        (matmul(normed, w_qkv) + qkv_bias).astype(jnp.bfloat16).reshape(images, length, 3 * width)
    )
    attended, log_total = attend(mixed)
    middle = (
        flat_in
        + matmul(attended.reshape(images * length, width), w_proj)
        + bias_proj.astype(jnp.float32)
    )
    normed_two = layer_norm(
        middle, gain_two.astype(jnp.float32), shift_two.astype(jnp.float32)
    ).astype(jnp.bfloat16)
    hidden = matmul(normed_two, w_up) + bias_up.astype(jnp.float32)
    active = gelu_exact(hidden).astype(jnp.bfloat16)
    output = middle + matmul(active, w_down) + bias_down.astype(jnp.float32)
    kept = (flat_in, mixed, attended, log_total, middle, hidden)
    return (output.reshape(images, length, width), kept)


def backward_layer(grad_out, kept, weights):
    (
        gain_one,
        shift_one,
        w_qkv,
        bias_query,
        bias_value,
        w_proj,
        bias_proj,
        gain_two,
        shift_two,
        w_up,
        bias_up,
        w_down,
        bias_down,
    ) = weights
    flat_in, mixed, attended, log_total, middle, hidden = kept
    images, length, triple = mixed.shape
    width = triple // 3
    grad_down = grad_out.astype(jnp.bfloat16)
    active = gelu_exact(hidden).astype(jnp.bfloat16)
    g_w_down = left_product(active, grad_down)
    g_b_down = jnp.sum(grad_down.astype(jnp.float32), 0)
    grad_active = right_product(grad_down, w_down)
    hidden_pull = jax.vjp(gelu_exact, hidden)[1]
    grad_hidden = hidden_pull(grad_active)[0].astype(jnp.bfloat16)
    g_b_up = jnp.sum(grad_hidden.astype(jnp.float32), 0)
    normed_two, norm_pull_two = jax.vjp(
        layer_norm, middle, gain_two.astype(jnp.float32), shift_two.astype(jnp.float32)
    )
    g_w_up = left_product(normed_two.astype(jnp.bfloat16), grad_hidden)
    grad_mid, g_gain_two, g_shift_two = norm_pull_two(right_product(grad_hidden, w_up))
    grad_middle = grad_out + grad_mid
    grad_branch = grad_middle.astype(jnp.bfloat16)
    g_b_proj = jnp.sum(grad_branch.astype(jnp.float32), 0)
    g_w_proj = left_product(attended.reshape(images * length, width), grad_branch)
    grad_attended = right_product(grad_branch, w_proj).astype(jnp.bfloat16)
    grad_mixed = attend_back(mixed, log_total, grad_attended.reshape(images, length, width)).astype(
        jnp.bfloat16
    )
    g_b_query = jnp.sum(grad_mixed[:, :width].astype(jnp.float32), 0)
    g_b_value = jnp.sum(grad_mixed[:, 2 * width :].astype(jnp.float32), 0)
    normed, norm_pull_one = jax.vjp(
        layer_norm, flat_in, gain_one.astype(jnp.float32), shift_one.astype(jnp.float32)
    )
    g_w_qkv = left_product(normed.astype(jnp.bfloat16), grad_mixed)
    grad_first, g_gain_one, g_shift_one = norm_pull_one(right_product(grad_mixed, w_qkv))
    gradients = [
        g_gain_one,
        g_shift_one,
        g_w_qkv,
        g_b_query,
        g_b_value,
        g_w_proj,
        g_b_proj,
        g_gain_two,
        g_shift_two,
        g_w_up,
        g_b_up,
        g_w_down,
        g_b_down,
    ]
    return (grad_middle + grad_first, gradients)


def body(
    tokens,
    norm1_gain,
    norm1_shift,
    qkv_weight,
    query_bias,
    value_bias,
    proj_weight,
    proj_bias,
    norm2_gain,
    norm2_shift,
    fc1_weight,
    fc1_bias,
    fc2_weight,
    fc2_bias,
    cotangent,
):
    images, length, width = tokens.shape
    current = tokens.astype(jnp.float32)
    gathered = []
    kept_all = []
    outputs = []
    for layer_index in range(2):
        weights = (
            lax.all_gather(norm1_gain[layer_index], "shard", axis=0, tiled=True),
            lax.all_gather(norm1_shift[layer_index], "shard", axis=0, tiled=True),
            lax.all_gather(qkv_weight[layer_index], "shard", axis=0, tiled=True),
            lax.all_gather(query_bias[layer_index], "shard", axis=0, tiled=True),
            lax.all_gather(value_bias[layer_index], "shard", axis=0, tiled=True),
            lax.all_gather(proj_weight[layer_index], "shard", axis=0, tiled=True),
            lax.all_gather(proj_bias[layer_index], "shard", axis=0, tiled=True),
            lax.all_gather(norm2_gain[layer_index], "shard", axis=0, tiled=True),
            lax.all_gather(norm2_shift[layer_index], "shard", axis=0, tiled=True),
            lax.all_gather(fc1_weight[layer_index], "shard", axis=0, tiled=True),
            lax.all_gather(fc1_bias[layer_index], "shard", axis=0, tiled=True),
            lax.all_gather(fc2_weight[layer_index], "shard", axis=0, tiled=True),
            lax.all_gather(fc2_bias[layer_index], "shard", axis=0, tiled=True),
        )
        gathered.append(weights)
        current, kept = forward_layer(current, weights)
        outputs.append(current)
        kept_all.append(kept)
    grad_current = cotangent.astype(jnp.float32).reshape(images * length, width)
    layer_grads = [None, None]
    for layer_index in (1, 0):
        weights = (
            lax.all_gather(norm1_gain[layer_index], "shard", axis=0, tiled=True),
            lax.all_gather(norm1_shift[layer_index], "shard", axis=0, tiled=True),
            lax.all_gather(qkv_weight[layer_index], "shard", axis=0, tiled=True),
            lax.all_gather(query_bias[layer_index], "shard", axis=0, tiled=True),
            lax.all_gather(value_bias[layer_index], "shard", axis=0, tiled=True),
            lax.all_gather(proj_weight[layer_index], "shard", axis=0, tiled=True),
            lax.all_gather(proj_bias[layer_index], "shard", axis=0, tiled=True),
            lax.all_gather(norm2_gain[layer_index], "shard", axis=0, tiled=True),
            lax.all_gather(norm2_shift[layer_index], "shard", axis=0, tiled=True),
            lax.all_gather(fc1_weight[layer_index], "shard", axis=0, tiled=True),
            lax.all_gather(fc1_bias[layer_index], "shard", axis=0, tiled=True),
            lax.all_gather(fc2_weight[layer_index], "shard", axis=0, tiled=True),
            lax.all_gather(fc2_bias[layer_index], "shard", axis=0, tiled=True),
        )
        grad_current, gradients = backward_layer(grad_current, kept_all[layer_index], weights)
        gradients = (
            lax.psum(
                lax.psum_scatter(
                    gradients[0].astype(jnp.bfloat16), "shard", scatter_dimension=0, tiled=True
                ),
                "replica",
            ).astype(jnp.float32),
            lax.psum(
                lax.psum_scatter(
                    gradients[1].astype(jnp.bfloat16), "shard", scatter_dimension=0, tiled=True
                ),
                "replica",
            ).astype(jnp.float32),
            lax.psum(
                lax.psum_scatter(
                    gradients[2].astype(jnp.bfloat16), "shard", scatter_dimension=0, tiled=True
                ),
                "replica",
            ).astype(jnp.float32),
            lax.psum(
                lax.psum_scatter(
                    gradients[3].astype(jnp.bfloat16), "shard", scatter_dimension=0, tiled=True
                ),
                "replica",
            ).astype(jnp.float32),
            lax.psum(
                lax.psum_scatter(
                    gradients[4].astype(jnp.bfloat16), "shard", scatter_dimension=0, tiled=True
                ),
                "replica",
            ).astype(jnp.float32),
            lax.psum(
                lax.psum_scatter(
                    gradients[5].astype(jnp.bfloat16), "shard", scatter_dimension=0, tiled=True
                ),
                "replica",
            ).astype(jnp.float32),
            lax.psum(
                lax.psum_scatter(
                    gradients[6].astype(jnp.bfloat16), "shard", scatter_dimension=0, tiled=True
                ),
                "replica",
            ).astype(jnp.float32),
            lax.psum(
                lax.psum_scatter(
                    gradients[7].astype(jnp.bfloat16), "shard", scatter_dimension=0, tiled=True
                ),
                "replica",
            ).astype(jnp.float32),
            lax.psum(
                lax.psum_scatter(
                    gradients[8].astype(jnp.bfloat16), "shard", scatter_dimension=0, tiled=True
                ),
                "replica",
            ).astype(jnp.float32),
            lax.psum(
                lax.psum_scatter(
                    gradients[9].astype(jnp.bfloat16), "shard", scatter_dimension=0, tiled=True
                ),
                "replica",
            ).astype(jnp.float32),
            lax.psum(
                lax.psum_scatter(
                    gradients[10].astype(jnp.bfloat16), "shard", scatter_dimension=0, tiled=True
                ),
                "replica",
            ).astype(jnp.float32),
            lax.psum(
                lax.psum_scatter(
                    gradients[11].astype(jnp.bfloat16), "shard", scatter_dimension=0, tiled=True
                ),
                "replica",
            ).astype(jnp.float32),
            lax.psum(
                lax.psum_scatter(
                    gradients[12].astype(jnp.bfloat16), "shard", scatter_dimension=0, tiled=True
                ),
                "replica",
            ).astype(jnp.float32),
        )
        layer_grads[layer_index] = gradients
    stacked = [
        jnp.stack([first_grad, second_grad])
        for first_grad, second_grad in zip(layer_grads[0], layer_grads[1])
    ]
    return (
        outputs[0],
        outputs[1],
        grad_current.reshape(images, length, width),
        stacked[0],
        stacked[1],
        stacked[2],
        stacked[3],
        stacked[4],
        stacked[5],
        stacked[6],
        stacked[7],
        stacked[8],
        stacked[9],
        stacked[10],
        stacked[11],
        stacked[12],
    )


def solution(mesh):
    in_specs = (
        P(("replica", "shard"), None, None),
        P(None, "shard"),
        P(None, "shard"),
        P(None, "shard", None),
        P(None, "shard"),
        P(None, "shard"),
        P(None, "shard", None),
        P(None, "shard"),
        P(None, "shard"),
        P(None, "shard"),
        P(None, "shard", None),
        P(None, "shard"),
        P(None, "shard", None),
        P(None, "shard"),
        P(("replica", "shard"), None, None),
    )
    out_specs = (
        P(("replica", "shard"), None, None),
        P(("replica", "shard"), None, None),
        P(("replica", "shard"), None, None),
        P(None, "shard"),
        P(None, "shard"),
        P(None, "shard", None),
        P(None, "shard"),
        P(None, "shard"),
        P(None, "shard", None),
        P(None, "shard"),
        P(None, "shard"),
        P(None, "shard"),
        P(None, "shard", None),
        P(None, "shard"),
        P(None, "shard", None),
        P(None, "shard"),
    )
    return jax.shard_map(body, mesh=mesh, in_specs=in_specs, out_specs=out_specs, check_vma=False)
```

profile of v0, /device:TPU:0, one launch (start us, length us, event | category | flops | bytes accessed | tf_op | source)
XLA Modules:
  0.0 1069.2 jit_solution(11431475563173901419)
XLA Ops:
  24.9 63.2 %all-reduce.41 = (bf16[384]{0:T(512)(128)(2,1)S(1)}, bf16[384]{0:T(512)(128)(2,1)S(1)}, bf16[384]{0:T(512)(128)(2,1)S(1)}, bf16[384]{0:T(512)(128)(2,1)S(1)}, bf...) all-reduce(bf16[384]{0:T(512)(128)(2,1)S(1)} %dynamic-update-slice., ...), channel_id=6, replica_groups=mesh['replica'=2,'shard'=16] {'shard'}, use_global_device_ids=true, to_apply=%add.3 | all-reduce | flops 8832 | bytes 35328
  88.9 20.5 %all-gather.2 = bf16[1,384,1152]{2,1,0:T(8,128)(2,1)S(1)} all-gather(bf16[1,24,1152]{2,1,0:T(8,128)(2,1)S(1)} %get-tuple-element.119), channel_id=4, replica_groups=mesh['replica'=2,'shard'=16] {'shard'}, dimensions={1}, use_global_device_ids=true | all-gather | bytes 940032 | tf_op jit(solution)/shard_map/all_gather | solution.py:248
  157.7 19.8 %all-gather.5 = bf16[1,384,384]{2,1,0:T(8,128)(2,1)S(1)} all-gather(bf16[1,24,384]{2,1,0:T(8,128)(2,1)S(1)} %get-tuple-element.121), channel_id=7, replica_groups=mesh['replica'=2,'shard'=16] {'shard'}, dimensions={1}, use_global_device_ids=true | all-gather | bytes 313344 | tf_op jit(solution)/shard_map/all_gather | solution.py:251
  183.0 21.5 %all-gather.15 = bf16[1,384,1152]{2,1,0:T(8,128)(2,1)} all-gather(bf16[1,24,1152]{2,1,0:T(8,128)(2,1)S(1)} %get-tuple-element.118), channel_id=17, replica_groups=mesh['replica'=2,'shard'=16] {'shard'}, dimensions={1}, use_global_device_ids=true | all-gather | bytes 940032 | tf_op jit(solution)/shard_map/all_gather | solution.py:248
  205.0 21.2 %all-gather.18 = bf16[1,384,384]{2,1,0:T(8,128)(2,1)} all-gather(bf16[1,24,384]{2,1,0:T(8,128)(2,1)S(1)} %get-tuple-element.120), channel_id=20, replica_groups=mesh['replica'=2,'shard'=16] {'shard'}, dimensions={1}, use_global_device_ids=true | all-gather | bytes 313344 | tf_op jit(solution)/shard_map/all_gather | solution.py:251
  234.6 32.9 %multiply_convert_fusion.3 = (bf16[1970,1536]{1,0:T(8,128)(2,1)}, f32[1970,1536]{1,0:T(8,128)}, f32[1970,1536]{1,0:T(8,128)}) fusion(f32[1536]{0:T(1024)S(1)} %convert_element_type.340, bf16[1,384,1536]{2,1,0:T(8,128)(2,1)} %all-gather.31.cloned.1.call-done, f32[1970,384]{1,0:T(8,128)S(1)} %copy-done.11, f32[384]{0:T(512)S(1)} %convert_element_type.339, ...), kind=kOutput, calls=%fused_computation.29 | convolution fusion | flops 2527399680 | bytes 34489744 | tf_op jit(solution)/shard_map/dot_general | solution.py:24
  329.4 33.5 %multiply_convert_fusion.2 = (bf16[1970,1536]{1,0:T(8,128)(2,1)}, f32[1970,1536]{1,0:T(8,128)}, f32[1970,1536]{1,0:T(8,128)}) fusion(f32[1536]{0:T(1024)S(1)} %copy-done.68, bf16[1,384,1536]{2,1,0:T(8,128)(2,1)} %all-gather.35.cloned.1.call-done, f32[1970,384]{1,0:T(8,128)} %copy-done.13, f32[384]{0:T(512)S(1)} %copy-done.83, f32[384]{0:T(512)S(1)} %copy-done.74, ...), kind=kOutput, calls=%fused_computation.16 | convolution fusion | flops 2527399680 | bytes 34489744 | tf_op jit(solution)/shard_map/dot_general | solution.py:24
  363.0 15.5 %fusion.95 = (bf16[1536]{0:T(1024)(128)(2,1)}, bf16[1970,1536]{1,0:T(8,128)(2,1)}) fusion(f32[1970,1536]{1,0:T(8,128)} %get-tuple-element.105, bf16[1970,384]{1,0:T(8,128)(2,1)S(1)} %copy-done.21, bf16[1,1536,384]{2,1,0:T(8,128)(2,1)} %all-gather.37.cloned.1.call-done, f32[1970,1536]{1,0:T(8,128)} %get-tuple-element.155, f32[1536]{0:T(1024)S(1)} %copy-done.68), kind=kOutput, calls=%fused_computation.244 | convolution fusion | flops 2372319744 | bytes 32961024 | tf_op jit(solution)/shard_map/nd,fd->nf/dot_general | solution.py:32
  399.3 8.5 fusion.93
  407.8 9.0 multiply_reduce_fusion.1
  467.1 16.1 %fusion.96 = (bf16[1536]{0:T(1024)(128)(2,1)S(1)}, bf16[1970,1536]{1,0:T(8,128)(2,1)}) fusion(f32[1970,1536]{1,0:T(8,128)} %get-tuple-element.107, bf16[1,1536,384]{2,1,0:T(8,128)(2,1)S(1)} %copy-done.101, f32[1970,384]{1,0:T(8,128)S(1)} %get-tuple-element.93, f32[1970,1536]{1,0:T(8,128)} %get-tuple-element.148, f32[1536]{0:T(1024)S(1)} %copy-done.67), kind=kOutput, calls=%fused_computation.245 | convolution fusion | flops 2373076224 | bytes 34473984 | tf_op jit(solution)/shard_map/nd,fd->nf/dot_general | solution.py:32
  507.9 9.3 fusion.94
  517.2 8.9 multiply_reduce_fusion
  533.6 9.8 multiply_convert_fusion
  599.1 9.0 multiply_reduce_fusion.8
  608.5 57.9 %all-reduce.40 = (bf16[384]{0:T(512)(128)(2,1)S(1)}, bf16[384]{0:T(512)(128)(2,1)S(1)}, bf16[384]{0:T(512)(128)(2,1)S(1)}, bf16[384]{0:T(512)(128)(2,1)S(1)}, bf...) all-reduce(bf16[384]{0:T(512)(128)(2,1)S(1)} %copy-done.99, ...), channel_id=27, replica_groups=mesh['replica'=2,'shard'=16] {'shard'}, use_global_device_ids=true, to_apply=%add.17 | all-reduce | flops 9600 | bytes 38400
  671.9 29.0 %reduce-scatter.27.cloned.1.call-done = bf16[24,1152]{1,0:T(8,128)(2,1)} async-done(((bf16[384,1152]{1,0:T(8,128)(2,1)}), bf16[24,1152]{1,0:T(8,128)(2,1)}) %reduce-scatter.27.cloned.1.call-update) | async-done | bytes 55312
  700.9 58.9 %reduce-scatter.25.cloned.1.call-done = bf16[24,1152]{1,0:T(8,128)(2,1)} async-done(((bf16[384,1152]{1,0:T(8,128)(2,1)}), bf16[24,1152]{1,0:T(8,128)(2,1)}) %reduce-scatter.25.cloned.1.call-update) | async-done | bytes 55312
  775.4 8.1 convolution_convert_fusion.1
  827.4 24.0 %reduce-scatter.17.cloned.1.call-done = bf16[24,1536]{1,0:T(8,128)(2,1)} async-done(((bf16[384,1536]{1,0:T(8,128)(2,1)}), bf16[24,1536]{1,0:T(8,128)(2,1)}) %reduce-scatter.17.cloned.1.call-update) | async-done | bytes 73744 | tf_op jit(solution)/shard_map/reduce_scatter | solution.py:339
  851.4 60.7 %reduce-scatter.19.cloned.1.call-done = bf16[24,1536]{1,0:T(8,128)(2,1)} async-done(((bf16[384,1536]{1,0:T(8,128)(2,1)}), bf16[24,1536]{1,0:T(8,128)(2,1)}) %reduce-scatter.19.cloned.1.call-update) | async-done | bytes 73744 | tf_op jit(solution)/shard_map/reduce_scatter | solution.py:339
  912.1 60.6 %reduce-scatter.21.cloned.1.call-done = bf16[96,384]{1,0:T(8,128)(2,1)} async-done(((bf16[1536,384]{1,0:T(8,128)(2,1)}), bf16[96,384]{1,0:T(8,128)(2,1)}) %reduce-scatter.21.cloned.1.call-update) | async-done | bytes 73744 | tf_op jit(solution)/shard_map/reduce_scatter | solution.py:351
  972.7 60.7 %reduce-scatter.23.cloned.1.call-done = bf16[96,384]{1,0:T(8,128)(2,1)} async-done(((bf16[1536,384]{1,0:T(8,128)(2,1)}), bf16[96,384]{1,0:T(8,128)(2,1)}) %reduce-scatter.23.cloned.1.call-update) | async-done | bytes 73744 | tf_op jit(solution)/shard_map/reduce_scatter | solution.py:351
  1036.2 22.8 %all-reduce.49.cloned.1.call-done = (bf16[1,24,1536]{2,1,0:T(8,128)(2,1)}, bf16[1,24,1536]{2,1,0:T(8,128)(2,1)}, bf16[1,96,384]{2,1,0:T(8,128)(2,1)}, bf16[1,96,384]{2,1,0:T(8,128)(2,1)}) async-done(((bf16[1,24,1536]{2,1,0:T(8,128)(2,1)}, bf16[1,24,1536]{2,1,0:T(8,128)(2,1)}, bf16[1,96,384]{2,1,0:T(8,128)(2,1)}, bf16[1,96,384]{2,1,0:T(8,128)(2,1)}), (bf16[1,24,1536]{2,1,0:T(8,128)(2,1)}, ...) | async-done | bytes 294928 | tf_op jit(solution)/shard_map/psum | solution.py:338
  (454 shorter events, 369.2 us)
Async XLA Ops:
  7.2 227.5 %all-gather.31.cloned.1.call-start = ((), (), s32[]{:S(2)}) async-start(), calls=%async_computation.12 | async-start | bytes 1253376 | tf_op jit(solution)/shard_map/all_gather | solution.py:255
  8.8 258.8 %all-gather.33.cloned.1.call-start = ((), (), s32[]{:S(2)}) async-start(), calls=%async_computation.13 | async-start | bytes 1253376 | tf_op jit(solution)/shard_map/all_gather | solution.py:257
  10.5 318.8 %all-gather.35.cloned.1.call-start = ((), (), s32[]{:S(2)}) async-start(), calls=%async_computation.14 | async-start | bytes 1253376 | tf_op jit(solution)/shard_map/all_gather | solution.py:255
  11.3 351.7 %all-gather.37.cloned.1.call-start = ((), (), s32[]{:S(2)}) async-start(), calls=%async_computation.15 | async-start | bytes 1253376 | tf_op jit(solution)/shard_map/all_gather | solution.py:257
  11.8 660.1 %reduce-scatter.29.cloned.1.call-start = ((), (), s32[]{:S(2)}) async-start(), calls=%async_computation.18 | async-start | bytes 313344
  13.8 75.1 %copy-start.41 = (bf16[2,24,1152]{2,1,0:T(8,128)(2,1)S(1)}, bf16[2,24,1152]{2,1,0:T(8,128)(2,1)}, u32[]{:S(2)}) copy-start(bf16[2,24,1152]{2,1,0:T(8,128)(2,1)} %param.18) | copy-start | bytes 331780
  15.6 162.0 %copy-start.8 = (f32[1970,384]{1,0:T(8,128)}, f32[1970,384]{1,0:T(8,128)S(1)}, u32[]{:S(2)}) copy-start(f32[1970,384]{1,0:T(8,128)S(1)} %reshape.291) | copy-start | bytes 9077764
  19.0 96.3 %copy-start.55 = (f32[1970]{0:T(1024)}, f32[1970]{0:T(1024)S(1)}, u32[]{:S(2)}) copy-start(f32[1970]{0:T(1024)S(1)} %div.99) | copy-start | bytes 23644
  182.9 84.7 %copy-start.59 = (f32[1970]{0:T(1024)}, f32[1970]{0:T(1024)S(1)}, u32[]{:S(2)}) copy-start(f32[1970]{0:T(1024)S(1)} %fusion.62) | copy-start | bytes 23644
  182.9 84.7 %copy-start.72 = (f32[384]{0:T(512)}, f32[384]{0:T(512)S(1)}, u32[]{:S(2)}) copy-start(f32[384]{0:T(512)S(1)} %convert_element_type.338) | copy-start | bytes 4612
  182.9 84.7 %copy-start.66 = (f32[1536]{0:T(1024)}, f32[1536]{0:T(1024)S(1)}, u32[]{:S(2)}) copy-start(f32[1536]{0:T(1024)S(1)} %convert_element_type.340) | copy-start | bytes 18436
  183.0 84.6 %copy-start.81 = (f32[384]{0:T(512)}, f32[384]{0:T(512)S(1)}, u32[]{:S(2)}) copy-start(f32[384]{0:T(512)S(1)} %convert_element_type.339) | copy-start | bytes 4612
  183.0 93.4 %copy-start.76 = (f32[384]{0:T(512)}, f32[384]{0:T(512)S(1)}, u32[]{:S(2)}) copy-start(f32[384]{0:T(512)S(1)} %convert_element_type.342) | copy-start | bytes 4612
  183.0 93.4 %copy-start.87 = (f32[384]{0:T(512)}, f32[384]{0:T(512)S(1)}, u32[]{:S(2)}) copy-start(f32[384]{0:T(512)S(1)} %convert_element_type.343) | copy-start | bytes 4612
  533.5 138.5 %reduce-scatter.31.cloned.1.call-start = ((), (), s32[]{:S(2)}) async-start(), calls=%async_computation.19 | async-start | bytes 313344
  558.3 142.6 %reduce-scatter.27.cloned.1.call-start = ((), (), s32[]{:S(2)}) async-start(), calls=%async_computation.17 | async-start | bytes 940032
  565.0 194.7 %reduce-scatter.25.cloned.1.call-start = ((), (), s32[]{:S(2)}) async-start(), calls=%async_computation.16 | async-start | bytes 940032
  599.1 161.0 %copy-start.82 = (f32[384]{0:T(512)S(1)}, f32[384]{0:T(512)}, u32[]{:S(2)}) copy-start(f32[384]{0:T(512)} %copy-done.81) | copy-start | bytes 4612
  599.1 217.2 %all-reduce.47.cloned.1.call-start = ((), (), s32[]{:S(2)}) async-start(), calls=%async_computation.20 | async-start | bytes 313344 | tf_op jit(solution)/shard_map/psum | solution.py:284
  759.8 91.6 %reduce-scatter.17.cloned.1.call-start = ((), (), s32[]{:S(2)}) async-start(), calls=%async_computation.8 | async-start | bytes 1253376 | tf_op jit(solution)/shard_map/reduce_scatter | solution.py:339
  767.6 144.5 %reduce-scatter.19.cloned.1.call-start = ((), (), s32[]{:S(2)}) async-start(), calls=%async_computation.9 | async-start | bytes 1253376 | tf_op jit(solution)/shard_map/reduce_scatter | solution.py:339
  775.4 197.4 %reduce-scatter.21.cloned.1.call-start = ((), (), s32[]{:S(2)}) async-start(), calls=%async_computation.10 | async-start | bytes 1253376 | tf_op jit(solution)/shard_map/reduce_scatter | solution.py:351
  783.6 249.8 %reduce-scatter.23.cloned.1.call-start = ((), (), s32[]{:S(2)}) async-start(), calls=%async_computation.11 | async-start | bytes 1253376 | tf_op jit(solution)/shard_map/reduce_scatter | solution.py:351
  804.5 254.4 %all-reduce.49.cloned.1.call-start = ((), (), s32[]{:S(2)}) async-start(), calls=%async_computation.21 | async-start | bytes 589824 | tf_op jit(solution)/shard_map/psum | solution.py:338
  (98 other events, 968.8 us)
Sparse Core Ops, SparseCore 0:
  10.9 41.1 all-gather.30
  54.3 37.5 all-gather.32
  94.8 37.5 all-gather.34
  134.5 37.8 all-gather.36
  533.6 51.1 reduce-scatter.28
  589.1 52.9 reduce-scatter.30
  645.7 55.1 reduce-scatter.26
  704.5 55.1 reduce-scatter.24
  764.5 25.2 all-reduce.46
  793.3 58.0 reduce-scatter.16
  855.1 57.0 reduce-scatter.18
  915.6 57.0 reduce-scatter.20
  976.3 56.9 reduce-scatter.22
  1035.6 23.2 all-reduce.48
where the time goes:
time: 1080 us; the launch traced here: 1070 us
  waiting for transfers between devices  318 us (29%)
  matrix products  269 us (25%)
  blocking collectives  204 us (19%)
  local copies, waits for them, and re-layouts  189 us (18%)
  other arithmetic  69.4 us (6%)
  between operations  18.6 us (2%)
    reduce_scatter x2, waiting for transfers between devices, body(): lax.psum_scatter(gradients[11].astype(jnp.bfloat16), 'shard', scatter_dim...  121 us
    unnamed x2, blocking collectives  121 us
    dot_general x8, matrix products, matmul(): return jnp.dot(left, right, preferred_element_type=jnp.float32)  97.6 us
    unnamed x18, waiting for transfers between devices  89.2 us
    reduce_scatter x2, waiting for transfers between devices, body(): lax.psum_scatter(gradients[9].astype(jnp.bfloat16), 'shard', scatter_dime...  84.7 us
    dot_general x8, matrix products, right_product(): jnp.einsum('nd,fd->nf', left, right, preferred_element_type=jnp.float32)  60.6 us
    dot_general x8, matrix products, left_product(): jnp.einsum('nf,nd->fd', left, right, preferred_element_type=jnp.float32)  48.1 us
    all_gather x2, blocking collectives, body(): lax.all_gather(qkv_weight[layer_index], 'shard', axis=0, tiled=True)  42 us
  transfers between devices with their start and end apart: 14, of which 7 were waited for; matrix products, arithmetic and copies ran while one was open for 32% of the time, Pallas kernels for 0%

commit v1 on v0

v1 whole, which is shorter than its diff:
```python
import functools
import jax
import jax.numpy as jnp
from jax import lax
from jax.sharding import PartitionSpec as P
from jax.experimental import pallas as pl
from jax.experimental.pallas import tpu as pltpu

BF = jnp.bfloat16
F32 = jnp.float32
HEADS = 6
EPS = 1e-06
NEG = -1e30
LOG2E = 1.4426950408889634


def dot(a, b):
    return jnp.dot(a, b, preferred_element_type=F32)


def dot_nt(a, b):
    return lax.dot_general(a, b, (((1,), (1,)), ((), ())), preferred_element_type=F32)


def dot_tn(a, b):
    return lax.dot_general(a, b, (((0,), (0,)), ((), ())), preferred_element_type=F32)


def pad_rows(seq):
    return (seq + 15) // 16 * 16


def normalise(x):
    mean = jnp.mean(x, -1, keepdims=True)
    cen = x - mean
    rstd = lax.rsqrt(jnp.mean(cen * cen, -1, keepdims=True) + EPS)
    return cen * rstd, rstd


def norm_back(dxhat, xhat, rstd):
    return rstd * (
        dxhat
        - jnp.mean(dxhat, -1, keepdims=True)
        - xhat * jnp.mean(dxhat * xhat, -1, keepdims=True)
    )


def gelu_both(h):
    ax = jnp.abs(h) * 0.7071067811865476
    t = 1.0 / (1.0 + 0.3275911 * ax)
    e = jnp.exp(h * h * -0.5)
    poly = t * (0.127414796 + t * (-0.142248368 + t * (0.7107068705 + t * (-0.7265760135 + t * 0.5307027145))))
    tail = poly * e
    phi = jnp.where(h >= 0, 1.0 - tail, tail)
    return h * phi, phi + h * e * 0.3989422804014327


def load_padded(dst, src, seq, rows, images):
    for g in range(images):
        dst[g * rows : g * rows + seq] = src[g].astype(F32)
        dst[g * rows + seq : (g + 1) * rows] = jnp.zeros((rows - seq, dst.shape[1]), F32)


def fa_kernel(seq, x_ref, vec, wqkv, wp, m_ref, o_ref, aux_ref, xh_ref, x1_ref, xs):
    images = x_ref.shape[0]
    rows = pad_rows(seq)
    width = x_ref.shape[2]
    load_padded(xs, x_ref, seq, rows, images)
    xhat, rstd = normalise(xs[...])
    xh_ref[...] = xhat.astype(BF).reshape(images, rows, width)
    n1 = (xhat * vec[0:1, :] + vec[1:2, :]).astype(BF)
    for c in range(3):
        cs = slice(c * width, (c + 1) * width)
        mc = dot(n1, wqkv[:, cs])
        if c != 1:
            mc = mc + (vec[2:3, :] if c == 0 else vec[3:4, :])
        m_ref[:, :, cs] = mc.astype(BF).reshape(images, rows, width)
    lane = lax.broadcasted_iota(jnp.int32, (rows, 128), 1)
    row = lax.broadcasted_iota(jnp.int32, (rows, 128), 0)
    low = lane < 64
    kpad = jnp.where(row >= seq, NEG, 0.0).astype(BF)
    ones = jnp.where(row >= seq, 0.0, 1.0).astype(BF)
    qone0 = jnp.where(lane == 64, 1.0, 0.0).astype(BF)
    qone1 = jnp.where(lane == 0, 1.0, 0.0).astype(BF)
    valid = row < seq
    for g in range(images):
        aux = jnp.broadcast_to(rstd[g * rows : (g + 1) * rows], (rows, 128))
        for p in range(width // 128):
            q2 = m_ref[g, :, p * 128 : (p + 1) * 128] * jnp.asarray(0.125, BF)
            k2 = m_ref[g, :, width + p * 128 : width + (p + 1) * 128]
            v2 = m_ref[g, :, 2 * width + p * 128 : 2 * width + (p + 1) * 128]
            v2 = jnp.where(valid, v2, jnp.zeros_like(v2))
            vext = jnp.concatenate([v2, ones], 1)
            parts = []
            for half in range(2):
                mine = low if half == 0 else ~low
                qh = jnp.where(mine, q2, qone0 if half == 0 else qone1)
                kh = jnp.where(mine, k2, kpad)
                s = dot_nt(qh, kh)
                mx = jnp.max(s, -1, keepdims=True)
                pr = jnp.exp(s - mx).astype(BF)
                oe = dot(pr, vext)
                tot = oe[:, 128:]
                parts.append(oe[:, :128] / tot)
                aux = jnp.where(lane == 2 * p + half, mx + jnp.log(tot), aux)
            o_ref[g, :, p * 128 : (p + 1) * 128] = jnp.where(low, parts[0], parts[1]).astype(BF)
        aux_ref[g] = aux
    of = o_ref[...].reshape(images * rows, width)
    x1 = xs[...] + dot(of, wp[...]) + vec[4:5, :]
    x1_ref[...] = x1.reshape(images, rows, width)


def fm_kernel(seq, x1_ref, vec, w1, w2, out_ref, a_ref, d_ref, xh_ref, rs_ref, *, chunk=512):
    images, rows, width = x1_ref.shape
    x1 = x1_ref[...].reshape(images * rows, width)
    xhat, rstd = normalise(x1)
    xh_ref[...] = xhat.astype(BF).reshape(images, rows, width)
    rs_ref[...] = jnp.broadcast_to(rstd, (images * rows, 128)).reshape(images, rows, 128)
    n2 = (xhat * vec[5:6, :] + vec[6:7, :]).astype(BF)
    acc = x1 + vec[7:8, :]
    bias = jnp.concatenate([vec[r : r + 1, :] for r in range(8, 8 + w1.shape[1] // width)], 1)
    for c in range(w1.shape[1] // chunk):
        cs = slice(c * chunk, (c + 1) * chunk)
        h = dot(n2, w1[:, cs]) + bias[:, cs]
        a, d = gelu_both(h)
        a = a.astype(BF)
        a_ref[:, :, cs] = a.reshape(images, rows, chunk)
        d_ref[:, :, cs] = d.astype(BF).reshape(images, rows, chunk)
        acc = acc + dot(a, w2[cs, :])
    acc = acc.reshape(images, rows, width)
    for g in range(images):
        out_ref[g] = acc[g, :seq]


def colsum(x):
    return jnp.sum(x, 0, keepdims=True)


def bm_kernel(seq, gr_ref, a_ref, d_ref, xh_ref, rs_ref, vec, w1, w2,
              dx1_ref, dw1_o, dw2_o, vec_o, db1_o, gs, dw1, dw2, *, chunk=512):
    images, rows, width = xh_ref.shape
    n = images * rows
    step = pl.program_id(0)

    @pl.when(step == 0)
    def _():
        dw1[...] = jnp.zeros_like(dw1)
        dw2[...] = jnp.zeros_like(dw2)
        vec_o[...] = jnp.zeros_like(vec_o)
        db1_o[...] = jnp.zeros_like(db1_o)

    load_padded(gs, gr_ref, seq, rows, images)
    dz = gs[...].astype(BF)
    xhat = xh_ref[...].reshape(n, width).astype(F32)
    n2 = (xhat * vec[5:6, :] + vec[6:7, :]).astype(BF)
    dn2 = jnp.zeros((n, width), F32)
    for c in range(w1.shape[1] // chunk):
        cs = slice(c * chunk, (c + 1) * chunk)
        a = a_ref[:, :, cs].reshape(n, chunk)
        d = d_ref[:, :, cs].reshape(n, chunk)
        da = dot_nt(dz, w2[cs, :])
        dhf = d.astype(F32) * da
        dh = dhf.astype(BF)
        db1_o[:, cs] += colsum(dh.astype(F32))
        dw2[cs, :] += dot_tn(a, dz)
        dw1[:, cs] += dot_tn(n2, dh)
        dn2 = dn2 + dot_nt(dh, w1[:, cs])
    vec_o[0:1, :] += colsum(dz.astype(F32))
    vec_o[1:2, :] += colsum(dn2 * xhat)
    vec_o[2:3, :] += colsum(dn2)
    rs = rs_ref[...].reshape(n, 128)
    rstd = jnp.concatenate([rs] * (width // 128), 1)
    dx1 = gs[...] + norm_back(dn2 * vec[5:6, :], xhat, rstd)
    dx1_ref[...] = dx1.reshape(images, rows, width)

    @pl.when(step == pl.num_programs(0) - 1)
    def _():
        dw1_o[...] = dw1[...].astype(BF)
        dw2_o[...] = dw2[...].astype(BF)


def ba_kernel(seq, dx1_ref, m_ref, o_ref, aux_ref, xh_ref, vec, wqkv, wp,
              dx_ref, dwqkv_o, dwp_o, vec_o, dbm_o, dm, do, dwqkv, dwp):
    images, rows, width = xh_ref.shape
    n = images * rows
    step = pl.program_id(0)

    @pl.when(step == 0)
    def _():
        dwqkv[...] = jnp.zeros_like(dwqkv)
        dwp[...] = jnp.zeros_like(dwp)
        vec_o[...] = jnp.zeros_like(vec_o)
        dbm_o[...] = jnp.zeros_like(dbm_o)

    dx1 = dx1_ref[...].reshape(n, width)
    dy = dx1.astype(BF)
    of = o_ref[...].reshape(n, width)
    vec_o[0:1, :] += colsum(dy.astype(F32))
    dwp[...] += dot_tn(of, dy)
    do[...] = dot_nt(dy, wp[...]).astype(BF)
    lane = lax.broadcasted_iota(jnp.int32, (rows, 128), 1)
    row = lax.broadcasted_iota(jnp.int32, (rows, 128), 0)
    low = lane < 64
    kpad = jnp.where(row >= seq, NEG, 0.0).astype(BF)
    for g in range(images):
        aux = aux_ref[g]
        for p in range(width // 128):
            ps = slice(p * 128, (p + 1) * 128)
            q2 = m_ref[g, :, p * 128 : (p + 1) * 128] * jnp.asarray(0.125, BF)
            k2 = m_ref[g, :, width + p * 128 : width + (p + 1) * 128]
            v2 = m_ref[g, :, 2 * width + p * 128 : 2 * width + (p + 1) * 128]
            do2 = do[g * rows : (g + 1) * rows, ps]
            prod = o_ref[g, :, ps].astype(F32) * do2.astype(F32)
            outs = []
            for half in range(2):
                mine = low if half == 0 else ~low
                base = 64 if half == 0 else 0
                lse = aux[:, 2 * p + half : 2 * p + half + 1]
                l0 = (-lse).astype(BF)
                r1 = -lse - l0.astype(F32)
                l1 = r1.astype(BF)
                l2 = (r1 - l1.astype(F32)).astype(BF)
                dd = -jnp.sum(jnp.where(mine, prod, 0.0), -1, keepdims=True)
                d0 = dd.astype(BF)
                d1 = (dd - d0.astype(F32)).astype(BF)
                zero = jnp.zeros((rows, 128), BF)
                one = jnp.ones((rows, 128), BF)
                qx = jnp.where(lane == base, l0, jnp.where(lane == base + 1, l1, jnp.where(lane == base + 2, l2, jnp.where(lane == base + 3, one, zero))))
                kx = jnp.where((lane >= base) & (lane < base + 3), one, jnp.where(lane == base + 3, kpad, zero))
                dx_ = jnp.where(lane == base, d0, jnp.where(lane == base + 1, d1, zero))
                qh = jnp.where(mine, q2, qx)
                kh = jnp.where(mine, k2, kx)
                doh = jnp.where(mine, do2, dx_)
                vh = jnp.where(mine, v2, jnp.where((lane >= base) & (lane < base + 2), one, zero))
                st = dot_nt(kh, qh)
                pt = jnp.exp(st)
                dpt = dot_nt(vh, doh)
                dst = (pt * dpt).astype(BF)
                dv = dot(pt.astype(BF), do2)
                dk = dot(dst, q2)
                dq = dot_tn(dst, k2) * 0.125
                outs.append((dq, dk, dv))
            for j in range(3):
                val = jnp.where(low, outs[0][j], outs[1][j]).astype(BF)
                dm[g * rows : (g + 1) * rows, j * width + p * 128 : j * width + (p + 1) * 128] = val
    dbm_o[...] += colsum(dm[...].astype(F32))
    xhat = xh_ref[...].reshape(n, width).astype(F32)
    n1 = (xhat * vec[0:1, :] + vec[1:2, :]).astype(BF)
    for c in range(3):
        cs = slice(c * width, (c + 1) * width)
        dwqkv[:, cs] += dot_tn(n1, dm[:, cs])
    dn1 = dot_nt(dm[...], wqkv[...])
    vec_o[1:2, :] += colsum(dn1 * xhat)
    vec_o[2:3, :] += colsum(dn1)
    rstd = aux_ref[...].reshape(n, 128)[:, 127:128]
    dx = dx1 + norm_back(dn1 * vec[0:1, :], xhat, rstd)
    dx = dx.reshape(images, rows, width)
    for g in range(images):
        dx_ref[g] = dx[g, :seq]

    @pl.when(step == pl.num_programs(0) - 1)
    def _():
        dwqkv_o[...] = dwqkv[...].astype(BF)
        dwp_o[...] = dwp[...].astype(BF)


VMEM_LIMIT = 60 * 2**20


def blk(shape):
    nd = len(shape)
    return pl.BlockSpec(shape, lambda i: (i,) + (0,) * (nd - 1))


def whole(arr):
    nd = len(arr.shape)
    return pl.BlockSpec(arr.shape, lambda i: (0,) * nd)


def sds(shape, dt):
    return jax.ShapeDtypeStruct(shape, dt)


def call(kern, grid, blocked_in, whole_in, blocked_out, whole_out, scratch, per, name=None, flops=0):
    in_specs = [blk((per,) + a.shape[1:]) for a in blocked_in] + [whole(a) for a in whole_in]
    out_specs = [blk((per,) + a.shape[1:]) for a in blocked_out] + [whole(a) for a in whole_out]
    return pl.pallas_call(
        kern,
        grid=(grid,),
        in_specs=in_specs,
        out_specs=out_specs,
        out_shape=list(blocked_out) + list(whole_out),
        scratch_shapes=scratch,
        compiler_params=pltpu.CompilerParams(vmem_limit_bytes=VMEM_LIMIT),
        name=name,
        cost_estimate=pl.CostEstimate(flops=flops, bytes_accessed=0, transcendentals=0),
    )(*blocked_in, *whole_in)


def run_fa(x, vec, wqkv, wp, per):
    images, seq, width = x.shape
    rows = pad_rows(seq)
    return call(
        functools.partial(fa_kernel, seq), images // per, [x], [vec, wqkv, wp],
        [sds((images, rows, 3 * width), BF), sds((images, rows, width), BF), sds((images, rows, 128), F32),
         sds((images, rows, width), BF), sds((images, rows, width), F32)], [],
        [pltpu.VMEM((per * rows, width), F32)], per, "fa")


def run_fm(seq, x1, vec, w1, w2, per):
    images, rows, width = x1.shape
    ff = w1.shape[1]
    return call(
        functools.partial(fm_kernel, seq), images // per, [x1], [vec, w1, w2],
        [sds((images, seq, width), F32), sds((images, rows, ff), BF), sds((images, rows, ff), BF),
         sds((images, rows, width), BF), sds((images, rows, 128), F32)], [], [], per, "fm")


def run_bm(gr, a, d, xh, rs, vec, w1, w2, per):
    images, seq, width = gr.shape
    rows = a.shape[1]
    ff = w1.shape[1]
    return call(
        functools.partial(bm_kernel, seq), images // per, [gr, a, d, xh, rs], [vec, w1, w2],
        [sds((images, rows, width), F32)],
        [sds((width, ff), BF), sds((ff, width), BF), sds((8, width), F32), sds((1, ff), F32)],
        [pltpu.VMEM((per * rows, width), F32), pltpu.VMEM((width, ff), F32), pltpu.VMEM((ff, width), F32)], per, "bm")


def run_ba(seq, dx1, m, o, aux, xh, vec, wqkv, wp, per):
    images, rows, width = dx1.shape
    return call(
        functools.partial(ba_kernel, seq), images // per, [dx1, m, o, aux, xh], [vec, wqkv, wp],
        [sds((images, seq, width), F32)],
        [sds((width, 3 * width), BF), sds((width, width), BF), sds((8, width), F32), sds((1, 3 * width), F32)],
        [pltpu.VMEM((per * rows, 3 * width), BF), pltpu.VMEM((per * rows, width), BF),
         pltpu.VMEM((width, 3 * width), F32), pltpu.VMEM((width, width), F32)], per, "ba")


def bits_of(count):
    out = []
    b = 1
    while b < count:
        out.append(b)
        b *= 2
    return out


def xor_pairs(count, b):
    return [(i, i ^ b) for i in range(count)]


def gather(x, n, idx):
    buf = x[None]
    for b in reversed(bits_of(n)):
        recv = lax.ppermute(buf, "shard", xor_pairs(n, b))
        flag = (idx & b) != 0
        low = jnp.where(flag, recv, buf)
        high = jnp.where(flag, buf, recv)
        buf = jnp.stack([low, high], 1).reshape((2 * buf.shape[0],) + x.shape)
    return buf


def reduce_to_owner(x, n, idx, reps):
    buf = x
    for b in bits_of(n):
        half = buf.reshape((buf.shape[0] // 2, 2) + buf.shape[1:])
        flag = ((idx & b) != 0).astype(jnp.int32)
        send = lax.dynamic_index_in_dim(half, 1 - flag, 1, keepdims=False)
        keep = lax.dynamic_index_in_dim(half, flag, 1, keepdims=False)
        recv = lax.ppermute(send, "shard", xor_pairs(n, b))
        buf = (keep.astype(F32) + recv.astype(F32)).astype(BF)
    buf = buf[0]
    for b in bits_of(reps):
        recv = lax.ppermute(buf, "replica", xor_pairs(reps, b))
        buf = (buf.astype(F32) + recv.astype(F32)).astype(BF)
    return buf.astype(F32)


def body(n, reps, tokens, norm1_gain, norm1_shift, qkv_weight, query_bias, value_bias, proj_weight, proj_bias,
         norm2_gain, norm2_shift, fc1_weight, fc1_bias, fc2_weight, fc2_bias, cotangent):
    images, seq, width = tokens.shape
    part = width // n
    ff = fc1_weight.shape[2]
    quart = ff // width
    idx = lax.axis_index("shard")
    per = 2 if images % 2 == 0 else 1
    layers = range(2)

    smalls = [norm1_gain, norm1_shift, query_bias, value_bias, proj_bias, norm2_gain, norm2_shift, fc2_bias]
    small = jnp.concatenate([jnp.stack(smalls, 1), fc1_bias.reshape(2, quart, part)], 1)
    rows_small = small.shape[1]
    small = jnp.pad(small.reshape(2 * rows_small, part).T, ((0, 0), (0, 128 - 2 * rows_small)))

    def full(x):
        g = gather(x, n, idx)
        return g.reshape((n * x.shape[0],) + x.shape[1:])

    def attn_pack(layer):
        parts = [qkv_weight[layer], proj_weight[layer]] + ([small] if layer == 0 else [])
        return jnp.concatenate(parts, 1)

    attn_full, fc1_full, fc2_full = [], [], []
    for layer in layers:
        attn_full.append(full(attn_pack(layer)))
        fc1_full.append(full(fc1_weight[layer]))
        fc2_full.append(full(fc2_weight[layer]))
    sm = attn_full[0][:, 4 * width : 4 * width + 2 * rows_small].astype(F32)
    vec_all = sm.T.reshape(2, rows_small, width)
    vecs = []
    for layer in layers:
        b1 = vec_all[layer, 8:].reshape(quart, n, part).transpose(1, 0, 2).reshape(quart, width)
        vecs.append(jnp.concatenate([vec_all[layer, :8], b1, jnp.zeros((4, width), F32)]))

    current = tokens
    outs, kept = [], []
    for layer in layers:
        vec = vecs[layer]
        wqkv = attn_full[layer][:, : 3 * width]
        wp = attn_full[layer][:, 3 * width : 4 * width]
        m, o, aux, xh1, x1 = run_fa(current, vec, wqkv, wp, per)
        current, a, d, xh2, rs = run_fm(seq, x1, vec, fc1_full[layer], fc2_full[layer], per)
        outs.append(current)
        kept.append((m, o, aux, xh1, a, d, xh2, rs, wqkv, wp))
    grad = cotangent
    grads = [None, None]
    small_grads = [None, None]
    for layer in (1, 0):
        m, o, aux, xh1, a, d, xh2, rs, wqkv, wp = kept[layer]
        vec = vecs[layer]
        dx1, dw1, dw2, v2, db1 = run_bm(grad, a, d, xh2, rs, vec, fc1_full[layer], fc2_full[layer], per)
        g_fc1 = reduce_to_owner(dw1.reshape(n, part, ff), n, idx, reps)
        g_fc2 = reduce_to_owner(dw2.reshape(n, ff // n, width), n, idx, reps)
        grad, dwqkv, dwp, v1, dbm = run_ba(seq, dx1, m, o, aux, xh1, vec, wqkv, wp, per)
        gb1 = db1.reshape(n, quart, part).transpose(1, 0, 2).reshape(quart, width)
        small_grads[layer] = jnp.concatenate(
            [v1[1:3], dbm[:, :width], dbm[:, 2 * width :], v1[0:1], v2[1:3], v2[0:1], gb1])
        parts = [dwqkv, dwp]
        if layer == 0:
            sg = jnp.concatenate(small_grads).astype(BF).T
            parts.append(jnp.pad(sg, ((0, 0), (0, 128 - sg.shape[1]))))
        pack = jnp.concatenate(parts, 1)
        g_attn = reduce_to_owner(pack.reshape(n, part, pack.shape[1]), n, idx, reps)
        grads[layer] = (g_attn, g_fc1, g_fc2)
    g0, g1 = grads[0][0], grads[1][0]
    sgrad = g0[:, 4 * width : 4 * width + 2 * rows_small].T.reshape(2, rows_small, part)
    one = lambda j: sgrad[:, j]
    return (
        outs[0], outs[1], grad,
        one(0), one(1),
        jnp.stack([g0[:, : 3 * width], g1[:, : 3 * width]]),
        one(2), one(3),
        jnp.stack([g0[:, 3 * width : 4 * width], g1[:, 3 * width : 4 * width]]),
        one(4), one(5), one(6),
        jnp.stack([grads[0][1], grads[1][1]]),
        sgrad[:, 8:].reshape(2, ff // n),
        jnp.stack([grads[0][2], grads[1][2]]),
        one(7),
    )


def solution(mesh):
    n = mesh.shape["shard"]
    reps = mesh.shape["replica"]
    batch = P(("replica", "shard"), None, None)
    row2 = P(None, "shard")
    row3 = P(None, "shard", None)
    in_specs = (batch, row2, row2, row3, row2, row2, row3, row2, row2, row2, row3, row2, row3, row2, batch)
    out_specs = (batch, batch, batch, row2, row2, row3, row2, row2, row3, row2, row2, row2, row3, row2, row3, row2)
    return jax.shard_map(
        functools.partial(body, n, reps), mesh=mesh, in_specs=in_specs, out_specs=out_specs, check_vma=False
    )
```

time: 1080 us -> 377 us (0.35)
  matrix products: 269 us -> 0 us
  waiting for transfers between devices: 318 us -> 91.6 us
  blocking collectives: 204 us -> 0 us
  Pallas kernels: 0 us -> 192 us
  local copies, waits for them, and re-layouts: 189 us -> 24.8 us
  other arithmetic: 69.4 us -> 12.4 us
  starting transfers between devices: 1.12 us -> 47.8 us
  between operations: 18.6 us -> 2.16 us
    dot_general x36 -> x0, matrix products: 269 us -> none  [the longest x8 97.6 us: matmul(): return jnp.dot(left, right, preferred_element_type=jnp.float32)]
    reduce_scatter x4 -> x0, waiting for transfers between devices: 206 us -> none  [the longest x2 121 us: body(): lax.psum_scatter(gradients[11].astype(jnp.bfloat16), 'shard', scatter_dim...]
    pallas_call x0 -> x8, Pallas kernels: none -> 192 us  [call(): pl.pallas_call(kern, grid=(grid,), in_specs=in_specs, out_specs=out_specs...]
    unnamed x2 -> x0, blocking collectives: 121 us -> none
    ppermute x0 -> x54, waiting for transfers between devices: none -> 91.6 us  [the longest x24 45.6 us: reduce_to_owner(): recv = lax.ppermute(send, 'shard', xor_pairs(n, b))]
    unnamed x18 -> x0, waiting for transfers between devices: 89.2 us -> none
    all_gather x4 -> x0, blocking collectives: 83 us -> none  [the longest x2 42 us: body(): lax.all_gather(qkv_weight[layer_index], 'shard', axis=0, tiled=True)]
    reshape x13 -> x12, local copies, waits for them, and re-layouts: 56.9 us -> 2.08 us  [the longest x1 0.74 us: body(): fc1_bias.reshape(2, quart, part)]
  transfers between devices with their start and end apart: 14 -> 54, of which waited for: 7 -> 31; matrix products, arithmetic and copies ran while one was open for 32% -> 4% of each run, Pallas kernels for 0% -> 0%
where the time goes in v1:
time: 377 us; the launch traced here: 370 us
  Pallas kernels  192 us (51%)
  waiting for transfers between devices  91.6 us (24%)
  starting transfers between devices  47.8 us (13%)
  local copies, waits for them, and re-layouts  24.8 us (7%)
  other arithmetic  12.4 us (3%)
    pallas_call x8, Pallas kernels, call(): pl.pallas_call(kern, grid=(grid,), in_specs=in_specs, out_specs=out_specs...  192 us
    ppermute x24, waiting for transfers between devices, reduce_to_owner(): recv = lax.ppermute(send, 'shard', xor_pairs(n, b))  45.6 us
    ppermute x24, waiting for transfers between devices, gather(): recv = lax.ppermute(buf, 'shard', xor_pairs(n, b))  40.5 us
    ppermute x24, starting transfers between devices, gather(): recv = lax.ppermute(buf, 'shard', xor_pairs(n, b))  26.7 us
    ppermute x24, starting transfers between devices, reduce_to_owner(): recv = lax.ppermute(send, 'shard', xor_pairs(n, b))  15.1 us
  transfers between devices with their start and end apart: 54, of which 31 were waited for; matrix products, arithmetic and copies ran while one was open for 4% of the time, Pallas kernels for 0%

profile of v1, /device:TPU:0, one launch (start us, length us, event | category | flops | bytes accessed | tf_op | source)
XLA Modules:
  0.0 370.5 jit_solution(11509057088746627496)
XLA Ops:
  8.5 4.1 %collective-permute-start = (bf16[1,24,1664]{2,1,0:T(8,128)(2,1)S(1)}, bf16[1,24,1664]{2,1,0:T(8,128)(2,1)S(1)}, u32[]{:S(2)}, u32[]{:S(2)}) collective-permute-start(bf16[1,24,1664]{2,1,0:T(8,128)(2,1)S(1)} %fusion.22), channel_id=1, source_target_pairs={{0,8},{1,9},{2,10},{3,11},{4,12},{5,13},{6,14},{7,15},{8,0},{9,1},... | collective-permute-start | bytes 239624 | tf_op jit(solution)/shard_map/ppermute | solution.py:356
  14.4 2.9 collective-permute-start.20
  17.5 6.5 %collective-permute-done.16 = bf16[1,24,1536]{2,1,0:T(8,128)(2,1)S(1)} collective-permute-done((bf16[1,24,1536]{2,1,0:T(8,128)(2,1)S(1)}, bf16[1,24,1536]{2,1,0:T(8,128)(2,1)S(1)}, u32[]{:S(2)}, u32[]{:S(2)}) %collective-permute-start.16) | collective-permute-done | bytes 73760 | tf_op jit(solution)/shard_map/ppermute | solution.py:356
  55.6 6.1 %collective-permute-done.22 = bf16[4,96,384]{2,1,0:T(8,128)(2,1)S(1)} collective-permute-done((bf16[4,96,384]{2,1,0:T(8,128)(2,1)S(1)}, bf16[4,96,384]{2,1,0:T(8,128)(2,1)S(1)}, u32[]{:S(2)}, u32[]{:S(2)}) %collective-permute-start.22) | collective-permute-done | bytes 294944 | tf_op jit(solution)/shard_map/ppermute | solution.py:356
  62.0 6.6 %collective-permute-done.2 = bf16[4,24,1664]{2,1,0:T(8,128)(2,1)S(1)} collective-permute-done((bf16[4,24,1664]{2,1,0:T(8,128)(2,1)S(1)}, bf16[4,24,1664]{2,1,0:T(8,128)(2,1)S(1)}, u32[]{:S(2)}, u32[]{:S(2)}) %collective-permute-start.2) | collective-permute-done | bytes 319520 | tf_op jit(solution)/shard_map/ppermute | solution.py:356
  68.8 6.1 %collective-permute-done.6 = bf16[4,24,1536]{2,1,0:T(8,128)(2,1)S(1)} collective-permute-done((bf16[4,24,1536]{2,1,0:T(8,128)(2,1)S(1)}, bf16[4,24,1536]{2,1,0:T(8,128)(2,1)S(1)}, u32[]{:S(2)}, u32[]{:S(2)}) %collective-permute-start.6) | collective-permute-done | bytes 294944 | tf_op jit(solution)/shard_map/ppermute | solution.py:356
  75.1 4.6 %collective-permute-done.10 = bf16[4,96,384]{2,1,0:T(8,128)(2,1)S(1)} collective-permute-done((bf16[4,96,384]{2,1,0:T(8,128)(2,1)S(1)}, bf16[4,96,384]{2,1,0:T(8,128)(2,1)S(1)}, u32[]{:S(2)}, u32[]{:S(2)}) %collective-permute-start.10) | collective-permute-done | bytes 294944 | tf_op jit(solution)/shard_map/ppermute | solution.py:356
  91.8 14.5 %fa.2 = (bf16[10,208,1152]{2,1,0:T(8,128)(2,1)}, bf16[10,208,384]{2,1,0:T(8,128)(2,1)}, f32[10,208,128]{2,1,0:T(8,128)}, bf16[10,208,384]{2,1,0:T(8,128)(2,1)}, f32[10,208,384]{2,1,0:T(8,128)}) custom-call(bf16[10,197,384]{2,1,0:T(8,128)(2,1)} %x_ref.1, f32[16,384]{1,0:T(8,128)} %get-tuple-element.167.vec, bf16[384,1152]{1,0:T(8,128)(2,1)} %slice.187.wqkv, ...), custom_call_target="tpu_custom_call" | custom-call | tf_op jit(solution)/shard_map/fa/pallas_call | solution.py:287
  106.4 21.1 %fm.2 = (f32[10,197,384]{2,1,0:T(8,128)}, bf16[10,208,1536]{2,1,0:T(8,128)(2,1)}, bf16[10,208,1536]{2,1,0:T(8,128)(2,1)}, bf16[10,208,384]{2,1,0:T(8,128)(2,1)}, f32[10,208,128]{2,1,0:T(8,128)}) custom-call(f32[10,208,384]{2,1,0:T(8,128)} %get-tuple-element.56.x1_ref, f32[16,384]{1,0:T(8,128)} %get-tuple-element.167.vec, bf16[384,1536]{1,0:T(8,128)(2,1)} %bitcast.390, ...), custom_call_target="tpu_custom_call" | custom-call | tf_op jit(solution)/shard_map/fm/pallas_call | solution.py:287
  127.4 14.0 %fa.3 = (bf16[10,208,1152]{2,1,0:T(8,128)(2,1)}, bf16[10,208,384]{2,1,0:T(8,128)(2,1)}, f32[10,208,128]{2,1,0:T(8,128)}, bf16[10,208,384]{2,1,0:T(8,128)(2,1)}, f32[10,208,384]{2,1,0:T(8,128)}) custom-call(f32[10,197,384]{2,1,0:T(8,128)} %get-tuple-element.40.x_ref, f32[16,384]{1,0:T(8,128)} %get-tuple-element.166.vec, bf16[384,1152]{1,0:T(8,128)(2,1)} %slice.191.wqkv, ...), custom_call_target="tpu_custom_call" | custom-call | tf_op jit(solution)/shard_map/fa/pallas_call | solution.py:287
  141.4 21.1 %fm.3 = (f32[10,197,384]{2,1,0:T(8,128)}, bf16[10,208,1536]{2,1,0:T(8,128)(2,1)}, bf16[10,208,1536]{2,1,0:T(8,128)(2,1)}, bf16[10,208,384]{2,1,0:T(8,128)(2,1)}, f32[10,208,128]{2,1,0:T(8,128)}) custom-call(f32[10,208,384]{2,1,0:T(8,128)} %get-tuple-element.58.x1_ref, f32[16,384]{1,0:T(8,128)} %get-tuple-element.166.vec, bf16[384,1536]{1,0:T(8,128)(2,1)} %bitcast.388, ...), custom_call_target="tpu_custom_call" | custom-call | tf_op jit(solution)/shard_map/fm/pallas_call | solution.py:287
  162.5 21.7 %bm.2 = (f32[10,208,384]{2,1,0:T(8,128)}, bf16[384,1536]{1,0:T(8,128)(2,1)}, bf16[1536,384]{1,0:T(8,128)(2,1)}, f32[8,384]{1,0:T(8,128)}, f32[1,1536]{1,0:T(1,128)}) custom-call(bf16[10,197,384]{2,1,0:T(8,128)(2,1)} %gr_ref.1, bf16[10,208,1536]{2,1,0:T(8,128)(2,1)} %get-tuple-element.60.a_ref, bf16[10,208,1536]{2,1,0:T(8,128)(2,1)} %get-tuple-element.61.d_ref, ...), custom_call_target="tpu_custom_call" | custom-call | tf_op jit(solution)/shard_map/bm/pallas_call | solution.py:287
  184.2 38.6 %ba.2 = (f32[10,197,384]{2,1,0:T(8,128)}, bf16[384,1152]{1,0:T(8,128)(2,1)}, bf16[384,384]{1,0:T(8,128)(2,1)}, f32[8,384]{1,0:T(8,128)}, f32[1,1152]{1,0:T(1,128)}) custom-call(f32[10,208,384]{2,1,0:T(8,128)} %get-tuple-element.64.dx1_ref, bf16[10,208,1152]{2,1,0:T(8,128)(2,1)} %get-tuple-element.65.m_ref, bf16[10,208,384]{2,1,0:T(8,128)(2,1)} %get-tuple-element.66.o_ref, ...), custom_call_target="tpu_custom_call" | custom-call | tf_op jit(solution)/shard_map/ba/pallas_call | solution.py:287
  222.8 21.9 %bm.3 = (f32[10,208,384]{2,1,0:T(8,128)}, bf16[384,1536]{1,0:T(8,128)(2,1)}, bf16[1536,384]{1,0:T(8,128)(2,1)}, f32[8,384]{1,0:T(8,128)}, f32[1,1536]{1,0:T(1,128)}) custom-call(f32[10,197,384]{2,1,0:T(8,128)} %get-tuple-element.69.gr_ref, bf16[10,208,1536]{2,1,0:T(8,128)(2,1)} %get-tuple-element.70.a_ref, bf16[10,208,1536]{2,1,0:T(8,128)(2,1)} %get-tuple-element.71.d_ref, ...), custom_call_target="tpu_custom_call" | custom-call | tf_op jit(solution)/shard_map/bm/pallas_call | solution.py:287
  244.8 38.8 %ba.3 = (f32[10,197,384]{2,1,0:T(8,128)}, bf16[384,1152]{1,0:T(8,128)(2,1)}, bf16[384,384]{1,0:T(8,128)(2,1)}, f32[8,384]{1,0:T(8,128)}, f32[1,1152]{1,0:T(1,128)}) custom-call(f32[10,208,384]{2,1,0:T(8,128)} %get-tuple-element.74.dx1_ref, bf16[10,208,1152]{2,1,0:T(8,128)(2,1)} %get-tuple-element.75.m_ref, bf16[10,208,384]{2,1,0:T(8,128)(2,1)} %get-tuple-element.76.o_ref, ...), custom_call_target="tpu_custom_call" | custom-call | tf_op jit(solution)/shard_map/ba/pallas_call | solution.py:287
  297.9 4.2 %collective-permute-done.30 = bf16[4,24,1536]{2,1,0:T(8,128)(2,1)S(1)} collective-permute-done((bf16[4,24,1536]{2,1,0:T(8,128)(2,1)S(1)}, bf16[4,24,1536]{2,1,0:T(8,128)(2,1)S(1)}, u32[]{:S(2)}, u32[]{:S(2)}) %collective-permute-start.30) | collective-permute-done | bytes 294944 | tf_op jit(solution)/shard_map/ppermute | solution.py:371
  302.5 5.9 %collective-permute-done.40 = bf16[4,24,1536]{2,1,0:T(8,128)(2,1)S(1)} collective-permute-done((bf16[4,24,1536]{2,1,0:T(8,128)(2,1)S(1)}, bf16[4,24,1536]{2,1,0:T(8,128)(2,1)S(1)}, u32[]{:S(2)}, u32[]{:S(2)}) %collective-permute-start.40) | collective-permute-done | bytes 294944 | tf_op jit(solution)/shard_map/ppermute | solution.py:371
  308.5 6.2 %collective-permute-done.35 = bf16[4,24,1536]{2,1,0:T(8,128)(2,1)S(1)} collective-permute-done((bf16[4,24,1536]{2,1,0:T(8,128)(2,1)S(1)}, bf16[4,24,1536]{2,1,0:T(8,128)(2,1)S(1)}, u32[]{:S(2)}, u32[]{:S(2)}) %collective-permute-start.35) | collective-permute-done | bytes 294944 | tf_op jit(solution)/shard_map/ppermute | solution.py:371
  314.9 6.2 %collective-permute-done.50 = bf16[4,96,384]{2,1,0:T(8,128)(2,1)S(1)} collective-permute-done((bf16[4,96,384]{2,1,0:T(8,128)(2,1)S(1)}, bf16[4,96,384]{2,1,0:T(8,128)(2,1)S(1)}, u32[]{:S(2)}, u32[]{:S(2)}) %collective-permute-start.50) | collective-permute-done | bytes 294944 | tf_op jit(solution)/shard_map/ppermute | solution.py:371
  321.2 6.2 %collective-permute-done.45 = bf16[4,96,384]{2,1,0:T(8,128)(2,1)S(1)} collective-permute-done((bf16[4,96,384]{2,1,0:T(8,128)(2,1)S(1)}, bf16[4,96,384]{2,1,0:T(8,128)(2,1)S(1)}, u32[]{:S(2)}, u32[]{:S(2)}) %collective-permute-start.45) | collective-permute-done | bytes 294944 | tf_op jit(solution)/shard_map/ppermute | solution.py:371
  327.5 6.0 %collective-permute-done.25 = bf16[4,24,1664]{2,1,0:T(8,128)(2,1)S(1)} collective-permute-done((bf16[4,24,1664]{2,1,0:T(8,128)(2,1)S(1)}, bf16[4,24,1664]{2,1,0:T(8,128)(2,1)S(1)}, u32[]{:S(2)}, u32[]{:S(2)}) %collective-permute-start.25) | collective-permute-done | bytes 319520 | tf_op jit(solution)/shard_map/ppermute | solution.py:371
  340.0 4.3 %collective-permute-done.46 = bf16[2,96,384]{2,1,0:T(8,128)(2,1)S(1)} collective-permute-done((bf16[2,96,384]{2,1,0:T(8,128)(2,1)S(1)}, bf16[2,96,384]{2,1,0:T(8,128)(2,1)S(1)}, u32[]{:S(2)}, u32[]{:S(2)}) %collective-permute-start.46) | collective-permute-done | bytes 147488 | tf_op jit(solution)/shard_map/ppermute | solution.py:371
  344.4 3.0 collective-permute-start.47
  364.6 2.9 collective-permute-done.28
  (314 shorter events, 94.8 us)
Async XLA Ops:
  8.5 22.2 %collective-permute-start = (bf16[1,24,1664]{2,1,0:T(8,128)(2,1)S(1)}, bf16[1,24,1664]{2,1,0:T(8,128)(2,1)S(1)}, u32[]{:S(2)}, u32[]{:S(2)}) collective-permute-start(bf16[1,24,1664]{2,1,0:T(8,128)(2,1)S(1)} %fusion.22), channel_id=1, source_target_pairs={{0,8},{1,9},{2,10},{3,11},{4,12},{5,13},{6,14},{7,15},{8,0},{9,1},... | collective-permute-start | bytes 239624 | tf_op jit(solution)/shard_map/ppermute | solution.py:356
  33.3 15.5 %collective-permute-start.5 = (bf16[2,24,1536]{2,1,0:T(8,128)(2,1)S(1)}, bf16[2,24,1536]{2,1,0:T(8,128)(2,1)S(1)}, u32[]{:S(2)}, u32[]{:S(2)}) collective-permute-start(bf16[2,24,1536]{2,1,0:T(8,128)(2,1)S(1)} %maximum_bitcast_fusion.1), channel_id=1, source_target_pairs={{0,4},{1,5},{2,6},{3,7},{4,0},{5,1},{6,2},{7,3},{8,12},{9,13},{10,... | collective-permute-start | bytes 442376 | tf_op jit(solution)/shard_map/ppermute | solution.py:356
  35.9 15.8 %collective-permute-start.9 = (bf16[2,96,384]{2,1,0:T(8,128)(2,1)S(1)}, bf16[2,96,384]{2,1,0:T(8,128)(2,1)S(1)}, u32[]{:S(2)}, u32[]{:S(2)}) collective-permute-start(bf16[2,96,384]{2,1,0:T(8,128)(2,1)S(1)} %maximum_bitcast_fusion.2), channel_id=1, source_target_pairs={{0,4},{1,5},{2,6},{3,7},{4,0},{5,1},{6,2},{7,3},{8,12},{9,13},{10,... | collective-permute-start | bytes 442376 | tf_op jit(solution)/shard_map/ppermute | solution.py:356
  39.1 13.4 %collective-permute-start.14 = (bf16[4,24,1536]{2,1,0:T(8,128)(2,1)S(1)}, bf16[4,24,1536]{2,1,0:T(8,128)(2,1)S(1)}, u32[]{:S(2)}, u32[]{:S(2)}) collective-permute-start(bf16[4,24,1536]{2,1,0:T(8,128)(2,1)S(1)} %bitcast.448), channel_id=1, source_target_pairs={{0,2},{1,3},{2,0},{3,1},{4,6},{5,7},{6,4},{7,5},{8,10},{9,11},{10,... | collective-permute-start | bytes 884744 | tf_op jit(solution)/shard_map/ppermute | solution.py:356
  42.2 13.3 %collective-permute-start.18 = (bf16[4,24,1536]{2,1,0:T(8,128)(2,1)S(1)}, bf16[4,24,1536]{2,1,0:T(8,128)(2,1)S(1)}, u32[]{:S(2)}, u32[]{:S(2)}) collective-permute-start(bf16[4,24,1536]{2,1,0:T(8,128)(2,1)S(1)} %bitcast.444), channel_id=1, source_target_pairs={{0,2},{1,3},{2,0},{3,1},{4,6},{5,7},{6,4},{7,5},{8,10},{9,11},{10,... | collective-permute-start | bytes 884744 | tf_op jit(solution)/shard_map/ppermute | solution.py:356
  45.6 16.2 %collective-permute-start.22 = (bf16[4,96,384]{2,1,0:T(8,128)(2,1)S(1)}, bf16[4,96,384]{2,1,0:T(8,128)(2,1)S(1)}, u32[]{:S(2)}, u32[]{:S(2)}) collective-permute-start(bf16[4,96,384]{2,1,0:T(8,128)(2,1)S(1)} %bitcast.447), channel_id=1, source_target_pairs={{0,2},{1,3},{2,0},{3,1},{4,6},{5,7},{6,4},{7,5},{8,10},{9,11},{10,... | collective-permute-start | bytes 884744 | tf_op jit(solution)/shard_map/ppermute | solution.py:356
  48.8 19.9 %collective-permute-start.2 = (bf16[4,24,1664]{2,1,0:T(8,128)(2,1)S(1)}, bf16[4,24,1664]{2,1,0:T(8,128)(2,1)S(1)}, u32[]{:S(2)}, u32[]{:S(2)}) collective-permute-start(bf16[4,24,1664]{2,1,0:T(8,128)(2,1)S(1)} %bitcast.425), channel_id=1, source_target_pairs={{0,2},{1,3},{2,0},{3,1},{4,6},{5,7},{6,4},{7,5},{8,10},{9,11},{10,... | collective-permute-start | bytes 958472 | tf_op jit(solution)/shard_map/ppermute | solution.py:356
  51.6 23.3 %collective-permute-start.6 = (bf16[4,24,1536]{2,1,0:T(8,128)(2,1)S(1)}, bf16[4,24,1536]{2,1,0:T(8,128)(2,1)S(1)}, u32[]{:S(2)}, u32[]{:S(2)}) collective-permute-start(bf16[4,24,1536]{2,1,0:T(8,128)(2,1)S(1)} %bitcast.445), channel_id=1, source_target_pairs={{0,2},{1,3},{2,0},{3,1},{4,6},{5,7},{6,4},{7,5},{8,10},{9,11},{10,... | collective-permute-start | bytes 884744 | tf_op jit(solution)/shard_map/ppermute | solution.py:356
  52.6 27.2 %collective-permute-start.10 = (bf16[4,96,384]{2,1,0:T(8,128)(2,1)S(1)}, bf16[4,96,384]{2,1,0:T(8,128)(2,1)S(1)}, u32[]{:S(2)}, u32[]{:S(2)}) collective-permute-start(bf16[4,96,384]{2,1,0:T(8,128)(2,1)S(1)} %bitcast.446), channel_id=1, source_target_pairs={{0,2},{1,3},{2,0},{3,1},{4,6},{5,7},{6,4},{7,5},{8,10},{9,11},{10,... | collective-permute-start | bytes 884744 | tf_op jit(solution)/shard_map/ppermute | solution.py:356
  55.5 24.5 %collective-permute-start.15 = (bf16[8,24,1536]{2,1,0:T(8,128)(2,1)S(1)}, bf16[8,24,1536]{2,1,0:T(8,128)(2,1)S(1)}, u32[]{:S(2)}, u32[]{:S(2)}) collective-permute-start(bf16[8,24,1536]{2,1,0:T(8,128)(2,1)S(1)} %bitcast.408), channel_id=1, source_target_pairs={{0,1},{1,0},{2,3},{3,2},{4,5},{5,4},{6,7},{7,6},{8,9},{9,8},{10,11... | collective-permute-start | bytes 1769480 | tf_op jit(solution)/shard_map/ppermute | solution.py:356
  61.8 20.9 %collective-permute-start.19 = (bf16[8,24,1536]{2,1,0:T(8,128)(2,1)S(1)}, bf16[8,24,1536]{2,1,0:T(8,128)(2,1)S(1)}, u32[]{:S(2)}, u32[]{:S(2)}) collective-permute-start(bf16[8,24,1536]{2,1,0:T(8,128)(2,1)S(1)} %bitcast.409), channel_id=1, source_target_pairs={{0,1},{1,0},{2,3},{3,2},{4,5},{5,4},{6,7},{7,6},{8,9},{9,8},{10,11... | collective-permute-start | bytes 1769480 | tf_op jit(solution)/shard_map/ppermute | solution.py:356
  68.6 15.4 %collective-permute-start.23 = (bf16[8,96,384]{2,1,0:T(8,128)(2,1)S(1)}, bf16[8,96,384]{2,1,0:T(8,128)(2,1)S(1)}, u32[]{:S(2)}, u32[]{:S(2)}) collective-permute-start(bf16[8,96,384]{2,1,0:T(8,128)(2,1)S(1)} %bitcast.410), channel_id=1, source_target_pairs={{0,1},{1,0},{2,3},{3,2},{4,5},{5,4},{6,7},{7,6},{8,9},{9,8},{10,11... | collective-permute-start | bytes 1769480 | tf_op jit(solution)/shard_map/ppermute | solution.py:356
  74.9 13.5 %collective-permute-start.3 = (bf16[8,24,1664]{2,1,0:T(8,128)(2,1)S(1)}, bf16[8,24,1664]{2,1,0:T(8,128)(2,1)S(1)}, u32[]{:S(2)}, u32[]{:S(2)}) collective-permute-start(bf16[8,24,1664]{2,1,0:T(8,128)(2,1)S(1)} %bitcast.405), channel_id=1, source_target_pairs={{0,1},{1,0},{2,3},{3,2},{4,5},{5,4},{6,7},{7,6},{8,9},{9,8},{10,11... | collective-permute-start | bytes 1916936 | tf_op jit(solution)/shard_map/ppermute | solution.py:356
  292.8 15.6 %collective-permute-start.40 = (bf16[4,24,1536]{2,1,0:T(8,128)(2,1)S(1)}, bf16[4,24,1536]{2,1,0:T(8,128)(2,1)S(1)}, u32[]{:S(2)}, u32[]{:S(2)}) collective-permute-start(bf16[4,24,1536]{2,1,0:T(8,128)(2,1)S(1)} %dynamic-slice_bitcast_fusion.9), channel_id=1, source_target_pairs={{0,2},{1,3},{2,0},{3,1},{4,6},{5,7},{6,4},{7,5},{8,10},{9,11},{10,... | collective-permute-start | bytes 884744 | tf_op jit(solution)/shard_map/ppermute | solution.py:371
  294.8 20.0 %collective-permute-start.35 = (bf16[4,24,1536]{2,1,0:T(8,128)(2,1)S(1)}, bf16[4,24,1536]{2,1,0:T(8,128)(2,1)S(1)}, u32[]{:S(2)}, u32[]{:S(2)}) collective-permute-start(bf16[4,24,1536]{2,1,0:T(8,128)(2,1)S(1)} %dynamic-slice_bitcast_fusion.10), channel_id=1, source_target_pairs={{0,2},{1,3},{2,0},{3,1},{4,6},{5,7},{6,4},{7,5},{8,10},{9,11},{10,... | collective-permute-start | bytes 884744 | tf_op jit(solution)/shard_map/ppermute | solution.py:371
  295.3 25.7 %collective-permute-start.50 = (bf16[4,96,384]{2,1,0:T(8,128)(2,1)S(1)}, bf16[4,96,384]{2,1,0:T(8,128)(2,1)S(1)}, u32[]{:S(2)}, u32[]{:S(2)}) collective-permute-start(bf16[4,96,384]{2,1,0:T(8,128)(2,1)S(1)} %dynamic-slice_bitcast_fusion.7), channel_id=1, source_target_pairs={{0,2},{1,3},{2,0},{3,1},{4,6},{5,7},{6,4},{7,5},{8,10},{9,11},{10,... | collective-permute-start | bytes 884744 | tf_op jit(solution)/shard_map/ppermute | solution.py:371
  297.4 30.0 %collective-permute-start.45 = (bf16[4,96,384]{2,1,0:T(8,128)(2,1)S(1)}, bf16[4,96,384]{2,1,0:T(8,128)(2,1)S(1)}, u32[]{:S(2)}, u32[]{:S(2)}) collective-permute-start(bf16[4,96,384]{2,1,0:T(8,128)(2,1)S(1)} %dynamic-slice_bitcast_fusion.8), channel_id=1, source_target_pairs={{0,2},{1,3},{2,0},{3,1},{4,6},{5,7},{6,4},{7,5},{8,10},{9,11},{10,... | collective-permute-start | bytes 884744 | tf_op jit(solution)/shard_map/ppermute | solution.py:371
  302.1 31.4 %collective-permute-start.25 = (bf16[4,24,1664]{2,1,0:T(8,128)(2,1)S(1)}, bf16[4,24,1664]{2,1,0:T(8,128)(2,1)S(1)}, u32[]{:S(2)}, u32[]{:S(2)}) collective-permute-start(bf16[4,24,1664]{2,1,0:T(8,128)(2,1)S(1)} %dynamic-slice_bitcast_fusion.6), channel_id=1, source_target_pairs={{0,2},{1,3},{2,0},{3,1},{4,6},{5,7},{6,4},{7,5},{8,10},{9,11},{10,... | collective-permute-start | bytes 958472 | tf_op jit(solution)/shard_map/ppermute | solution.py:371
  308.4 25.2 %collective-permute-start.31 = (bf16[2,24,1536]{2,1,0:T(8,128)(2,1)S(1)}, bf16[2,24,1536]{2,1,0:T(8,128)(2,1)S(1)}, u32[]{:S(2)}, u32[]{:S(2)}) collective-permute-start(bf16[2,24,1536]{2,1,0:T(8,128)(2,1)S(1)} %dynamic-slice_bitcast_fusion.17), channel_id=1, source_target_pairs={{0,4},{1,5},{2,6},{3,7},{4,0},{5,1},{6,2},{7,3},{8,12},{9,13},{10,... | collective-permute-start | bytes 442376 | tf_op jit(solution)/shard_map/ppermute | solution.py:371
  314.8 21.1 %collective-permute-start.41 = (bf16[2,24,1536]{2,1,0:T(8,128)(2,1)S(1)}, bf16[2,24,1536]{2,1,0:T(8,128)(2,1)S(1)}, u32[]{:S(2)}, u32[]{:S(2)}) collective-permute-start(bf16[2,24,1536]{2,1,0:T(8,128)(2,1)S(1)} %dynamic-slice_bitcast_fusion.15), channel_id=1, source_target_pairs={{0,4},{1,5},{2,6},{3,7},{4,0},{5,1},{6,2},{7,3},{8,12},{9,13},{10,... | collective-permute-start | bytes 442376 | tf_op jit(solution)/shard_map/ppermute | solution.py:371
  321.1 15.7 %collective-permute-start.36 = (bf16[2,24,1536]{2,1,0:T(8,128)(2,1)S(1)}, bf16[2,24,1536]{2,1,0:T(8,128)(2,1)S(1)}, u32[]{:S(2)}, u32[]{:S(2)}) collective-permute-start(bf16[2,24,1536]{2,1,0:T(8,128)(2,1)S(1)} %dynamic-slice_bitcast_fusion.16), channel_id=1, source_target_pairs={{0,4},{1,5},{2,6},{3,7},{4,0},{5,1},{6,2},{7,3},{8,12},{9,13},{10,... | collective-permute-start | bytes 442376 | tf_op jit(solution)/shard_map/ppermute | solution.py:371
  333.7 22.3 %collective-permute-start.26 = (bf16[2,24,1664]{2,1,0:T(8,128)(2,1)S(1)}, bf16[2,24,1664]{2,1,0:T(8,128)(2,1)S(1)}, u32[]{:S(2)}, u32[]{:S(2)}) collective-permute-start(bf16[2,24,1664]{2,1,0:T(8,128)(2,1)S(1)} %dynamic-slice_bitcast_fusion.12), channel_id=1, source_target_pairs={{0,4},{1,5},{2,6},{3,7},{4,0},{5,1},{6,2},{7,3},{8,12},{9,13},{10,... | collective-permute-start | bytes 479240 | tf_op jit(solution)/shard_map/ppermute | solution.py:371
  336.8 13.4 %collective-permute-start.42 = (bf16[1,24,1536]{2,1,0:T(8,128)(2,1)S(1)}, bf16[1,24,1536]{2,1,0:T(8,128)(2,1)S(1)}, u32[]{:S(2)}, u32[]{:S(2)}) collective-permute-start(bf16[1,24,1536]{2,1,0:T(8,128)(2,1)S(1)} %constant_dynamic-slice_fusion.2), channel_id=1, source_target_pairs={{0,8},{1,9},{2,10},{3,11},{4,12},{5,13},{6,14},{7,15},{8,0},{9,1},... | collective-permute-start | bytes 221192 | tf_op jit(solution)/shard_map/ppermute | solution.py:371
  339.1 13.5 %collective-permute-start.37 = (bf16[1,24,1536]{2,1,0:T(8,128)(2,1)S(1)}, bf16[1,24,1536]{2,1,0:T(8,128)(2,1)S(1)}, u32[]{:S(2)}, u32[]{:S(2)}) collective-permute-start(bf16[1,24,1536]{2,1,0:T(8,128)(2,1)S(1)} %constant_dynamic-slice_fusion.3), channel_id=1, source_target_pairs={{0,8},{1,9},{2,10},{3,11},{4,12},{5,13},{6,14},{7,15},{8,0},{9,1},... | collective-permute-start | bytes 221192 | tf_op jit(solution)/shard_map/ppermute | solution.py:371
  (44 other events, 508.8 us)

commit v2 on v1

v2 whole, which is shorter than its diff:
```python
import functools
import jax
import jax.numpy as jnp
from jax import lax
from jax.sharding import PartitionSpec as P
from jax.experimental import pallas as pl
from jax.experimental.pallas import tpu as pltpu

BF = jnp.bfloat16
F32 = jnp.float32
HEADS = 6
EPS = 1e-06
NEG = -1e30
VMEM_LIMIT = 60 * 2**20


def dot(a, b):
    return jnp.dot(a, b, preferred_element_type=F32)


def dot_nt(a, b):
    return lax.dot_general(a, b, (((1,), (1,)), ((), ())), preferred_element_type=F32)


def dot_tn(a, b):
    return lax.dot_general(a, b, (((0,), (0,)), ((), ())), preferred_element_type=F32)


def pad_rows(seq):
    return (seq + 15) // 16 * 16


def colsum(x):
    return jnp.sum(x, 0, keepdims=True)


def slot_masks(n):
    masks = [0]
    b = n // 2
    while b > 1:
        masks = masks + [m ^ b for m in masks]
        b //= 2
    return masks


def start_weights(own, other, dst, sems):
    idx = lax.axis_index("shard")
    for s, mask in enumerate(slot_masks(dst.shape[0])):
        pltpu.make_async_copy(own.at[s], dst.at[jnp.bitwise_xor(idx, mask)], sems.at[2 * s]).start()
        pltpu.make_async_copy(other.at[s], dst.at[jnp.bitwise_xor(idx, mask + 1)], sems.at[2 * s + 1]).start()


def wait_weights(own, other, dst, sems):
    idx = lax.axis_index("shard")
    for s, mask in enumerate(slot_masks(dst.shape[0])):
        pltpu.make_async_copy(own.at[s], dst.at[jnp.bitwise_xor(idx, mask)], sems.at[2 * s]).wait()
        pltpu.make_async_copy(other.at[s], dst.at[jnp.bitwise_xor(idx, mask + 1)], sems.at[2 * s + 1]).wait()


def first_step(*fs):
    @pl.when(pl.program_id(0) == 0)
    def _():
        for f in fs:
            f()


def flat(v):
    return v.reshape(v.shape[0] * v.shape[1], v.shape[2])


def slabs(w, first, count):
    return jnp.concatenate([flat(w[:, k]) for k in range(first, first + count)], 1) if count > 1 else flat(w[:, first])


def tall(w, first, count):
    v = w[:, first : first + count]
    return v.reshape(v.shape[0] * v.shape[1] * v.shape[2], v.shape[3])


def store_slots(keep, send, pieces):
    half = keep.shape[0]
    idx = lax.axis_index("shard")
    for s, mask in enumerate(slot_masks(2 * half)):
        for dst, extra in ((keep, 0), (send, 1)):
            owner = jnp.bitwise_xor(idx, mask + extra)
            for k, piece in enumerate(pieces):
                dst[s, k] = piece(owner).astype(dst.dtype)


def rows_of(ref, part, col, width):
    return lambda owner: ref[pl.ds(pl.multiple_of(owner * part, 8), part), col * width : (col + 1) * width]


def tall_rows_of(ref, part, q, count):
    return lambda owner: ref[pl.ds(pl.multiple_of((owner * count + q) * part, 8), part), :]


def normalise(x):
    mean = jnp.mean(x, -1, keepdims=True)
    cen = x - mean
    rstd = lax.rsqrt(jnp.mean(cen * cen, -1, keepdims=True) + EPS)
    return cen * rstd, rstd


def norm_back(dxhat, xhat, rstd):
    return rstd * (
        dxhat
        - jnp.mean(dxhat, -1, keepdims=True)
        - xhat * jnp.mean(dxhat * xhat, -1, keepdims=True)
    )


def gelu_both(h):
    phi = 0.5 + 0.5 * lax.erf(h * 0.7071067811865476)
    return h * phi, phi + h * (jnp.exp(h * h * -0.5) * 0.3989422804014327)


def to_rows(cols):
    return cols.T[0:8]


def to_column(rows8, r):
    full = jnp.concatenate([rows8, jnp.zeros((120, rows8.shape[1]), F32)], 0)
    return full.T[:, r : r + 1]


def load_padded(dst, src, seq, rows, images):
    for g in range(images):
        dst[g * rows : g * rows + seq] = src[g].astype(F32)
        dst[g * rows + seq : (g + 1) * rows] = jnp.zeros((rows - seq, dst.shape[1]), F32)


def pack_kernel(*refs):
    smalls, (bias_up, w_qkv, w_proj, w_up, w_down) = refs[:8], refs[8:13]
    out_a0, out_m0, out_l1, sq = refs[13:]
    part, width = out_a0.shape[1:]
    sq[...] = jnp.zeros_like(sq)
    for p, ref in enumerate(smalls):
        sq[2 * p : 2 * p + 2, 0:part] = ref[...].astype(F32)
    hid = bias_up.shape[1]
    out_a0[3] = jnp.zeros((part, width), BF)
    out_a0[3, :, 0:128] = sq[...].T[0:part].astype(BF)
    out_a0[3, 0:2, width - hid :] = bias_up[...]
    quart = w_up.shape[2] // width
    for layer in range(2):
        attn = out_a0 if layer == 0 else out_l1
        rest, base = (out_m0, 0) if layer == 0 else (out_l1, 3)
        for k in range(3):
            attn[k] = w_qkv[layer, :, k * width : (k + 1) * width]
        rest[base] = w_proj[layer]
        for q in range(quart):
            rest[base + 1 + q] = w_up[layer, :, q * width : (q + 1) * width]
            rest[base + 1 + quart + q] = w_down[layer, q * part : (q + 1) * part]


def unpack_small(w, vec, tmp):
    shards, _, part, width = w.shape
    hid = tmp.shape[1] // shards
    rows = flat(w[:, 3, :, 0:128]).astype(F32).T
    for j in range(shards):
        tmp[:, j * hid : (j + 1) * hid] = w[j, 3, 0:2, width - hid :].astype(F32)
    quart = tmp.shape[1] // width
    for layer in range(2):
        for p in range(8):
            vec[layer, p : p + 1] = rows[2 * p + layer : 2 * p + layer + 1]
        for q in range(quart):
            vec[layer, 8 + q : 9 + q] = tmp[layer : layer + 1, q * width : (q + 1) * width]
        vec[layer, 8 + quart :] = jnp.zeros((8 - quart, width), F32)


def fa_kernel(seq, layer, x_ref, *refs):
    if layer == 0:
        own, other, m_ref, o_ref, aux_ref, xh_ref, vec_ref, xs, w, sems, tmp = refs
    else:
        vec_ref, own, other, m_ref, o_ref, aux_ref, xh_ref, xs, w, sems = refs
    vec = vec_ref.at[layer]
    first_step(lambda: start_weights(own, other, w, sems))
    images = x_ref.shape[0]
    rows = pad_rows(seq)
    width = x_ref.shape[2]
    load_padded(xs, x_ref, seq, rows, images)
    xhat, rstd = normalise(xs[...])
    xh_ref[...] = xhat.astype(BF).reshape(images, rows, width)
    first_step(lambda: wait_weights(own, other, w, sems))
    if layer == 0:
        first_step(lambda: unpack_small(w, vec_ref, tmp))
    n1 = (xhat * vec[0:1, :] + vec[1:2, :]).astype(BF)
    for c in range(3):
        cs = slice(c * width, (c + 1) * width)
        mc = dot(n1, slabs(w, c, 1))
        if c != 1:
            mc = mc + (vec[2:3, :] if c == 0 else vec[3:4, :])
        m_ref[:, :, cs] = mc.astype(BF).reshape(images, rows, width)
    lane = lax.broadcasted_iota(jnp.int32, (rows, 128), 1)
    row = lax.broadcasted_iota(jnp.int32, (rows, 128), 0)
    low = lane < 64
    kpad = jnp.where(row >= seq, NEG, 0.0).astype(BF)
    ones = jnp.where(row >= seq, 0.0, 1.0).astype(BF)
    qone0 = jnp.where(lane == 64, 1.0, 0.0).astype(BF)
    qone1 = jnp.where(lane == 0, 1.0, 0.0).astype(BF)
    valid = row < seq
    for g in range(images):
        aux = jnp.broadcast_to(rstd[g * rows : (g + 1) * rows], (rows, 128))
        for p in range(width // 128):
            q2 = m_ref[g, :, p * 128 : (p + 1) * 128] * jnp.asarray(0.125, BF)
            k2 = m_ref[g, :, width + p * 128 : width + (p + 1) * 128]
            v2 = m_ref[g, :, 2 * width + p * 128 : 2 * width + (p + 1) * 128]
            v2 = jnp.where(valid, v2, jnp.zeros_like(v2))
            vext = jnp.concatenate([v2, ones], 1)
            parts = []
            for half in range(2):
                mine = low if half == 0 else ~low
                qh = jnp.where(mine, q2, qone0 if half == 0 else qone1)
                kh = jnp.where(mine, k2, kpad)
                s = dot_nt(qh, kh)
                mx = jnp.max(s, -1, keepdims=True)
                pr = jnp.exp(s - mx).astype(BF)
                oe = dot(pr, vext)
                tot = oe[:, 128:]
                parts.append(oe[:, :128] / tot)
                aux = jnp.where(lane == 2 * p + half, mx + jnp.log(tot), aux)
            o_ref[g, :, p * 128 : (p + 1) * 128] = jnp.where(low, parts[0], parts[1]).astype(BF)
        aux_ref[g] = to_rows(aux)


def fm_kernel(seq, layer, x_ref, o_ref, vec_ref, own, other, out_ref, a_ref, d_ref, xh_ref, rs_ref, xs, w, sems):
    vec = vec_ref.at[layer]
    first_step(lambda: start_weights(own, other, w, sems))
    images, rows, width = o_ref.shape
    n = images * rows
    load_padded(xs, x_ref, seq, rows, images)
    first_step(lambda: wait_weights(own, other, w, sems))
    x1 = xs[...] + dot(flat(o_ref[...]), slabs(w, 0, 1)) + vec[4:5, :]
    xhat, rstd = normalise(x1)
    xh_ref[...] = xhat.astype(BF).reshape(images, rows, width)
    for g in range(images):
        rs_ref[g] = to_rows(jnp.broadcast_to(rstd[g * rows : (g + 1) * rows], (rows, 128)))
    n2 = (xhat * vec[5:6, :] + vec[6:7, :]).astype(BF)
    acc = x1 + vec[7:8, :]
    quart = (w.shape[1] - 1) // 2
    w2 = tall(w, 1 + quart, quart)
    for c in range(quart // 2):
        cs = slice(2 * c * width, 2 * (c + 1) * width)
        bias = jnp.concatenate([vec[8 + 2 * c : 9 + 2 * c, :], vec[9 + 2 * c : 10 + 2 * c, :]], 1)
        h = dot(n2, slabs(w, 1 + 2 * c, 2)) + bias
        a, d = gelu_both(h)
        a = a.astype(BF)
        a_ref[:, :, cs] = a.reshape(images, rows, 2 * width)
        d_ref[:, :, cs] = d.astype(BF).reshape(images, rows, 2 * width)
        acc = acc + dot(a, w2[cs, :])
    acc = acc.reshape(images, rows, width)
    for g in range(images):
        out_ref[g] = acc[g, :seq]


def bm_kernel(seq, layer, gr_ref, a_ref, d_ref, xh_ref, rs_ref, o_ref, vec_ref, own, other,
              dx1_ref, do_ref, keep, send, vec_o, db1_o, gs, dwp, dw1, dw2, w, sems):
    vec = vec_ref.at[layer]
    images, rows, width = xh_ref.shape
    n = images * rows
    shards, _, part, _ = w.shape
    step = pl.program_id(0)
    first_step(lambda: start_weights(own, other, w, sems))

    @pl.when(step == 0)
    def _():
        dwp[...] = jnp.zeros_like(dwp)
        dw1[...] = jnp.zeros_like(dw1)
        dw2[...] = jnp.zeros_like(dw2)
        vec_o[...] = jnp.zeros_like(vec_o)
        db1_o[...] = jnp.zeros_like(db1_o)

    load_padded(gs, gr_ref, seq, rows, images)
    dz = gs[...].astype(BF)
    xhat = flat(xh_ref[...]).astype(F32)
    n2 = (xhat * vec[5:6, :] + vec[6:7, :]).astype(BF)
    dn2 = jnp.zeros((n, width), F32)
    first_step(lambda: wait_weights(own, other, w, sems))
    quart = (w.shape[1] - 1) // 2
    w2 = tall(w, 1 + quart, quart)
    for c in range(quart // 2):
        cs = slice(2 * c * width, 2 * (c + 1) * width)
        a = flat(a_ref[:, :, cs])
        d = flat(d_ref[:, :, cs])
        da = dot_nt(dz, w2[cs, :])
        dh = (d.astype(F32) * da).astype(BF)
        db1_o[:, cs] += colsum(dh.astype(F32))
        dw2[cs, :] += dot_tn(a, dz)
        dw1[:, cs] += dot_tn(n2, dh)
        dn2 = dn2 + dot_nt(dh, slabs(w, 1 + 2 * c, 2))
    rstd = jnp.concatenate([to_column(rs_ref[g], 0) for g in range(images)], 0)
    dx1 = gs[...] + norm_back(dn2 * vec[5:6, :], xhat, rstd)
    dx1_ref[...] = dx1.reshape(images, rows, width)
    dy = dx1.astype(BF)
    dwp[...] += dot_tn(flat(o_ref[...]), dy)
    do_ref[...] = dot_nt(dy, slabs(w, 0, 1)).astype(BF).reshape(images, rows, width)
    vec_o[0:1, :] += colsum(dz.astype(F32))
    vec_o[1:2, :] += colsum(dn2 * xhat)
    vec_o[2:3, :] += colsum(dn2)
    vec_o[3:4, :] += colsum(dy.astype(F32))

    @pl.when(step == pl.num_programs(0) - 1)
    def _():
        store_slots(keep, send,
                    [rows_of(dwp, part, 0, width)]
                    + [rows_of(dw1, part, q, width) for q in range(quart)]
                    + [tall_rows_of(dw2, part, q, quart) for q in range(quart)])


def bs_kernel(seq, m_ref, o_ref, do_ref, aux_ref, *rest):
    dm_ref = rest[-1]
    images, rows, width = o_ref.shape
    lane = lax.broadcasted_iota(jnp.int32, (rows, 128), 1)
    low = lane < 64
    last = rows - 16
    valid = lax.broadcasted_iota(jnp.int32, (16, rows), 0) < seq - last
    head = lax.broadcasted_iota(jnp.int32, (8, width), 0)
    pick = jnp.where(lax.broadcasted_iota(jnp.int32, (8, width), 1) // 64 == head, 1.0, 0.0).astype(BF)
    zero = jnp.zeros((rows, 128), BF)
    for g in range(images):
        lse = aux_ref[g]
        inner = dot_nt(pick, (o_ref[g].astype(F32) * do_ref[g].astype(F32)).astype(BF))
        for p in range(width // 128):
            q2 = m_ref[g, :, p * 128 : (p + 1) * 128] * jnp.asarray(0.125, BF)
            k2 = m_ref[g, :, width + p * 128 : width + (p + 1) * 128]
            v2 = m_ref[g, :, 2 * width + p * 128 : 2 * width + (p + 1) * 128]
            do2 = do_ref[g, :, p * 128 : (p + 1) * 128]
            kt = (k2 * jnp.asarray(0.125, BF)).T
            dks, dvs, dqs = [], [], []
            for half in range(2):
                h = 2 * p + half
                kh = jnp.where(low, k2, zero) if half == 0 else jnp.where(low, zero, k2)
                vh = jnp.where(low, v2, zero) if half == 0 else jnp.where(low, zero, v2)
                st = dot_nt(kh, q2) - lse[h : h + 1, :]
                pt = jnp.exp(jnp.concatenate([st[:last], jnp.where(valid, st[last:], NEG)], 0))
                dst = (pt * (dot_nt(vh, do2) - inner[h : h + 1, :])).astype(BF)
                dvs.append(dot(pt.astype(BF), do2))
                dks.append(dot(dst, q2))
                dqs.append(dot(kt[half * 64 : half * 64 + 64], dst))
            dq = jnp.concatenate(dqs, 0).T
            dm_ref[g, :, p * 128 : (p + 1) * 128] = dq.astype(BF)
            dm_ref[g, :, width + p * 128 : width + (p + 1) * 128] = jnp.where(low, dks[0], dks[1]).astype(BF)
            dm_ref[g, :, 2 * width + p * 128 : 2 * width + (p + 1) * 128] = jnp.where(low, dvs[0], dvs[1]).astype(BF)


def bq_kernel(seq, layer, dx1_ref, dm_ref, xh_ref, aux_ref, vec_ref, vec2, db1, own, other,
              dx_ref, keep, send, dwqkv, vec_s, dbm_s, w, sems, sm):
    vec = vec_ref.at[layer]
    images, rows, width = xh_ref.shape
    n = images * rows
    shards, _, part, _ = w.shape
    step = pl.program_id(0)
    first_step(lambda: start_weights(own, other, w, sems))

    @pl.when(step == 0)
    def _():
        dwqkv[...] = jnp.zeros_like(dwqkv)
        vec_s[...] = jnp.zeros_like(vec_s)
        dbm_s[...] = jnp.zeros_like(dbm_s)

    dm = flat(dm_ref[...])
    dbm_s[...] += colsum(dm.astype(F32))
    xhat = flat(xh_ref[...]).astype(F32)
    n1 = (xhat * vec[0:1, :] + vec[1:2, :]).astype(BF)
    dwqkv[...] += dot_tn(n1, dm)
    first_step(lambda: wait_weights(own, other, w, sems))
    dn1 = dot_nt(dm, slabs(w, 0, 3))
    vec_s[0:1, :] += colsum(dn1 * xhat)
    vec_s[1:2, :] += colsum(dn1)
    rstd = jnp.concatenate([to_column(aux_ref[g], 7) for g in range(images)], 0)
    dx = flat(dx1_ref[...]) + norm_back(dn1 * vec[0:1, :], xhat, rstd)
    dx = dx.reshape(images, rows, width)
    for g in range(images):
        dx_ref[g] = dx[g, :seq]

    @pl.when(step == pl.num_programs(0) - 1)
    def _():
        small = jnp.concatenate(
            [vec_s[0:2, :], dbm_s[:, :width], dbm_s[:, 2 * width :], vec2[3:4, :], vec2[1:3, :], vec2[0:1, :],
             jnp.zeros((120, width), F32)], 0)
        sm[...] = jnp.zeros_like(sm)
        sm[:, 0:128] = small.T
        hid = db1.shape[1] // shards
        for j in range(shards):
            sm[j * part : j * part + 1, width - hid :] = db1[:, j * hid : (j + 1) * hid]
        store_slots(keep, send, [rows_of(dwqkv, part, k, width) for k in range(3)] + [rows_of(sm, part, 0, width)])


def finish_kernel(*refs):
    ins, outs = refs[:8], refs[8:]
    o_qkv, o_proj, o_up, o_down, o_bup = outs[:5]
    smalls = outs[5:]
    part, width = ins[0].shape[1:]
    hid = o_bup.shape[1]
    quart = o_up.shape[2] // width
    for layer in range(2):
        a1, a2, m1, m2 = ins[4 * layer : 4 * layer + 4]
        for k in range(3):
            o_qkv[layer, :, k * width : (k + 1) * width] = a1[k].astype(F32) + a2[k].astype(F32)
        small = a1[3].astype(F32) + a2[3].astype(F32)
        o_bup[layer : layer + 1, :] = small[0:1, width - hid :]
        pad = jnp.concatenate([small[:, 0:128], jnp.zeros((128 - part, 128), F32)], 0).T
        for p, ref in enumerate(smalls):
            ref[layer : layer + 1, :] = pad[p : p + 1, 0:part]
        o_proj[layer] = m1[0].astype(F32) + m2[0].astype(F32)
        for q in range(quart):
            o_up[layer, :, q * width : (q + 1) * width] = m1[1 + q].astype(F32) + m2[1 + q].astype(F32)
            o_down[layer, q * part : (q + 1) * part] = m1[1 + quart + q].astype(F32) + m2[1 + quart + q].astype(F32)


def blk(shape):
    nd = len(shape)
    return pl.BlockSpec(shape, lambda i: (i,) + (0,) * (nd - 1))


def whole(arr):
    nd = len(arr.shape)
    return pl.BlockSpec(arr.shape, lambda i: (0,) * nd)


def anyspec():
    return pl.BlockSpec(memory_space=pl.ANY)


def sds(shape, dt):
    return jax.ShapeDtypeStruct(shape, dt)


COST = {"fa": 14, "fm": 18, "bm": 27, "bq": 13}


def call(kern, name, per, blocked_in, whole_in, any_in, blocked_out, whole_out, scratch):
    in_specs = [blk((per,) + a.shape[1:]) for a in blocked_in] + [whole(a) for a in whole_in] + [anyspec() for _ in any_in]
    out_specs = [blk((per,) + a.shape[1:]) for a in blocked_out] + [whole(a) for a in whole_out]
    return pl.pallas_call(
        kern,
        grid=(blocked_in[0].shape[0] // per,),
        in_specs=in_specs,
        out_specs=out_specs,
        out_shape=list(blocked_out) + list(whole_out),
        scratch_shapes=scratch,
        compiler_params=pltpu.CompilerParams(vmem_limit_bytes=VMEM_LIMIT),
        name=name,
        cost_estimate=pl.CostEstimate(flops=COST[name] * 1_150_000_000, bytes_accessed=0, transcendentals=0),
    )(*blocked_in, *whole_in, *any_in)


def wscratch(own):
    return [pltpu.VMEM((2 * own.shape[0],) + own.shape[1:], BF), pltpu.SemaphoreType.DMA((2 * own.shape[0],))]


def run_pack(smalls, bias_up, w_qkv, w_proj, w_up, w_down):
    part, width = w_proj.shape[1:]
    quart = w_up.shape[2] // width
    return pl.pallas_call(
        pack_kernel,
        out_shape=[sds((4, part, width), BF), sds((1 + 2 * quart, part, width), BF), sds((4 + 2 * quart, part, width), BF)],
        scratch_shapes=[pltpu.VMEM((128, 128), F32)],
        name="pack",
    )(*smalls, bias_up, w_qkv, w_proj, w_up, w_down)


def run_fa(x, layer, vec, wa, ff, per):
    images, seq, width = x.shape
    rows = pad_rows(seq)
    outs = [sds((images, rows, 3 * width), BF), sds((images, rows, width), BF), sds((images, 8, rows), F32),
            sds((images, rows, width), BF)]
    scratch = [pltpu.VMEM((per * rows, width), F32)] + wscratch(wa[0])
    if layer == 0:
        return call(functools.partial(fa_kernel, seq, 0), "fa", per, [x], [], wa, outs, [sds((2, 16, width), F32)],
                    scratch + [pltpu.VMEM((2, ff), F32)])
    return call(functools.partial(fa_kernel, seq, 1), "fa", per, [x], [vec], wa, outs, [], scratch)


def run_fm(x, layer, o, vec, wm, per):
    images, seq, width = x.shape
    rows = o.shape[1]
    ff = (wm[0].shape[1] - 1) // 2 * width
    return call(
        functools.partial(fm_kernel, seq, layer), "fm", per, [x, o], [vec], wm,
        [sds((images, seq, width), F32), sds((images, rows, ff), BF), sds((images, rows, ff), BF),
         sds((images, rows, width), BF), sds((images, 8, rows), F32)], [],
        [pltpu.VMEM((per * rows, width), F32)] + wscratch(wm[0]))


def slots(own, count):
    half, _, part, width = own.shape
    return [sds((half, count, part, width), F32), sds((half, count, part, width), BF)]


def run_bm(gr, layer, a, d, xh, rs, o, vec, wm, per):
    images, seq, width = gr.shape
    rows, ff = a.shape[1:]
    return call(
        functools.partial(bm_kernel, seq, layer), "bm", per, [gr, a, d, xh, rs, o], [vec], wm,
        [sds((images, rows, width), F32), sds((images, rows, width), BF)],
        slots(wm[0], wm[0].shape[1]) + [sds((8, width), F32), sds((1, ff), F32)],
        [pltpu.VMEM((per * rows, width), F32), pltpu.VMEM((width, width), F32), pltpu.VMEM((width, ff), F32),
         pltpu.VMEM((ff, width), F32)] + wscratch(wm[0]))


def run_bs(seq, m, o, do, aux, per, first=0, count=None, prev=None):
    count = count or m.shape[0] - first
    base = first // per

    def at(shape):
        nd = len(shape)
        return pl.BlockSpec((per,) + shape[1:], lambda i: (i + base,) + (0,) * (nd - 1))

    more = [] if prev is None else [prev]
    return pl.pallas_call(
        functools.partial(bs_kernel, seq),
        grid=(count // per,),
        in_specs=[at(a.shape) for a in (m, o, do, aux)] + [anyspec() for _ in more],
        out_specs=at(m.shape),
        out_shape=sds(m.shape, BF),
        input_output_aliases={4: 0} if more else {},
        compiler_params=pltpu.CompilerParams(vmem_limit_bytes=VMEM_LIMIT),
        name="bs",
        cost_estimate=pl.CostEstimate(flops=18 * count // m.shape[0] * 1_150_000_000, bytes_accessed=0, transcendentals=0),
    )(m, o, do, aux, *more)


def run_bq(seq, layer, dx1, dm, xh, aux, vec, vec2, db1, wa, per):
    images, rows, width = dx1.shape
    return call(
        functools.partial(bq_kernel, seq, layer), "bq", per, [dx1, dm, xh, aux], [vec, vec2, db1], wa,
        [sds((images, seq, width), F32)], slots(wa[0], 4),
        [pltpu.VMEM((width, 3 * width), F32), pltpu.VMEM((8, width), F32), pltpu.VMEM((1, 3 * width), F32)]
        + wscratch(wa[0]) + [pltpu.VMEM((width, width), F32)])


def run_finish(a0, m0, a1, m1, ff):
    part, width = a0[0].shape[1:]
    return pl.pallas_call(
        finish_kernel,
        out_shape=[sds((2, part, 3 * width), F32), sds((2, part, width), F32), sds((2, part, ff), F32),
                   sds((2, ff // width * part, width), F32), sds((2, ff // width * part), F32)]
        + [sds((2, part), F32)] * 8,
        name="finish",
    )(*a0, *m0, *a1, *m1)


def xor_pairs(count, b):
    return [(i, i ^ b) for i in range(count)]


def tie(value, *others):
    return lax.optimization_barrier((value, *others))[0]


def group(*values):
    return lax.optimization_barrier(values)


def body(n, reps, tokens, norm1_gain, norm1_shift, qkv_weight, query_bias, value_bias, proj_weight, proj_bias,
         norm2_gain, norm2_shift, fc1_weight, fc1_bias, fc2_weight, fc2_bias, cotangent):
    images, seq, width = tokens.shape
    ff = fc1_weight.shape[2]
    per = 2 if images % 2 == 0 else 1
    upper = []
    b = n // 2
    while b > 2:
        upper.append(b)
        b //= 2

    def swap(x, b):
        return lax.ppermute(x, "shard", xor_pairs(n, b))

    def grow(x, b):
        return jnp.concatenate([x, swap(x, b)])

    def direct(x):
        masks = [0]
        for b in upper:
            masks = masks + [m ^ b for m in masks]
        return [x] + [swap(x, m) for m in masks[1:]]

    smalls = [norm1_gain, norm1_shift, query_bias, value_bias, proj_bias, norm2_gain, norm2_shift, fc2_bias]
    a0, m0, l1 = run_pack(smalls, fc1_bias, qkv_weight, proj_weight, fc1_weight, fc2_weight)

    a0 = jnp.stack(direct(a0))
    m0 = direct(tie(m0, a0))
    a0x = swap(a0, 2)
    a0 = jnp.concatenate([a0, a0x])
    a0 = (a0, swap(a0, 1))
    m0 = jnp.stack([m0[0]] + [tie(y, a0x) for y in m0[1:]])
    m0x = swap(m0, 2)
    l1 = direct(tie(l1, m0))
    mix0, o0, aux0, xa0, vec = run_fa(tie(tokens, m0, l1[0]), 0, None, a0, ff, per)
    o0, m0x, *l1 = group(o0, m0x, *l1)
    m0 = jnp.concatenate([m0, m0x])
    l1 = jnp.stack(l1)
    m0 = (m0, swap(tie(m0, l1), 1))
    l1x = swap(l1, 2)
    layer_one, act0, der0, xm0, rs0 = run_fm(tokens, 0, o0, vec, m0, per)
    layer_one, l1x = group(layer_one, l1x)
    a1 = jnp.concatenate([l1[:, :3], l1x[:, :3]])
    m1 = jnp.concatenate([l1[:, 3:], l1x[:, 3:]])
    a1 = (a1, swap(a1, 1))
    m1x = swap(m1, 1)
    mix1, o1, aux1, xa1 = run_fa(tie(layer_one, m1), 1, vec, a1, ff, per)
    o1, m1x = group(o1, m1x)
    m1 = (m1, m1x)
    layer_two, act1, der1, xm1, rs1 = run_fm(layer_one, 1, o1, vec, m1, per)

    class Sum:
        def __init__(self, keep, send):
            self.keep, self.got, self.send = keep, [], send
            self.bits = [1, 2] + upper[::-1]

        def start(self):
            self.flight = swap(self.send, self.bits[len(self.got)])
            return self

        def done(self):
            self.got.append(self.flight)
            size = self.flight.shape[0]
            if len(self.got) < len(self.bits):
                self.send = self.total(size // 2, size).astype(BF)
            else:
                self.send = self.total(0, 1)[0].astype(BF)
            return self

        def total(self, lo, hi):
            t = self.keep[lo:hi]
            for g in self.got:
                t = t + g[lo:hi].astype(F32)
            return t

        def replicas(self):
            mine, b = self.send, 1
            while True:
                other = lax.ppermute(mine, "replica", xor_pairs(reps, b))
                b *= 2
                if b >= reps:
                    return (mine, other)
                mine = (mine.astype(F32) + other.astype(F32)).astype(BF)

    def meet(value, *sums):
        value, *got = group(value, *[s.flight for s in sums])
        for s, g in zip(sums, got):
            s.flight = g
            s.done()
        return value

    def sent(value, *sums):
        return tie(value, *[s.send for s in sums])

    dx1, do, kp, sn, v2, db1 = run_bm(cotangent, 1, act1, der1, xm1, rs1, o1, vec, m1, per)
    gm1 = Sum(kp, sn).start()
    dm = run_bs(seq, mix1, o1, do, aux1, per)
    dm = meet(dm, gm1)
    gm1.start()
    grad, kp, sn = run_bq(seq, 1, dx1, sent(dm, gm1), xa1, aux1, vec, v2, db1, a1, per)
    ga1 = Sum(kp, sn).start()
    grad = meet(grad, gm1)
    gm1.start()
    dx1, do, kp, sn, v2, db1 = run_bm(sent(grad, gm1), 0, act0, der0, xm0, rs0, o0, vec, m0, per)
    gm0 = Sum(kp, sn).start()
    do = meet(do, gm1, ga1)
    gm1.start()
    ga1.start()
    first = images // (2 * per) * per
    dm = run_bs(seq, mix0, o0, sent(do, gm1, ga1), aux0, per, 0, first)
    dm = meet(dm, gm1, ga1, gm0)
    ga1.start()
    gm0.start()
    fin_m1 = gm1.replicas()
    dm = run_bs(seq, mix0, o0, do, aux0, per, first, None, sent(dm, gm1, ga1, gm0))
    dm = meet(dm, ga1, gm0)
    ga1.start()
    gm0.start()
    tokens_grad, kp, sn = run_bq(seq, 0, dx1, sent(dm, ga1, gm0), xa0, aux0, vec, v2, db1, a0, per)
    ga0 = Sum(kp, sn).start()
    tokens_grad = meet(tokens_grad, ga1, gm0)
    fin_a1 = ga1.replicas()
    gm0.start()
    ga0.done().start()
    gm0.flight = tie(gm0.flight, ga0.send)
    gm0.done()
    fin_m0 = gm0.replicas()
    ga0.done().start().done().start().done()
    fin_a0 = ga0.replicas()

    g_qkv, g_proj, g_up, g_down, g_bup, *s = run_finish(fin_a0, fin_m0, fin_a1, fin_m1, ff)
    return (layer_one, layer_two, tokens_grad, s[0], s[1], g_qkv, s[2], s[3], g_proj, s[4], s[5], s[6],
            g_up, g_bup, g_down, s[7])
def solution(mesh):
    n = mesh.shape["shard"]
    reps = mesh.shape["replica"]
    batch = P(("replica", "shard"), None, None)
    row2 = P(None, "shard")
    row3 = P(None, "shard", None)
    in_specs = (batch, row2, row2, row3, row2, row2, row3, row2, row2, row2, row3, row2, row3, row2, batch)
    out_specs = (batch, batch, batch, row2, row2, row3, row2, row2, row3, row2, row2, row2, row3, row2, row3, row2)
    return jax.shard_map(
        functools.partial(body, n, reps), mesh=mesh, in_specs=in_specs, out_specs=out_specs, check_vma=False
    )
```

time: 377 us -> 297 us (0.79); the launches traced: 370 us -> 296 us
  waiting for transfers between devices: 91.6 us -> 44.9 us
  local copies, waits for them, and re-layouts: 24.8 us -> 6.35 us
  starting transfers between devices: 47.8 us -> 38.8 us
  other arithmetic: 12.4 us -> 20.7 us
  Pallas kernels: 192 us -> 184 us
    ppermute x54 -> x36, waiting for transfers between devices: 91.6 us -> 44.9 us  [the longest x32 43 us: swap(): return lax.ppermute(x, 'shard', xor_pairs(n, b))]
    convert_element_type x20 -> x16, other arithmetic: 1.69 us -> 19.3 us  [the longest x12 15.2 us: done(): self.send = self.total(size // 2, size).astype(BF)]
    another operation x32 -> x0, local copies, waits for them, and re-layouts: 10.7 us -> none  [the longest x8 5.3 us: body(): jnp.stack(smalls, 1)]
    ppermute x54 -> x36, starting transfers between devices: 47.8 us -> 38.8 us  [the longest x32 31.8 us: swap(): return lax.ppermute(x, 'shard', xor_pairs(n, b))]
    pallas_call x8 -> x13, Pallas kernels: 192 us -> 184 us  [the longest x8 141 us: call(): pl.pallas_call(kern, grid=(blocked_in[0].shape[0] // per,), in_specs=in_s...]
    another operation x57 -> x3, other arithmetic: 8.25 us -> 1.22 us  [the longest x1 0.97 us: body(): a0 = jnp.stack(direct(a0))]
    slice x19 -> x4, local copies, waits for them, and re-layouts: 5.96 us -> 0.18 us  [the longest x2 0.14 us: body(): m1 = jnp.concatenate([l1[:, 3:], l1x[:, 3:]])]
  transfers between devices with their start and end apart: 54 -> 36, of which waited for: 31 -> 20; matrix products, arithmetic and copies ran while one was open for 4% -> 4% of each run, Pallas kernels for 0% -> 41%
where the time goes in v2:
time: 297 us; the launch traced here: 296 us
  Pallas kernels  184 us (62%)
  waiting for transfers between devices  44.9 us (15%)
  starting transfers between devices  38.8 us (13%)
  other arithmetic  20.7 us (7%)
  local copies, waits for them, and re-layouts  6.35 us (2%)
    pallas_call x8, Pallas kernels, call(): pl.pallas_call(kern, grid=(blocked_in[0].shape[0] // per,), in_specs=in_s...  141 us
    ppermute x32, waiting for transfers between devices, swap(): return lax.ppermute(x, 'shard', xor_pairs(n, b))  43 us
    pallas_call x3, Pallas kernels, run_bs(): pl.pallas_call(functools.partial(bs_kernel, seq), grid=(count // per,), i...  38.6 us
    ppermute x32, starting transfers between devices, swap(): return lax.ppermute(x, 'shard', xor_pairs(n, b))  31.8 us
    convert_element_type x12, other arithmetic, done(): self.send = self.total(size // 2, size).astype(BF)  15.2 us
    ppermute x4, starting transfers between devices, replicas(): other = lax.ppermute(mine, 'replica', xor_pairs(reps, b))  7 us
    unnamed x50, local copies, waits for them, and re-layouts  6 us
  transfers between devices with their start and end apart: 36, of which 20 were waited for; matrix products, arithmetic and copies ran while one was open for 4% of the time, Pallas kernels for 41%

profile of v2, /device:TPU:0, one launch (start us, length us, event | category | flops | bytes accessed | tf_op | source)
XLA Modules:
  0.0 295.8 jit_solution(2174971848734001720)
XLA Ops:
  2.6 5.0 %collective-permute-start.2 = (bf16[4,24,384]{2,1,0:T(8,128)(2,1)}, bf16[4,24,384]{2,1,0:T(8,128)(2,1)S(1)}, u32[]{:S(2)}, u32[]{:S(2)}) collective-permute-start(bf16[4,24,384]{2,1,0:T(8,128)(2,1)} %get-tuple-element.111), channel_id=1, source_target_pairs={{0,12},{1,13},{2,14},{3,15},{4,8},{5,9},{6,10},{7,11},{8,4},{9,5},... | collective-permute-start | bytes 221192 | tf_op jit(solution)/shard_map/ppermute | solution.py:568
  14.6 3.3 %collective-permute-start.6 = (bf16[9,24,384]{2,1,0:T(8,128)(2,1)}, bf16[9,24,384]{2,1,0:T(8,128)(2,1)S(1)}, u32[]{:S(2)}, u32[]{:S(2)}) collective-permute-start(bf16[9,24,384]{2,1,0:T(8,128)(2,1)} %get-tuple-element.112), channel_id=1, source_target_pairs={{0,12},{1,13},{2,14},{3,15},{4,8},{5,9},{6,10},{7,11},{8,4},{9,5},... | collective-permute-start | bytes 497672 | tf_op jit(solution)/shard_map/ppermute | solution.py:568
  26.4 5.3 %collective-permute-done.3 = bf16[9,24,384]{2,1,0:T(8,128)(2,1)S(1)} collective-permute-done((bf16[9,24,384]{2,1,0:T(8,128)(2,1)}, bf16[9,24,384]{2,1,0:T(8,128)(2,1)S(1)}, u32[]{:S(2)}, u32[]{:S(2)}) %collective-permute-start.3) | collective-permute-done | bytes 165920 | tf_op jit(solution)/shard_map/ppermute | solution.py:568
  31.8 2.7 collective-permute-start.11
  40.4 13.4 %fa.2 = (bf16[10,208,1152]{2,1,0:T(8,128)(2,1)}, bf16[10,208,384]{2,1,0:T(8,128)(2,1)}, f32[10,8,208]{2,1,0:T(8,128)}, bf16[10,208,384]{2,1,0:T(8,128)(2,1)}, f32[2,16,384]{2,1,0:T(8,128)}) custom-call(bf16[10,197,384]{2,1,0:T(8,128)(2,1)} %x_ref.2, bf16[8,4,24,384]{3,2,1,0:T(8,128)(2,1)} %copy-done.18, ...), custom_call_target="tpu_custom_call" | custom-call | flops 16099999744 | tf_op jit(solution)/shard_map/fa/pallas_call | solution.py:435
  54.6 2.7 collective-permute-done.12.other
  58.3 17.6 %fm.2 = (f32[10,197,384]{2,1,0:T(8,128)}, bf16[10,208,1536]{2,1,0:T(8,128)(2,1)}, bf16[10,208,1536]{2,1,0:T(8,128)(2,1)}, bf16[10,208,384]{2,1,0:T(8,128)(2,1)}, f32[10,8,208]{2,1,0:T(8,128)}) custom-call(bf16[10,197,384]{2,1,0:T(8,128)(2,1)} %x_ref.2, bf16[10,208,384]{2,1,0:T(8,128)(2,1)} %get-tuple-element.120.o_ref, ...), custom_call_target="tpu_custom_call" | custom-call | flops 20700000256 | tf_op jit(solution)/shard_map/fm/pallas_call | solution.py:435
  78.4 13.3 %fa.3 = (bf16[10,208,1152]{2,1,0:T(8,128)(2,1)}, bf16[10,208,384]{2,1,0:T(8,128)(2,1)}, f32[10,8,208]{2,1,0:T(8,128)}, bf16[10,208,384]{2,1,0:T(8,128)(2,1)}) custom-call(f32[10,197,384]{2,1,0:T(8,128)} %get-tuple-element.131.x_ref, f32[2,16,384]{2,1,0:T(8,128)} %get-tuple-element.121.vec_ref.refs_0_, bf16[8,3,24,384]{3,2,1,0:T(8,128)(2,1)} %copy-done.7, ...), custom_call_target="tpu_custom_call" | custom-call | flops 16099999744 | tf_op jit(solution)/shard_map/fa/pallas_call | solution.py:435
  92.8 17.8 %fm.3 = (f32[10,197,384]{2,1,0:T(8,128)}, bf16[10,208,1536]{2,1,0:T(8,128)(2,1)}, bf16[10,208,1536]{2,1,0:T(8,128)(2,1)}, bf16[10,208,384]{2,1,0:T(8,128)(2,1)}, f32[10,8,208]{2,1,0:T(8,128)}) custom-call(f32[10,197,384]{2,1,0:T(8,128)} %get-tuple-element.131.x_ref, bf16[10,208,384]{2,1,0:T(8,128)(2,1)} %get-tuple-element.133.o_ref, ...), custom_call_target="tpu_custom_call" | custom-call | flops 20700000256 | tf_op jit(solution)/shard_map/fm/pallas_call | solution.py:435
  110.6 26.9 %bm.2 = (f32[10,208,384]{2,1,0:T(8,128)}, bf16[10,208,384]{2,1,0:T(8,128)(2,1)}, f32[8,9,24,384]{3,2,1,0:T(8,128)}, bf16[8,9,24,384]{3,2,1,0:T(8,128)(2,1)}, f32[8,384]{1,0:T(8,128)}, /*index=5*/f32[1,1536]{1,0:T(1,128)}) custom-call(bf16[10,197,384]{2,1,0:T(8,128)(2,1)} %gr_ref.1, bf16[10,208,1536]{2,1,0:T(8,128)(2,1)} %get-tuple-element.136.a_ref, ...), custom_call_target="tpu_custom_call" | custom-call | flops 31050000384 | tf_op jit(solution)/shard_map/bm/pallas_call | solution.py:435
  137.7 18.2 %bs.3.dm_ref = bf16[10,208,1152]{2,1,0:T(8,128)(2,1)} custom-call(bf16[10,208,1152]{2,1,0:T(8,128)(2,1)} %get-tuple-element.141.m_ref, bf16[10,208,384]{2,1,0:T(8,128)(2,1)} %get-tuple-element.133.o_ref, bf16[10,208,384]{2,1,0:T(8,128)(2,1)} %get-tuple-element.142.do_ref, f32[10,8,208]{2,1,0:T(8,128)} %get-tuple-element.143.aux_ref), custom_call_target="tpu_custom_call" | custom-call | flops 20700000256 | tf_op jit(solution)/shard_map/bs/pallas_call | solution.py:511
  157.4 12.4 %bq.2 = (f32[10,197,384]{2,1,0:T(8,128)}, f32[8,4,24,384]{3,2,1,0:T(8,128)}, bf16[8,4,24,384]{3,2,1,0:T(8,128)(2,1)}) custom-call(f32[10,208,384]{2,1,0:T(8,128)} %get-tuple-element.140.dx1_ref, bf16[10,208,1152]{2,1,0:T(8,128)(2,1)} %bs.3.dm_ref, bf16[10,208,384]{2,1,0:T(8,128)(2,1)} %get-tuple-element.149.xh_ref, ...), custom_call_target="tpu_custom_call" | custom-call | flops 14949999616 | tf_op jit(solution)/shard_map/bq/pallas_call | solution.py:435
  169.9 4.6 %collective-permute-done.17 = bf16[4,9,24,384]{3,2,1,0:T(8,128)(2,1)} collective-permute-done((bf16[4,9,24,384]{3,2,1,0:T(8,128)(2,1)}, bf16[4,9,24,384]{3,2,1,0:T(8,128)(2,1)}, u32[]{:S(2)}, u32[]{:S(2)}) %collective-permute-start.17) | collective-permute-done | bytes 663584 | tf_op jit(solution)/shard_map/ppermute | solution.py:568
  177.2 27.0 %bm.3 = (f32[10,208,384]{2,1,0:T(8,128)}, bf16[10,208,384]{2,1,0:T(8,128)(2,1)}, f32[8,9,24,384]{3,2,1,0:T(8,128)}, bf16[8,9,24,384]{3,2,1,0:T(8,128)(2,1)}, f32[8,384]{1,0:T(8,128)}, /*index=5*/f32[1,1536]{1,0:T(1,128)}) custom-call(f32[10,197,384]{2,1,0:T(8,128)} %get-tuple-element.155.gr_ref, bf16[10,208,1536]{2,1,0:T(8,128)(2,1)} %get-tuple-element.156.a_ref, ...), custom_call_target="tpu_custom_call" | custom-call | flops 31050000384 | tf_op jit(solution)/shard_map/bm/pallas_call | solution.py:435
  206.2 2.9 collective-permute-start.20
  211.3 8.7 %bs.4.rest_0_ = bf16[10,208,1152]{2,1,0:T(8,128)(2,1)} custom-call(bf16[10,208,1152]{2,1,0:T(8,128)(2,1)} %get-tuple-element.161.m_ref, bf16[10,208,384]{2,1,0:T(8,128)(2,1)} %get-tuple-element.120.o_ref, bf16[10,208,384]{2,1,0:T(8,128)(2,1)} %get-tuple-element.169.do_ref, f32[10,8,208]{2,1,0:T(8,128)} %get-tuple-element.165.aux_ref), custom_call_target="tpu_custom_call" | custom-call | flops 8049999872 | tf_op jit(solution)/shard_map/bs/pallas_call | solution.py:511
  226.5 11.7 %bs.5.dm_ref = bf16[10,208,1152]{2,1,0:T(8,128)(2,1)} custom-call(bf16[10,208,1152]{2,1,0:T(8,128)(2,1)} %get-tuple-element.161.m_ref, bf16[10,208,384]{2,1,0:T(8,128)(2,1)} %get-tuple-element.120.o_ref, bf16[10,208,384]{2,1,0:T(8,128)(2,1)} %get-tuple-element.169.do_ref, f32[10,8,208]{2,1,0:T(8,128)} %get-tuple-element.165.aux_ref, ...), custom_call_target="tpu_custom_call", output_to_operand_aliasing={{}: (4, {})} | custom-call | flops 11500000256 | tf_op jit(solution)/shard_map/bs/pallas_call | solution.py:511
  238.2 3.6 %collective-permute-done.24 = bf16[4,9,24,384]{3,2,1,0:T(8,128)(2,1)} collective-permute-done((bf16[4,9,24,384]{3,2,1,0:T(8,128)(2,1)}, bf16[4,9,24,384]{3,2,1,0:T(8,128)(2,1)}, u32[]{:S(2)}, u32[]{:S(2)}) %collective-permute-start.24) | collective-permute-done | bytes 663584 | tf_op jit(solution)/shard_map/ppermute | solution.py:568
  245.3 12.6 %bq.3 = (f32[10,197,384]{2,1,0:T(8,128)}, f32[8,4,24,384]{3,2,1,0:T(8,128)}, bf16[8,4,24,384]{3,2,1,0:T(8,128)(2,1)}) custom-call(f32[10,208,384]{2,1,0:T(8,128)} %get-tuple-element.160.dx1_ref, bf16[10,208,1152]{2,1,0:T(8,128)(2,1)} %bs.5.dm_ref, bf16[10,208,384]{2,1,0:T(8,128)(2,1)} %get-tuple-element.181.xh_ref, ...), custom_call_target="tpu_custom_call" | custom-call | flops 14949999616 | tf_op jit(solution)/shard_map/bq/pallas_call | solution.py:435
  264.7 4.7 %collective-permute-done.25 = bf16[1,4,24,384]{3,2,1,0:T(8,128)(2,1)S(1)} collective-permute-done((bf16[1,4,24,384]{3,2,1,0:T(8,128)(2,1)}, bf16[1,4,24,384]{3,2,1,0:T(8,128)(2,1)S(1)}, u32[]{:S(2)}, u32[]{:S(2)}) %collective-permute-start.25) | collective-permute-done | bytes 73760 | tf_op jit(solution)/shard_map/ppermute | solution.py:568
  271.0 2.7 collective-permute-start.32
  276.7 4.7 %collective-permute-done.32 = bf16[1,9,24,384]{3,2,1,0:T(8,128)(2,1)S(1)} collective-permute-done((bf16[1,9,24,384]{3,2,1,0:T(8,128)(2,1)S(1)}, bf16[1,9,24,384]{3,2,1,0:T(8,128)(2,1)S(1)}, u32[]{:S(2)}, u32[]{:S(2)}) %collective-permute-start.32) | collective-permute-done | bytes 165920 | tf_op jit(solution)/shard_map/ppermute | solution.py:568
  285.1 3.2 %collective-permute-done.30 = bf16[1,4,24,384]{3,2,1,0:T(8,128)(2,1)S(1)} collective-permute-done((bf16[1,4,24,384]{3,2,1,0:T(8,128)(2,1)S(1)}, bf16[1,4,24,384]{3,2,1,0:T(8,128)(2,1)S(1)}, u32[]{:S(2)}, u32[]{:S(2)}) %collective-permute-start.30) | collective-permute-done | bytes 73760 | tf_op jit(solution)/shard_map/ppermute | solution.py:568
  293.4 2.2 finish.1
  (138 shorter events, 67.4 us)
Async XLA Ops:
  14.6 9.3 %collective-permute-start.6 = (bf16[9,24,384]{2,1,0:T(8,128)(2,1)}, bf16[9,24,384]{2,1,0:T(8,128)(2,1)S(1)}, u32[]{:S(2)}, u32[]{:S(2)}) collective-permute-start(bf16[9,24,384]{2,1,0:T(8,128)(2,1)} %get-tuple-element.112), channel_id=1, source_target_pairs={{0,12},{1,13},{2,14},{3,15},{4,8},{5,9},{6,10},{7,11},{8,4},{9,5},... | collective-permute-start | bytes 497672 | tf_op jit(solution)/shard_map/ppermute | solution.py:568
  17.9 8.5 %collective-permute-start.5 = (bf16[9,24,384]{2,1,0:T(8,128)(2,1)}, bf16[9,24,384]{2,1,0:T(8,128)(2,1)S(1)}, u32[]{:S(2)}, u32[]{:S(2)}) collective-permute-start(bf16[9,24,384]{2,1,0:T(8,128)(2,1)} %get-tuple-element.112), channel_id=1, source_target_pairs={{0,4},{1,5},{2,6},{3,7},{4,0},{5,1},{6,2},{7,3},{8,12},{9,13},{10,... | collective-permute-start | bytes 497672 | tf_op jit(solution)/shard_map/ppermute | solution.py:568
  17.9 13.8 %collective-permute-start.3 = (bf16[9,24,384]{2,1,0:T(8,128)(2,1)}, bf16[9,24,384]{2,1,0:T(8,128)(2,1)S(1)}, u32[]{:S(2)}, u32[]{:S(2)}) collective-permute-start(bf16[9,24,384]{2,1,0:T(8,128)(2,1)} %get-tuple-element.112), channel_id=1, source_target_pairs={{0,8},{1,9},{2,10},{3,11},{4,12},{5,13},{6,14},{7,15},{8,0},{9,1},... | collective-permute-start | bytes 497672 | tf_op jit(solution)/shard_map/ppermute | solution.py:568
  31.8 22.0 %collective-permute-start.11 = (bf16[12,24,384]{2,1,0:T(8,128)(2,1)S(1)}, bf16[12,24,384]{2,1,0:T(8,128)(2,1)S(1)}, u32[]{:S(2)}, u32[]{:S(2)}) collective-permute-start(bf16[12,24,384]{2,1,0:T(8,128)(2,1)S(1)} %copy-done.10), channel_id=1, source_target_pairs={{0,12},{1,13},{2,14},{3,15},{4,8},{5,9},{6,10},{7,11},{8,4},{9,5},... | collective-permute-start | bytes 663560 | tf_op jit(solution)/shard_map/ppermute | solution.py:568
  34.5 19.3 %collective-permute-start.10 = (bf16[12,24,384]{2,1,0:T(8,128)(2,1)S(1)}, bf16[12,24,384]{2,1,0:T(8,128)(2,1)S(1)}, u32[]{:S(2)}, u32[]{:S(2)}) collective-permute-start(bf16[12,24,384]{2,1,0:T(8,128)(2,1)S(1)} %copy-done.10), channel_id=1, source_target_pairs={{0,4},{1,5},{2,6},{3,7},{4,0},{5,1},{6,2},{7,3},{8,12},{9,13},{10,... | collective-permute-start | bytes 663560 | tf_op jit(solution)/shard_map/ppermute | solution.py:568
  34.5 19.3 %collective-permute-start.9 = (bf16[12,24,384]{2,1,0:T(8,128)(2,1)S(1)}, bf16[12,24,384]{2,1,0:T(8,128)(2,1)S(1)}, u32[]{:S(2)}, u32[]{:S(2)}) collective-permute-start(bf16[12,24,384]{2,1,0:T(8,128)(2,1)S(1)} %copy-done.10), channel_id=1, source_target_pairs={{0,8},{1,9},{2,10},{3,11},{4,12},{5,13},{6,14},{7,15},{8,0},{9,1},... | collective-permute-start | bytes 663560 | tf_op jit(solution)/shard_map/ppermute | solution.py:568
  36.3 17.6 %collective-permute-start.8 = (bf16[4,9,24,384]{3,2,1,0:T(8,128)(2,1)S(1)}, bf16[4,9,24,384]{3,2,1,0:T(8,128)(2,1)S(1)}, u32[]{:S(2)}, u32[]{:S(2)}) collective-permute-start(bf16[4,9,24,384]{3,2,1,0:T(8,128)(2,1)S(1)} %pad_maximum_fusion.2), channel_id=1, source_target_pairs={{0,2},{1,3},{2,0},{3,1},{4,6},{5,7},{6,4},{7,5},{8,10},{9,11},{10,... | collective-permute-start | bytes 1990664 | tf_op jit(solution)/shard_map/ppermute | solution.py:568
  54.3 22.0 %collective-permute-start.13 = (bf16[4,12,24,384]{3,2,1,0:T(8,128)(2,1)S(1)}, bf16[4,12,24,384]{3,2,1,0:T(8,128)(2,1)S(1)}, u32[]{:S(2)}, u32[]{:S(2)}) collective-permute-start(bf16[4,12,24,384]{3,2,1,0:T(8,128)(2,1)S(1)} %pad_maximum_fusion.1), channel_id=1, source_target_pairs={{0,2},{1,3},{2,0},{3,1},{4,6},{5,7},{6,4},{7,5},{8,10},{9,11},{10,... | collective-permute-start | bytes 2654216 | tf_op jit(solution)/shard_map/ppermute | solution.py:568
  77.4 14.3 %collective-permute-start.15 = (bf16[8,9,24,384]{3,2,1,0:T(8,128)(2,1)S(1)}, bf16[8,9,24,384]{3,2,1,0:T(8,128)(2,1)S(1)}, u32[]{:S(2)}, u32[]{:S(2)}) collective-permute-start(bf16[8,9,24,384]{3,2,1,0:T(8,128)(2,1)S(1)} %pad_maximum_fusion.own), channel_id=1, source_target_pairs={{0,1},{1,0},{2,3},{3,2},{4,5},{5,4},{6,7},{7,6},{8,9},{9,8},{10,11... | collective-permute-start | bytes 3981320 | tf_op jit(solution)/shard_map/ppermute | solution.py:568
  137.5 18.4 %collective-permute-start.16 = (bf16[8,9,24,384]{3,2,1,0:T(8,128)(2,1)}, bf16[8,9,24,384]{3,2,1,0:T(8,128)(2,1)S(1)}, u32[]{:S(2)}, u32[]{:S(2)}) collective-permute-start(bf16[8,9,24,384]{3,2,1,0:T(8,128)(2,1)} %get-tuple-element.144), channel_id=1, source_target_pairs={{0,1},{1,0},{2,3},{3,2},{4,5},{5,4},{6,7},{7,6},{8,9},{9,8},{10,11... | collective-permute-start | bytes 3981320 | tf_op jit(solution)/shard_map/ppermute | solution.py:568
  157.0 17.5 %collective-permute-start.17 = (bf16[4,9,24,384]{3,2,1,0:T(8,128)(2,1)}, bf16[4,9,24,384]{3,2,1,0:T(8,128)(2,1)}, u32[]{:S(2)}, u32[]{:S(2)}) collective-permute-start(bf16[4,9,24,384]{3,2,1,0:T(8,128)(2,1)} %add_convert_fusion.1), channel_id=1, source_target_pairs={{0,2},{1,3},{2,0},{3,1},{4,6},{5,7},{6,4},{7,5},{8,10},{9,11},{10,... | collective-permute-start | bytes 1990664 | tf_op jit(solution)/shard_map/ppermute | solution.py:568
  169.8 34.6 %collective-permute-start.19 = (bf16[8,4,24,384]{3,2,1,0:T(8,128)(2,1)}, bf16[8,4,24,384]{3,2,1,0:T(8,128)(2,1)}, u32[]{:S(2)}, u32[]{:S(2)}) collective-permute-start(bf16[8,4,24,384]{3,2,1,0:T(8,128)(2,1)} %get-tuple-element.163), channel_id=1, source_target_pairs={{0,1},{1,0},{2,3},{3,2},{4,5},{5,4},{6,7},{7,6},{8,9},{9,8},{10,11... | collective-permute-start | bytes 1769480 | tf_op jit(solution)/shard_map/ppermute | solution.py:568
  176.3 28.0 %collective-permute-start.18 = (bf16[2,9,24,384]{3,2,1,0:T(8,128)(2,1)}, bf16[2,9,24,384]{3,2,1,0:T(8,128)(2,1)}, u32[]{:S(2)}, u32[]{:S(2)}) collective-permute-start(bf16[2,9,24,384]{3,2,1,0:T(8,128)(2,1)} %add_convert_fusion.3), channel_id=1, source_target_pairs={{0,4},{1,5},{2,6},{3,7},{4,0},{5,1},{6,2},{7,3},{8,12},{9,13},{10,... | collective-permute-start | bytes 995336 | tf_op jit(solution)/shard_map/ppermute | solution.py:568
  204.2 16.2 %collective-permute-start.22 = (bf16[8,9,24,384]{3,2,1,0:T(8,128)(2,1)}, bf16[8,9,24,384]{3,2,1,0:T(8,128)(2,1)S(1)}, u32[]{:S(2)}, u32[]{:S(2)}) collective-permute-start(bf16[8,9,24,384]{3,2,1,0:T(8,128)(2,1)} %get-tuple-element.170), channel_id=1, source_target_pairs={{0,1},{1,0},{2,3},{3,2},{4,5},{5,4},{6,7},{7,6},{8,9},{9,8},{10,11... | collective-permute-start | bytes 3981320 | tf_op jit(solution)/shard_map/ppermute | solution.py:568
  206.2 13.8 %collective-permute-start.20 = (bf16[1,9,24,384]{3,2,1,0:T(8,128)(2,1)}, bf16[1,9,24,384]{3,2,1,0:T(8,128)(2,1)}, u32[]{:S(2)}, u32[]{:S(2)}) collective-permute-start(bf16[1,9,24,384]{3,2,1,0:T(8,128)(2,1)} %add_convert_fusion.9), channel_id=1, source_target_pairs={{0,8},{1,9},{2,10},{3,11},{4,12},{5,13},{6,14},{7,15},{8,0},{9,1},... | collective-permute-start | bytes 497672 | tf_op jit(solution)/shard_map/ppermute | solution.py:568
  211.0 9.4 %collective-permute-start.21 = (bf16[4,4,24,384]{3,2,1,0:T(8,128)(2,1)}, bf16[4,4,24,384]{3,2,1,0:T(8,128)(2,1)}, u32[]{:S(2)}, u32[]{:S(2)}) collective-permute-start(bf16[4,4,24,384]{3,2,1,0:T(8,128)(2,1)} %add_convert_fusion.5), channel_id=1, source_target_pairs={{0,2},{1,3},{2,0},{3,1},{4,6},{5,7},{6,4},{7,5},{8,10},{9,11},{10,... | collective-permute-start | bytes 884744 | tf_op jit(solution)/shard_map/ppermute | solution.py:568
  224.2 14.0 %collective-permute-start.23 = (bf16[2,4,24,384]{3,2,1,0:T(8,128)(2,1)}, bf16[2,4,24,384]{3,2,1,0:T(8,128)(2,1)S(1)}, u32[]{:S(2)}, u32[]{:S(2)}) collective-permute-start(bf16[2,4,24,384]{3,2,1,0:T(8,128)(2,1)} %add_convert_fusion.11), channel_id=1, source_target_pairs={{0,4},{1,5},{2,6},{3,7},{4,0},{5,1},{6,2},{7,3},{8,12},{9,13},{10,... | collective-permute-start | bytes 442376 | tf_op jit(solution)/shard_map/ppermute | solution.py:568
  225.2 16.6 %collective-permute-start.24 = (bf16[4,9,24,384]{3,2,1,0:T(8,128)(2,1)}, bf16[4,9,24,384]{3,2,1,0:T(8,128)(2,1)}, u32[]{:S(2)}, u32[]{:S(2)}) collective-permute-start(bf16[4,9,24,384]{3,2,1,0:T(8,128)(2,1)} %add_convert_fusion), channel_id=1, source_target_pairs={{0,2},{1,3},{2,0},{3,1},{4,6},{5,7},{6,4},{7,5},{8,10},{9,11},{10,... | collective-permute-start | bytes 1990664 | tf_op jit(solution)/shard_map/ppermute | solution.py:568
  258.0 12.0 %collective-permute-start.26 = (bf16[2,9,24,384]{3,2,1,0:T(8,128)(2,1)}, bf16[2,9,24,384]{3,2,1,0:T(8,128)(2,1)S(1)}, u32[]{:S(2)}, u32[]{:S(2)}) collective-permute-start(bf16[2,9,24,384]{3,2,1,0:T(8,128)(2,1)} %add_convert_fusion.2), channel_id=1, source_target_pairs={{0,4},{1,5},{2,6},{3,7},{4,0},{5,1},{6,2},{7,3},{8,12},{9,13},{10,... | collective-permute-start | bytes 995336 | tf_op jit(solution)/shard_map/ppermute | solution.py:568
  259.8 9.6 %collective-permute-start.25 = (bf16[1,4,24,384]{3,2,1,0:T(8,128)(2,1)}, bf16[1,4,24,384]{3,2,1,0:T(8,128)(2,1)S(1)}, u32[]{:S(2)}, u32[]{:S(2)}) collective-permute-start(bf16[1,4,24,384]{3,2,1,0:T(8,128)(2,1)} %add_convert_fusion.15), channel_id=1, source_target_pairs={{0,8},{1,9},{2,10},{3,11},{4,12},{5,13},{6,14},{7,15},{8,0},{9,1},... | collective-permute-start | bytes 221192 | tf_op jit(solution)/shard_map/ppermute | solution.py:568
  261.4 12.3 %collective-permute-start.28 = (bf16[4,4,24,384]{3,2,1,0:T(8,128)(2,1)S(1)}, bf16[4,4,24,384]{3,2,1,0:T(8,128)(2,1)S(1)}, u32[]{:S(2)}, u32[]{:S(2)}) collective-permute-start(bf16[4,4,24,384]{3,2,1,0:T(8,128)(2,1)S(1)} %add_convert_fusion.4), channel_id=1, source_target_pairs={{0,2},{1,3},{2,0},{3,1},{4,6},{5,7},{6,4},{7,5},{8,10},{9,11},{10,... | collective-permute-start | bytes 884744 | tf_op jit(solution)/shard_map/ppermute | solution.py:568
  263.1 27.0 %collective-permute-start.35 = (bf16[9,24,384]{2,1,0:T(8,128)(2,1)}, bf16[9,24,384]{2,1,0:T(8,128)(2,1)S(1)}, u32[]{:S(2)}, u32[]{:S(2)}) collective-permute-start(bf16[9,24,384]{2,1,0:T(8,128)(2,1)} %fusion.refs_6_), channel_id=1, source_target_pairs={{0,16},{16,0},{1,17},{17,1},{2,18},{18,2},{3,19},{19,3},{4,20},{20... | collective-permute-start | bytes 497672 | tf_op jit(solution)/shard_map/ppermute | solution.py:634
  271.0 10.4 %collective-permute-start.32 = (bf16[1,9,24,384]{3,2,1,0:T(8,128)(2,1)S(1)}, bf16[1,9,24,384]{3,2,1,0:T(8,128)(2,1)S(1)}, u32[]{:S(2)}, u32[]{:S(2)}) collective-permute-start(bf16[1,9,24,384]{3,2,1,0:T(8,128)(2,1)S(1)} %add_convert_fusion.7), channel_id=1, source_target_pairs={{0,8},{1,9},{2,10},{3,11},{4,12},{5,13},{6,14},{7,15},{8,0},{9,1},... | collective-permute-start | bytes 497672 | tf_op jit(solution)/shard_map/ppermute | solution.py:568
  274.9 15.3 %collective-permute-start.34 = (bf16[4,24,384]{2,1,0:T(8,128)(2,1)S(1)}, bf16[4,24,384]{2,1,0:T(8,128)(2,1)S(1)}, u32[]{:S(2)}, u32[]{:S(2)}) collective-permute-start(bf16[4,24,384]{2,1,0:T(8,128)(2,1)S(1)} %fusion.3.refs_4_), channel_id=1, source_target_pairs={{0,16},{16,0},{1,17},{17,1},{2,18},{18,2},{3,19},{19,3},{4,20},{20... | collective-permute-start | bytes 221192 | tf_op jit(solution)/shard_map/ppermute | solution.py:634
  (33 other events, 265.0 us)

commit v3 on v2

--- a/solution.py
+++ b/solution.py
@@ -168,22 +168,10 @@
         vec[layer, 8 + quart :] = jnp.zeros((8 - quart, width), F32)
 
 
-def fa_kernel(seq, layer, x_ref, *refs):
-    if layer == 0:
-        own, other, m_ref, o_ref, aux_ref, xh_ref, vec_ref, xs, w, sems, tmp = refs
-    else:
-        vec_ref, own, other, m_ref, o_ref, aux_ref, xh_ref, xs, w, sems = refs
-    vec = vec_ref.at[layer]
-    first_step(lambda: start_weights(own, other, w, sems))
-    images = x_ref.shape[0]
-    rows = pad_rows(seq)
-    width = x_ref.shape[2]
-    load_padded(xs, x_ref, seq, rows, images)
+def attn_forward(seq, xs, vec, w, m_ref, o_ref, aux_ref, xh_ref):
+    images, rows, width = o_ref.shape
     xhat, rstd = normalise(xs[...])
     xh_ref[...] = xhat.astype(BF).reshape(images, rows, width)
-    first_step(lambda: wait_weights(own, other, w, sems))
-    if layer == 0:
-        first_step(lambda: unpack_small(w, vec_ref, tmp))
     n1 = (xhat * vec[0:1, :] + vec[1:2, :]).astype(BF)
     for c in range(3):
         cs = slice(c * width, (c + 1) * width)
@@ -223,26 +211,21 @@
         aux_ref[g] = to_rows(aux)
 
 
-def fm_kernel(seq, layer, x_ref, o_ref, vec_ref, own, other, out_ref, a_ref, d_ref, xh_ref, rs_ref, xs, w, sems):
-    vec = vec_ref.at[layer]
-    first_step(lambda: start_weights(own, other, w, sems))
+def mlp_forward(seq, xs, o_ref, vec, w, base, out_ref, a_ref, d_ref, xh_ref, rs_ref):
     images, rows, width = o_ref.shape
-    n = images * rows
-    load_padded(xs, x_ref, seq, rows, images)
-    first_step(lambda: wait_weights(own, other, w, sems))
-    x1 = xs[...] + dot(flat(o_ref[...]), slabs(w, 0, 1)) + vec[4:5, :]
+    x1 = xs[...] + dot(flat(o_ref[...]), slabs(w, base, 1)) + vec[4:5, :]
     xhat, rstd = normalise(x1)
     xh_ref[...] = xhat.astype(BF).reshape(images, rows, width)
     for g in range(images):
         rs_ref[g] = to_rows(jnp.broadcast_to(rstd[g * rows : (g + 1) * rows], (rows, 128)))
     n2 = (xhat * vec[5:6, :] + vec[6:7, :]).astype(BF)
     acc = x1 + vec[7:8, :]
-    quart = (w.shape[1] - 1) // 2
-    w2 = tall(w, 1 + quart, quart)
+    quart = a_ref.shape[2] // width
+    w2 = tall(w, base + 1 + quart, quart)
     for c in range(quart // 2):
         cs = slice(2 * c * width, 2 * (c + 1) * width)
         bias = jnp.concatenate([vec[8 + 2 * c : 9 + 2 * c, :], vec[9 + 2 * c : 10 + 2 * c, :]], 1)
-        h = dot(n2, slabs(w, 1 + 2 * c, 2)) + bias
+        h = dot(n2, slabs(w, base + 1 + 2 * c, 2)) + bias
         a, d = gelu_both(h)
         a = a.astype(BF)
         a_ref[:, :, cs] = a.reshape(images, rows, 2 * width)
@@ -253,31 +236,20 @@
         out_ref[g] = acc[g, :seq]
 
 
-def bm_kernel(seq, layer, gr_ref, a_ref, d_ref, xh_ref, rs_ref, o_ref, vec_ref, own, other,
-              dx1_ref, do_ref, keep, send, vec_o, db1_o, gs, dwp, dw1, dw2, w, sems):
-    vec = vec_ref.at[layer]
+def zero(*refs):
+    for r in refs:
+        r[...] = jnp.zeros_like(r)
+
+
+def mlp_backward(gs, a_ref, d_ref, xh_ref, rs_ref, o_ref, vec, w, base, dx1_ref, do_ref, dwp, dw1, dw2, vec_o, db1_o):
     images, rows, width = xh_ref.shape
     n = images * rows
-    shards, _, part, _ = w.shape
-    step = pl.program_id(0)
-    first_step(lambda: start_weights(own, other, w, sems))
-
-    @pl.when(step == 0)
-    def _():
-        dwp[...] = jnp.zeros_like(dwp)
-        dw1[...] = jnp.zeros_like(dw1)
-        dw2[...] = jnp.zeros_like(dw2)
-        vec_o[...] = jnp.zeros_like(vec_o)
-        db1_o[...] = jnp.zeros_like(db1_o)
-
-    load_padded(gs, gr_ref, seq, rows, images)
     dz = gs[...].astype(BF)
     xhat = flat(xh_ref[...]).astype(F32)
     n2 = (xhat * vec[5:6, :] + vec[6:7, :]).astype(BF)
     dn2 = jnp.zeros((n, width), F32)
-    first_step(lambda: wait_weights(own, other, w, sems))
-    quart = (w.shape[1] - 1) // 2
-    w2 = tall(w, 1 + quart, quart)
+    quart = a_ref.shape[2] // width
+    w2 = tall(w, base + 1 + quart, quart)
     for c in range(quart // 2):
         cs = slice(2 * c * width, 2 * (c + 1) * width)
         a = flat(a_ref[:, :, cs])
@@ -287,39 +259,28 @@
         db1_o[:, cs] += colsum(dh.astype(F32))
         dw2[cs, :] += dot_tn(a, dz)
         dw1[:, cs] += dot_tn(n2, dh)
-        dn2 = dn2 + dot_nt(dh, slabs(w, 1 + 2 * c, 2))
+        dn2 = dn2 + dot_nt(dh, slabs(w, base + 1 + 2 * c, 2))
     rstd = jnp.concatenate([to_column(rs_ref[g], 0) for g in range(images)], 0)
     dx1 = gs[...] + norm_back(dn2 * vec[5:6, :], xhat, rstd)
     dx1_ref[...] = dx1.reshape(images, rows, width)
     dy = dx1.astype(BF)
     dwp[...] += dot_tn(flat(o_ref[...]), dy)
-    do_ref[...] = dot_nt(dy, slabs(w, 0, 1)).astype(BF).reshape(images, rows, width)
+    do_ref[...] = dot_nt(dy, slabs(w, base, 1)).astype(BF).reshape(images, rows, width)
     vec_o[0:1, :] += colsum(dz.astype(F32))
     vec_o[1:2, :] += colsum(dn2 * xhat)
     vec_o[2:3, :] += colsum(dn2)
     vec_o[3:4, :] += colsum(dy.astype(F32))
 
-    @pl.when(step == pl.num_programs(0) - 1)
-    def _():
-        store_slots(keep, send,
-                    [rows_of(dwp, part, 0, width)]
-                    + [rows_of(dw1, part, q, width) for q in range(quart)]
-                    + [tall_rows_of(dw2, part, q, quart) for q in range(quart)])
-
-
-def bs_kernel(seq, m_ref, o_ref, do_ref, aux_ref, *rest):
-    dm_ref = rest[-1]
-    images, rows, width = o_ref.shape
+
+def attn_backward(seq, m_ref, do_ref, aux_ref, dm_ref):
+    images, rows, width = do_ref.shape
     lane = lax.broadcasted_iota(jnp.int32, (rows, 128), 1)
     low = lane < 64
     last = rows - 16
     valid = lax.broadcasted_iota(jnp.int32, (16, rows), 0) < seq - last
-    head = lax.broadcasted_iota(jnp.int32, (8, width), 0)
-    pick = jnp.where(lax.broadcasted_iota(jnp.int32, (8, width), 1) // 64 == head, 1.0, 0.0).astype(BF)
-    zero = jnp.zeros((rows, 128), BF)
+    none = jnp.zeros((rows, 128), BF)
     for g in range(images):
         lse = aux_ref[g]
-        inner = dot_nt(pick, (o_ref[g].astype(F32) * do_ref[g].astype(F32)).astype(BF))
         for p in range(width // 128):
             q2 = m_ref[g, :, p * 128 : (p + 1) * 128] * jnp.asarray(0.125, BF)
             k2 = m_ref[g, :, width + p * 128 : width + (p + 1) * 128]
@@ -329,11 +290,12 @@
             dks, dvs, dqs = [], [], []
             for half in range(2):
                 h = 2 * p + half
-                kh = jnp.where(low, k2, zero) if half == 0 else jnp.where(low, zero, k2)
-                vh = jnp.where(low, v2, zero) if half == 0 else jnp.where(low, zero, v2)
+                kh = jnp.where(low, k2, none) if half == 0 else jnp.where(low, none, k2)
+                vh = jnp.where(low, v2, none) if half == 0 else jnp.where(low, none, v2)
                 st = dot_nt(kh, q2) - lse[h : h + 1, :]
                 pt = jnp.exp(jnp.concatenate([st[:last], jnp.where(valid, st[last:], NEG)], 0))
-                dst = (pt * (dot_nt(vh, do2) - inner[h : h + 1, :])).astype(BF)
+                pd = pt * dot_nt(vh, do2)
+                dst = (pd - pt * colsum(pd)).astype(BF)
                 dvs.append(dot(pt.astype(BF), do2))
                 dks.append(dot(dst, q2))
                 dqs.append(dot(kt[half * 64 : half * 64 + 64], dst))
@@ -343,27 +305,13 @@
             dm_ref[g, :, 2 * width + p * 128 : 2 * width + (p + 1) * 128] = jnp.where(low, dvs[0], dvs[1]).astype(BF)
 
 
-def bq_kernel(seq, layer, dx1_ref, dm_ref, xh_ref, aux_ref, vec_ref, vec2, db1, own, other,
-              dx_ref, keep, send, dwqkv, vec_s, dbm_s, w, sems, sm):
-    vec = vec_ref.at[layer]
+def qkv_backward(seq, dx1_ref, dm_ref, xh_ref, aux_ref, vec, w, dx_ref, dwqkv, vec_s, dbm_s):
     images, rows, width = xh_ref.shape
-    n = images * rows
-    shards, _, part, _ = w.shape
-    step = pl.program_id(0)
-    first_step(lambda: start_weights(own, other, w, sems))
-
-    @pl.when(step == 0)
-    def _():
-        dwqkv[...] = jnp.zeros_like(dwqkv)
-        vec_s[...] = jnp.zeros_like(vec_s)
-        dbm_s[...] = jnp.zeros_like(dbm_s)
-
     dm = flat(dm_ref[...])
     dbm_s[...] += colsum(dm.astype(F32))
     xhat = flat(xh_ref[...]).astype(F32)
     n1 = (xhat * vec[0:1, :] + vec[1:2, :]).astype(BF)
     dwqkv[...] += dot_tn(n1, dm)
-    first_step(lambda: wait_weights(own, other, w, sems))
     dn1 = dot_nt(dm, slabs(w, 0, 3))
     vec_s[0:1, :] += colsum(dn1 * xhat)
     vec_s[1:2, :] += colsum(dn1)
@@ -373,28 +321,112 @@
     for g in range(images):
         dx_ref[g] = dx[g, :seq]
 
-    @pl.when(step == pl.num_programs(0) - 1)
+
+def small_slab(sm, vec_s, dbm_s, vec2, db1, part):
+    width = sm.shape[0]
+    small = jnp.concatenate(
+        [vec_s[0:2, :], dbm_s[:, :width], dbm_s[:, 2 * width :], vec2[3:4, :], vec2[1:3, :], vec2[0:1, :],
+         jnp.zeros((120, width), F32)], 0)
+    sm[...] = jnp.zeros_like(sm)
+    sm[:, 0:128] = small.T
+    shards = width // part
+    hid = db1.shape[1] // shards
+    for j in range(shards):
+        sm[j * part : j * part + 1, width - hid :] = db1[:, j * hid : (j + 1) * hid]
+
+
+def attn_pieces(dwqkv, sm, part):
+    width = sm.shape[0]
+    return [rows_of(dwqkv, part, c, width) for c in range(3)] + [rows_of(sm, part, 0, width)]
+
+
+def mlp_pieces(dwp, dw1, dw2, part):
+    width = dwp.shape[0]
+    quart = dw1.shape[1] // width
+    return ([rows_of(dwp, part, 0, width)] + [rows_of(dw1, part, q, width) for q in range(quart)]
+            + [tall_rows_of(dw2, part, q, quart) for q in range(quart)])
+
+
+def last_step(f):
+    pl.when(pl.program_id(0) == pl.num_programs(0) - 1)(f)
+
+
+def fa_kernel(seq, x_ref, own, other, m_ref, o_ref, aux_ref, xh_ref, vec_ref, xs, w, sems, tmp):
+    first_step(lambda: start_weights(own, other, w, sems))
+    images, rows, _ = o_ref.shape
+    load_padded(xs, x_ref, seq, rows, images)
+    first_step(lambda: wait_weights(own, other, w, sems), lambda: unpack_small(w, vec_ref, tmp))
+    attn_forward(seq, xs, vec_ref.at[0], w, m_ref, o_ref, aux_ref, xh_ref)
+
+
+def fm_kernel(seq, x_ref, o_ref, vec_ref, own, other, out_ref, a_ref, d_ref, xh_ref, rs_ref, xs, w, sems):
+    first_step(lambda: start_weights(own, other, w, sems))
+    images, rows, _ = o_ref.shape
+    load_padded(xs, x_ref, seq, rows, images)
+    first_step(lambda: wait_weights(own, other, w, sems))
+    mlp_forward(seq, xs, o_ref, vec_ref.at[0], w, 0, out_ref, a_ref, d_ref, xh_ref, rs_ref)
+
+
+def bm_kernel(seq, gr_ref, a_ref, d_ref, xh_ref, rs_ref, o_ref, vec_ref, own, other,
+              dx1_ref, do_ref, keep, send, vec_o, db1_o, gs, dwp, dw1, dw2, w, sems):
+    images, rows, width = xh_ref.shape
+    first_step(lambda: start_weights(own, other, w, sems), lambda: zero(dwp, dw1, dw2, vec_o, db1_o))
+    load_padded(gs, gr_ref, seq, rows, images)
+    first_step(lambda: wait_weights(own, other, w, sems))
+    mlp_backward(gs, a_ref, d_ref, xh_ref, rs_ref, o_ref, vec_ref.at[0], w, 0, dx1_ref, do_ref, dwp, dw1, dw2, vec_o, db1_o)
+
+    @last_step
     def _():
-        small = jnp.concatenate(
-            [vec_s[0:2, :], dbm_s[:, :width], dbm_s[:, 2 * width :], vec2[3:4, :], vec2[1:3, :], vec2[0:1, :],
-             jnp.zeros((120, width), F32)], 0)
-        sm[...] = jnp.zeros_like(sm)
-        sm[:, 0:128] = small.T
-        hid = db1.shape[1] // shards
-        for j in range(shards):
-            sm[j * part : j * part + 1, width - hid :] = db1[:, j * hid : (j + 1) * hid]
-        store_slots(keep, send, [rows_of(dwqkv, part, k, width) for k in range(3)] + [rows_of(sm, part, 0, width)])
+        store_slots(keep, send, mlp_pieces(dwp, dw1, dw2, w.shape[2]))
+
+
+def ba_kernel(seq, dx1_ref, m_ref, do_ref, xh_ref, aux_ref, vec_ref, vec2, db1, own, other,
+              dx_ref, keep, send, dm_s, dwqkv, vec_s, dbm_s, w, sems, sm):
+    first_step(lambda: start_weights(own, other, w, sems), lambda: zero(dwqkv, vec_s, dbm_s))
+    attn_backward(seq, m_ref, do_ref, aux_ref, dm_s)
+    first_step(lambda: wait_weights(own, other, w, sems))
+    qkv_backward(seq, dx1_ref, dm_s, xh_ref, aux_ref, vec_ref.at[0], w, dx_ref, dwqkv, vec_s, dbm_s)
+
+    @last_step
+    def _():
+        part = w.shape[2]
+        small_slab(sm, vec_s, dbm_s, vec2, db1, part)
+        store_slots(keep, send, attn_pieces(dwqkv, sm, part))
+
+
+def top_kernel(seq, x_ref, cot_ref, vec_ref, own, other, out_ref, dx_ref, keep, send,
+               xs, gs, m_s, o_s, aux_s, xa_s, xm_s, rs_s, a_s, d_s, dx1_s, do_s, dm_s,
+               dwqkv, dwp, dw1, dw2, vec_a, vec_m, dbm_s, db1_s, sm, w, sems):
+    images, rows, width = o_s.shape
+    vec = vec_ref.at[1]
+    first_step(lambda: start_weights(own, other, w, sems),
+               lambda: zero(dwqkv, dwp, dw1, dw2, vec_a, vec_m, dbm_s, db1_s))
+    load_padded(xs, x_ref, seq, rows, images)
+    load_padded(gs, cot_ref, seq, rows, images)
+    first_step(lambda: wait_weights(own, other, w, sems))
+    attn_forward(seq, xs, vec, w, m_s, o_s, aux_s, xa_s)
+    mlp_forward(seq, xs, o_s, vec, w, 3, out_ref, a_s, d_s, xm_s, rs_s)
+    mlp_backward(gs, a_s, d_s, xm_s, rs_s, o_s, vec, w, 3, dx1_s, do_s, dwp, dw1, dw2, vec_m, db1_s)
+    attn_backward(seq, m_s, do_s, aux_s, dm_s)
+    qkv_backward(seq, dx1_s, dm_s, xa_s, aux_s, vec, w, dx_ref, dwqkv, vec_a, dbm_s)
+
+    @last_step
+    def _():
+        part = w.shape[2]
+        small_slab(sm, vec_a, dbm_s, vec_m, db1_s, part)
+        store_slots(keep, send, attn_pieces(dwqkv, sm, part) + mlp_pieces(dwp, dw1, dw2, part))
 
 
 def finish_kernel(*refs):
-    ins, outs = refs[:8], refs[8:]
+    ins, outs = refs[:6], refs[6:]
     o_qkv, o_proj, o_up, o_down, o_bup = outs[:5]
     smalls = outs[5:]
     part, width = ins[0].shape[1:]
     hid = o_bup.shape[1]
     quart = o_up.shape[2] // width
     for layer in range(2):
-        a1, a2, m1, m2 = ins[4 * layer : 4 * layer + 4]
+        a1, a2 = ins[4:6] if layer == 1 else ins[0:2]
+        m1, m2, base = (*ins[4:6], 4) if layer == 1 else (*ins[2:4], 0)
         for k in range(3):
             o_qkv[layer, :, k * width : (k + 1) * width] = a1[k].astype(F32) + a2[k].astype(F32)
         small = a1[3].astype(F32) + a2[3].astype(F32)
@@ -402,10 +434,14 @@
         pad = jnp.concatenate([small[:, 0:128], jnp.zeros((128 - part, 128), F32)], 0).T
         for p, ref in enumerate(smalls):
             ref[layer : layer + 1, :] = pad[p : p + 1, 0:part]
-        o_proj[layer] = m1[0].astype(F32) + m2[0].astype(F32)
+
+        def both(k):
+            return m1[base + k].astype(F32) + m2[base + k].astype(F32)
+
+        o_proj[layer] = both(0)
         for q in range(quart):
-            o_up[layer, :, q * width : (q + 1) * width] = m1[1 + q].astype(F32) + m2[1 + q].astype(F32)
-            o_down[layer, q * part : (q + 1) * part] = m1[1 + quart + q].astype(F32) + m2[1 + quart + q].astype(F32)
+            o_up[layer, :, q * width : (q + 1) * width] = both(1 + q)
+            o_down[layer, q * part : (q + 1) * part] = both(1 + quart + q)
 
 
 def blk(shape):
@@ -426,7 +462,7 @@
     return jax.ShapeDtypeStruct(shape, dt)
 
 
-COST = {"fa": 14, "fm": 18, "bm": 27, "bq": 13}
+COST = {"fa": 13, "fm": 18, "bm": 26, "ba": 28, "top": 70}
 
 
 def call(kern, name, per, blocked_in, whole_in, any_in, blocked_out, whole_out, scratch):
@@ -460,24 +496,39 @@
     )(*smalls, bias_up, w_qkv, w_proj, w_up, w_down)
 
 
-def run_fa(x, layer, vec, wa, ff, per):
+def run_fa(x, wa, ff, per):
     images, seq, width = x.shape
     rows = pad_rows(seq)
-    outs = [sds((images, rows, 3 * width), BF), sds((images, rows, width), BF), sds((images, 8, rows), F32),
-            sds((images, rows, width), BF)]
-    scratch = [pltpu.VMEM((per * rows, width), F32)] + wscratch(wa[0])
-    if layer == 0:
-        return call(functools.partial(fa_kernel, seq, 0), "fa", per, [x], [], wa, outs, [sds((2, 16, width), F32)],
-                    scratch + [pltpu.VMEM((2, ff), F32)])
-    return call(functools.partial(fa_kernel, seq, 1), "fa", per, [x], [vec], wa, outs, [], scratch)
-
-
-def run_fm(x, layer, o, vec, wm, per):
+    return call(
+        functools.partial(fa_kernel, seq), "fa", per, [x], [], wa,
+        [sds((images, rows, 3 * width), BF), sds((images, rows, width), BF), sds((images, 8, rows), F32),
+         sds((images, rows, width), BF)], [sds((2, 16, width), F32)],
+        [pltpu.VMEM((per * rows, width), F32)] + wscratch(wa[0]) + [pltpu.VMEM((2, ff), F32)])
+
+
+def run_top(x, cot, vec, wt, per):
+    images, seq, width = x.shape
+    rows = pad_rows(seq)
+    ff = (wt[0].shape[1] - 4) // 2 * width
+    n = per * rows
+    cells = lambda c: pltpu.VMEM((per, rows, c), BF)
+    tall8 = pltpu.VMEM((per, 8, rows), F32)
+    full = lambda r, c: pltpu.VMEM((r, c), F32)
+    return call(
+        functools.partial(top_kernel, seq), "top", per, [x, cot], [vec], wt,
+        [sds((images, seq, width), F32), sds((images, seq, width), F32)], slots(wt[0], wt[0].shape[1] + 1),
+        [full(n, width), full(n, width), cells(3 * width), cells(width), tall8, cells(width), cells(width), tall8,
+         cells(ff), cells(ff), pltpu.VMEM((per, rows, width), F32), cells(width), cells(3 * width),
+         full(width, 3 * width), full(width, width), full(width, ff), full(ff, width), full(8, width), full(8, width),
+         full(1, 3 * width), full(1, ff), full(width, width)] + wscratch(wt[0]))
+
+
+def run_fm(x, o, vec, wm, per):
     images, seq, width = x.shape
     rows = o.shape[1]
     ff = (wm[0].shape[1] - 1) // 2 * width
     return call(
-        functools.partial(fm_kernel, seq, layer), "fm", per, [x, o], [vec], wm,
+        functools.partial(fm_kernel, seq), "fm", per, [x, o], [vec], wm,
         [sds((images, seq, width), F32), sds((images, rows, ff), BF), sds((images, rows, ff), BF),
          sds((images, rows, width), BF), sds((images, 8, rows), F32)], [],
         [pltpu.VMEM((per * rows, width), F32)] + wscratch(wm[0]))
@@ -485,52 +536,30 @@
 
 def slots(own, count):
     half, _, part, width = own.shape
-    return [sds((half, count, part, width), F32), sds((half, count, part, width), BF)]
-
-
-def run_bm(gr, layer, a, d, xh, rs, o, vec, wm, per):
+    return [sds((half, count, part, width), BF)] * 2
+
+
+def run_bm(gr, a, d, xh, rs, o, vec, wm, per):
     images, seq, width = gr.shape
     rows, ff = a.shape[1:]
     return call(
-        functools.partial(bm_kernel, seq, layer), "bm", per, [gr, a, d, xh, rs, o], [vec], wm,
+        functools.partial(bm_kernel, seq), "bm", per, [gr, a, d, xh, rs, o], [vec], wm,
         [sds((images, rows, width), F32), sds((images, rows, width), BF)],
         slots(wm[0], wm[0].shape[1]) + [sds((8, width), F32), sds((1, ff), F32)],
         [pltpu.VMEM((per * rows, width), F32), pltpu.VMEM((width, width), F32), pltpu.VMEM((width, ff), F32),
          pltpu.VMEM((ff, width), F32)] + wscratch(wm[0]))
 
 
-def run_bs(seq, m, o, do, aux, per, first=0, count=None, prev=None):
-    count = count or m.shape[0] - first
-    base = first // per
-
-    def at(shape):
-        nd = len(shape)
-        return pl.BlockSpec((per,) + shape[1:], lambda i: (i + base,) + (0,) * (nd - 1))
-
-    more = [] if prev is None else [prev]
-    return pl.pallas_call(
-        functools.partial(bs_kernel, seq),
-        grid=(count // per,),
-        in_specs=[at(a.shape) for a in (m, o, do, aux)] + [anyspec() for _ in more],
-        out_specs=at(m.shape),
-        out_shape=sds(m.shape, BF),
-        input_output_aliases={4: 0} if more else {},
-        compiler_params=pltpu.CompilerParams(vmem_limit_bytes=VMEM_LIMIT),
-        name="bs",
-        cost_estimate=pl.CostEstimate(flops=18 * count // m.shape[0] * 1_150_000_000, bytes_accessed=0, transcendentals=0),
-    )(m, o, do, aux, *more)
-
-
-def run_bq(seq, layer, dx1, dm, xh, aux, vec, vec2, db1, wa, per):
+def run_ba(seq, dx1, m, do, xh, aux, vec, vec2, db1, wa, per):
     images, rows, width = dx1.shape
     return call(
-        functools.partial(bq_kernel, seq, layer), "bq", per, [dx1, dm, xh, aux], [vec, vec2, db1], wa,
+        functools.partial(ba_kernel, seq), "ba", per, [dx1, m, do, xh, aux], [vec, vec2, db1], wa,
         [sds((images, seq, width), F32)], slots(wa[0], 4),
-        [pltpu.VMEM((width, 3 * width), F32), pltpu.VMEM((8, width), F32), pltpu.VMEM((1, 3 * width), F32)]
-        + wscratch(wa[0]) + [pltpu.VMEM((width, width), F32)])
-
-
-def run_finish(a0, m0, a1, m1, ff):
+        [pltpu.VMEM((per, rows, 3 * width), BF), pltpu.VMEM((width, 3 * width), F32), pltpu.VMEM((8, width), F32),
+         pltpu.VMEM((1, 3 * width), F32)] + wscratch(wa[0]) + [pltpu.VMEM((width, width), F32)])
+
+
+def run_finish(a0, m0, l1, ff):
     part, width = a0[0].shape[1:]
     return pl.pallas_call(
         finish_kernel,
@@ -538,7 +567,7 @@
                    sds((2, ff // width * part, width), F32), sds((2, ff // width * part), F32)]
         + [sds((2, part), F32)] * 8,
         name="finish",
-    )(*a0, *m0, *a1, *m1)
+    )(*a0, *m0, *l1)
 
 
 def xor_pairs(count, b):
@@ -567,9 +596,6 @@
     def swap(x, b):
         return lax.ppermute(x, "shard", xor_pairs(n, b))
 
-    def grow(x, b):
-        return jnp.concatenate([x, swap(x, b)])
-
     def direct(x):
         masks = [0]
         for b in upper:
@@ -587,22 +613,17 @@
     m0 = jnp.stack([m0[0]] + [tie(y, a0x) for y in m0[1:]])
     m0x = swap(m0, 2)
     l1 = direct(tie(l1, m0))
-    mix0, o0, aux0, xa0, vec = run_fa(tie(tokens, m0, l1[0]), 0, None, a0, ff, per)
-    o0, m0x, *l1 = group(o0, m0x, *l1)
+    mix, o, aux, xa, vec = run_fa(tie(tokens, m0, l1[0]), a0, ff, per)
+    o, m0x, *l1 = group(o, m0x, *l1)
     m0 = jnp.concatenate([m0, m0x])
     l1 = jnp.stack(l1)
     m0 = (m0, swap(tie(m0, l1), 1))
     l1x = swap(l1, 2)
-    layer_one, act0, der0, xm0, rs0 = run_fm(tokens, 0, o0, vec, m0, per)
+    layer_one, act, der, xm, rs = run_fm(tokens, o, vec, m0, per)
     layer_one, l1x = group(layer_one, l1x)
-    a1 = jnp.concatenate([l1[:, :3], l1x[:, :3]])
-    m1 = jnp.concatenate([l1[:, 3:], l1x[:, 3:]])
-    a1 = (a1, swap(a1, 1))
-    m1x = swap(m1, 1)
-    mix1, o1, aux1, xa1 = run_fa(tie(layer_one, m1), 1, vec, a1, ff, per)
-    o1, m1x = group(o1, m1x)
-    m1 = (m1, m1x)
-    layer_two, act1, der1, xm1, rs1 = run_fm(layer_one, 1, o1, vec, m1, per)
+    l1 = jnp.concatenate([l1, l1x])
+    l1 = (l1, swap(l1, 1))
+    layer_two, grad, kp, sn = run_top(layer_one, cotangent, vec, l1, per)
 
     class Sum:
         def __init__(self, keep, send):
@@ -623,7 +644,7 @@
             return self
 
         def total(self, lo, hi):
-            t = self.keep[lo:hi]
+            t = self.keep[lo:hi].astype(F32)
             for g in self.got:
                 t = t + g[lo:hi].astype(F32)
             return t
@@ -647,43 +668,31 @@
     def sent(value, *sums):
         return tie(value, *[s.send for s in sums])
 
-    dx1, do, kp, sn, v2, db1 = run_bm(cotangent, 1, act1, der1, xm1, rs1, o1, vec, m1, per)
-    gm1 = Sum(kp, sn).start()
-    dm = run_bs(seq, mix1, o1, do, aux1, per)
-    dm = meet(dm, gm1)
-    gm1.start()
-    grad, kp, sn = run_bq(seq, 1, dx1, sent(dm, gm1), xa1, aux1, vec, v2, db1, a1, per)
-    ga1 = Sum(kp, sn).start()
-    grad = meet(grad, gm1)
-    gm1.start()
-    dx1, do, kp, sn, v2, db1 = run_bm(sent(grad, gm1), 0, act0, der0, xm0, rs0, o0, vec, m0, per)
+    g1 = Sum(kp, sn).start().done().start()
+    dx1, do, kp, sn, v2, db1 = run_bm(sent(grad, g1), act, der, xm, rs, o, vec, m0, per)
+    do = meet(do, g1)
+    g1.start()
     gm0 = Sum(kp, sn).start()
-    do = meet(do, gm1, ga1)
-    gm1.start()
-    ga1.start()
-    first = images // (2 * per) * per
-    dm = run_bs(seq, mix0, o0, sent(do, gm1, ga1), aux0, per, 0, first)
-    dm = meet(dm, gm1, ga1, gm0)
-    ga1.start()
-    gm0.start()
-    fin_m1 = gm1.replicas()
-    dm = run_bs(seq, mix0, o0, do, aux0, per, first, None, sent(dm, gm1, ga1, gm0))
-    dm = meet(dm, ga1, gm0)
-    ga1.start()
-    gm0.start()
-    tokens_grad, kp, sn = run_bq(seq, 0, dx1, sent(dm, ga1, gm0), xa0, aux0, vec, v2, db1, a0, per)
+    tokens_grad, kp, sn = run_ba(seq, dx1, mix, sent(do, g1), xa, aux, vec, v2, db1, a0, per)
+    sn, g1.flight, gm0.flight = group(sn, g1.flight, gm0.flight)
     ga0 = Sum(kp, sn).start()
-    tokens_grad = meet(tokens_grad, ga1, gm0)
-    fin_a1 = ga1.replicas()
-    gm0.start()
+    gm0.done().start()
+    g1.done().start()
+    ga0.flight = tie(ga0.flight, gm0.send)
     ga0.done().start()
-    gm0.flight = tie(gm0.flight, ga0.send)
+    gm0.done().start()
+    g1.flight = tie(g1.flight, ga0.send)
+    g1.done()
+    fin_1 = g1.replicas()
+    ga0.done().start()
+    gm0.done().start()
+    ga0.done().start()
     gm0.done()
     fin_m0 = gm0.replicas()
-    ga0.done().start().done().start().done()
+    ga0.done()
     fin_a0 = ga0.replicas()
 
-    g_qkv, g_proj, g_up, g_down, g_bup, *s = run_finish(fin_a0, fin_m0, fin_a1, fin_m1, ff)
+    g_qkv, g_proj, g_up, g_down, g_bup, *s = run_finish(fin_a0, fin_m0, fin_1, ff)
     return (layer_one, layer_two, tokens_grad, s[0], s[1], g_qkv, s[2], s[3], g_proj, s[4], s[5], s[6],
             g_up, g_bup, g_down, s[7])
 def solution(mesh):

time: 297 us -> 271 us (0.912)
  Pallas kernels: 184 us -> 160 us
  other arithmetic: 20.7 us -> 13.8 us
  waiting for transfers between devices: 44.9 us -> 48.8 us
    pallas_call x3 -> x0, Pallas kernels: 38.6 us -> none  [run_bs(): pl.pallas_call(functools.partial(bs_kernel, seq), grid=(count // per,), i...]
    pallas_call x8 -> x5, Pallas kernels: 141 us -> 156 us  [call(): pl.pallas_call(kern, grid=(blocked_in[0].shape[0] // per,), in_specs=in_s...]
    convert_element_type x12 -> x9, other arithmetic: 15.2 us -> 9.39 us  [done(): self.send = self.total(size // 2, size).astype(BF)]
    ppermute x4 -> x3, starting transfers between devices: 7 us -> 3.93 us  [replicas(): other = lax.ppermute(mine, 'replica', xor_pairs(reps, b))]
    unnamed x50 -> x48, local copies, waits for them, and re-layouts: 6 us -> 8.66 us
    ppermute x32 -> x27, waiting for transfers between devices: 43 us -> 44.8 us  [swap(): return lax.ppermute(x, 'shard', xor_pairs(n, b))]
    ppermute x32 -> x27, starting transfers between devices: 31.8 us -> 32.9 us  [swap(): return lax.ppermute(x, 'shard', xor_pairs(n, b))]
  transfers between devices with their start and end apart: 36 -> 30, of which waited for: 20 -> 18; matrix products, arithmetic and copies ran while one was open for 4% -> 4% of each run, Pallas kernels for 41% -> 32%
where the time goes in v3:
time: 271 us; the launch traced here: 270 us
  Pallas kernels  160 us (59%)
  waiting for transfers between devices  48.8 us (18%)
  starting transfers between devices  36.8 us (14%)
  other arithmetic  13.8 us (5%)
  local copies, waits for them, and re-layouts  9 us (3%)
    pallas_call x5, Pallas kernels, call(): pl.pallas_call(kern, grid=(blocked_in[0].shape[0] // per,), in_specs=in_s...  156 us
    ppermute x27, waiting for transfers between devices, swap(): return lax.ppermute(x, 'shard', xor_pairs(n, b))  44.8 us
    ppermute x27, starting transfers between devices, swap(): return lax.ppermute(x, 'shard', xor_pairs(n, b))  32.9 us
    convert_element_type x9, other arithmetic, done(): self.send = self.total(size // 2, size).astype(BF)  9.39 us
    unnamed x48, local copies, waits for them, and re-layouts  8.66 us
  transfers between devices with their start and end apart: 30, of which 18 were waited for; matrix products, arithmetic and copies ran while one was open for 4% of the time, Pallas kernels for 32%

profile of v3, /device:TPU:0, one launch (start us, length us, event | category | flops | bytes accessed | tf_op | source)
XLA Modules:
  0.0 269.9 jit_solution(17111068325755080983)
XLA Ops:
  0.7 1.9 pack.1
  2.6 5.0 %collective-permute-start.2 = (bf16[4,24,384]{2,1,0:T(8,128)(2,1)}, bf16[4,24,384]{2,1,0:T(8,128)(2,1)S(1)}, u32[]{:S(2)}, u32[]{:S(2)}) collective-permute-start(bf16[4,24,384]{2,1,0:T(8,128)(2,1)} %get-tuple-element.80), channel_id=1, source_target_pairs={{0,12},{1,13},{2,14},{3,15},{4,8},{5,9},{6,10},{7,11},{8,4},{9,5},... | collective-permute-start | bytes 221192 | tf_op jit(solution)/shard_map/ppermute | solution.py:597
  14.6 3.3 %collective-permute-start.6 = (bf16[9,24,384]{2,1,0:T(8,128)(2,1)}, bf16[9,24,384]{2,1,0:T(8,128)(2,1)S(1)}, u32[]{:S(2)}, u32[]{:S(2)}) collective-permute-start(bf16[9,24,384]{2,1,0:T(8,128)(2,1)} %get-tuple-element.81), channel_id=1, source_target_pairs={{0,12},{1,13},{2,14},{3,15},{4,8},{5,9},{6,10},{7,11},{8,4},{9,5},... | collective-permute-start | bytes 497672 | tf_op jit(solution)/shard_map/ppermute | solution.py:597
  21.7 2.2 collective-permute-done.6
  23.9 2.0 collective-permute-done.4
  26.4 4.5 %collective-permute-done.3 = bf16[9,24,384]{2,1,0:T(8,128)(2,1)S(1)} collective-permute-done((bf16[9,24,384]{2,1,0:T(8,128)(2,1)}, bf16[9,24,384]{2,1,0:T(8,128)(2,1)S(1)}, u32[]{:S(2)}, u32[]{:S(2)}) %collective-permute-start.3) | collective-permute-done | bytes 165920 | tf_op jit(solution)/shard_map/ppermute | solution.py:597
  31.9 2.7 %collective-permute-start.11 = (bf16[12,24,384]{2,1,0:T(8,128)(2,1)S(1)}, bf16[12,24,384]{2,1,0:T(8,128)(2,1)S(1)}, u32[]{:S(2)}, u32[]{:S(2)}) collective-permute-start(bf16[12,24,384]{2,1,0:T(8,128)(2,1)S(1)} %copy-done.3), channel_id=1, source_target_pairs={{0,12},{1,13},{2,14},{3,15},{4,8},{5,9},{6,10},{7,11},{8,4},{9,5},... | collective-permute-start | bytes 663560 | tf_op jit(solution)/shard_map/ppermute | solution.py:597
  41.1 13.9 %fa.1 = (bf16[10,208,1152]{2,1,0:T(8,128)(2,1)}, bf16[10,208,384]{2,1,0:T(8,128)(2,1)}, f32[10,8,208]{2,1,0:T(8,128)}, bf16[10,208,384]{2,1,0:T(8,128)(2,1)}, f32[2,16,384]{2,1,0:T(8,128)}) custom-call(bf16[10,197,384]{2,1,0:T(8,128)(2,1)} %x_ref.2, bf16[8,4,24,384]{3,2,1,0:T(8,128)(2,1)} %copy-done.14, bf16[8,4,24,384]{3,2,1,0:T(8,128)(2,1)} %copy-done.17), custom_call_target="tpu_custom_call" | custom-call | flops 14949999616 | tf_op jit(solution)/shard_map/fa/pallas_call | solution.py:471
  59.5 17.8 %fm.1 = (f32[10,197,384]{2,1,0:T(8,128)}, bf16[10,208,1536]{2,1,0:T(8,128)(2,1)}, bf16[10,208,1536]{2,1,0:T(8,128)(2,1)}, bf16[10,208,384]{2,1,0:T(8,128)(2,1)}, f32[10,8,208]{2,1,0:T(8,128)}) custom-call(bf16[10,197,384]{2,1,0:T(8,128)(2,1)} %x_ref.2, bf16[10,208,384]{2,1,0:T(8,128)(2,1)} %get-tuple-element.89.o_ref, ...), custom_call_target="tpu_custom_call" | custom-call | flops 20700000256 | tf_op jit(solution)/shard_map/fm/pallas_call | solution.py:471
  77.7 3.7 %collective-permute-done.14.other = bf16[8,12,24,384]{3,2,1,0:T(8,128)(2,1)S(1)} collective-permute-done((bf16[8,12,24,384]{3,2,1,0:T(8,128)(2,1)S(1)}, bf16[8,12,24,384]{3,2,1,0:T(8,128)(2,1)S(1)}, u32[]{:S(2)}, u32[]{:S(2)}) %collective-permute-start.14) | collective-permute-done | bytes 1769504 | tf_op jit(solution)/shard_map/ppermute | solution.py:597
  82.6 69.5 %top.1 = (f32[10,197,384]{2,1,0:T(8,128)}, f32[10,197,384]{2,1,0:T(8,128)}, bf16[8,13,24,384]{3,2,1,0:T(8,128)(2,1)}, bf16[8,13,24,384]{3,2,1,0:T(8,128)(2,1)}) custom-call(f32[10,197,384]{2,1,0:T(8,128)} %get-tuple-element.63.x_ref, bf16[10,197,384]{2,1,0:T(8,128)(2,1)} %cot_ref.1, f32[2,16,384]{2,1,0:T(8,128)} %get-tuple-element.90.vec_ref, ...), custom_call_target="tpu_custom_call" | custom-call | flops 80499998720 | tf_op jit(solution)/shard_map/top/pallas_call | solution.py:471
  152.3 4.0 %collective-permute-done.15 = bf16[8,13,24,384]{3,2,1,0:T(8,128)(2,1)S(1)} collective-permute-done((bf16[8,13,24,384]{3,2,1,0:T(8,128)(2,1)}, bf16[8,13,24,384]{3,2,1,0:T(8,128)(2,1)S(1)}, u32[]{:S(2)}, u32[]{:S(2)}) %collective-permute-start.15) | collective-permute-done | bytes 1916960 | tf_op jit(solution)/shard_map/ppermute | solution.py:597
  156.3 2.4 add_convert_fusion
  159.0 25.9 %bm.1 = (f32[10,208,384]{2,1,0:T(8,128)}, bf16[10,208,384]{2,1,0:T(8,128)(2,1)}, bf16[8,9,24,384]{3,2,1,0:T(8,128)(2,1)}, bf16[8,9,24,384]{3,2,1,0:T(8,128)(2,1)}, f32[8,384]{1,0:T(8,128)}, /*index=5*/f32[1,1536]{1,0:T(1,128)}) custom-call(f32[10,197,384]{2,1,0:T(8,128)} %get-tuple-element.104.gr_ref, bf16[10,208,1536]{2,1,0:T(8,128)(2,1)} %get-tuple-element.105.a_ref, ...), custom_call_target="tpu_custom_call" | custom-call | flops 29899999232 | tf_op jit(solution)/shard_map/bm/pallas_call | solution.py:471
  185.0 2.0 add_convert_fusion.2
  188.0 29.0 %ba.1 = (f32[10,197,384]{2,1,0:T(8,128)}, bf16[8,4,24,384]{3,2,1,0:T(8,128)(2,1)}, bf16[8,4,24,384]{3,2,1,0:T(8,128)(2,1)}) custom-call(f32[10,208,384]{2,1,0:T(8,128)} %get-tuple-element.109.dx1_ref, bf16[10,208,1152]{2,1,0:T(8,128)(2,1)} %get-tuple-element.110.m_ref, bf16[10,208,384]{2,1,0:T(8,128)(2,1)} %get-tuple-element.114.do_ref, ...), custom_call_target="tpu_custom_call" | custom-call | flops 32199999488 | tf_op jit(solution)/shard_map/ba/pallas_call | solution.py:471
  221.8 3.0 %collective-permute-start.28 = (bf16[1,13,24,384]{3,2,1,0:T(8,128)(2,1)S(1)}, bf16[1,13,24,384]{3,2,1,0:T(8,128)(2,1)S(1)}, u32[]{:S(2)}, u32[]{:S(2)}) collective-permute-start(bf16[1,13,24,384]{3,2,1,0:T(8,128)(2,1)S(1)} %add_convert_fusion.6), channel_id=1, source_target_pairs={{0,8},{1,9},{2,10},{3,11},{4,12},{5,13},{6,14},{7,15},{8,0},{9,1},... | collective-permute-start | bytes 718856 | tf_op jit(solution)/shard_map/ppermute | solution.py:597
  225.3 10.7 %collective-permute-done.28 = bf16[1,13,24,384]{3,2,1,0:T(8,128)(2,1)S(1)} collective-permute-done((bf16[1,13,24,384]{3,2,1,0:T(8,128)(2,1)S(1)}, bf16[1,13,24,384]{3,2,1,0:T(8,128)(2,1)S(1)}, u32[]{:S(2)}, u32[]{:S(2)}) %collective-permute-start.28) | collective-permute-done | bytes 239648 | tf_op jit(solution)/shard_map/ppermute | solution.py:597
  243.6 4.7 %collective-permute-done.25 = bf16[2,9,24,384]{3,2,1,0:T(8,128)(2,1)S(1)} collective-permute-done((bf16[2,9,24,384]{3,2,1,0:T(8,128)(2,1)S(1)}, bf16[2,9,24,384]{3,2,1,0:T(8,128)(2,1)S(1)}, u32[]{:S(2)}, u32[]{:S(2)}) %collective-permute-start.25) | collective-permute-done | bytes 331808 | tf_op jit(solution)/shard_map/ppermute | solution.py:597
  249.3 2.9 %collective-permute-start.26 = (bf16[1,9,24,384]{3,2,1,0:T(8,128)(2,1)S(1)}, bf16[1,9,24,384]{3,2,1,0:T(8,128)(2,1)S(1)}, u32[]{:S(2)}, u32[]{:S(2)}) collective-permute-start(bf16[1,9,24,384]{3,2,1,0:T(8,128)(2,1)S(1)} %add_convert_fusion.8), channel_id=1, source_target_pairs={{0,8},{1,9},{2,10},{3,11},{4,12},{5,13},{6,14},{7,15},{8,0},{9,1},... | collective-permute-start | bytes 497672 | tf_op jit(solution)/shard_map/ppermute | solution.py:597
  252.2 2.1 collective-permute-start.22
  254.4 4.5 %collective-permute-done.26 = bf16[1,9,24,384]{3,2,1,0:T(8,128)(2,1)S(1)} collective-permute-done((bf16[1,9,24,384]{3,2,1,0:T(8,128)(2,1)S(1)}, bf16[1,9,24,384]{3,2,1,0:T(8,128)(2,1)S(1)}, u32[]{:S(2)}, u32[]{:S(2)}) %collective-permute-start.26) | collective-permute-done | bytes 165920 | tf_op jit(solution)/shard_map/ppermute | solution.py:597
  262.2 4.0 %collective-permute-done.23.refs_1_ = bf16[4,24,384]{2,1,0:T(8,128)(2,1)S(1)} collective-permute-done((bf16[4,24,384]{2,1,0:T(8,128)(2,1)S(1)}, bf16[4,24,384]{2,1,0:T(8,128)(2,1)S(1)}, u32[]{:S(2)}, u32[]{:S(2)}) %collective-permute-start.23) | collective-permute-done | bytes 73760 | tf_op jit(solution)/shard_map/ppermute | solution.py:655
  267.4 2.2 finish.1
  (109 shorter events, 44.6 us)
Async XLA Ops:
  2.6 8.4 %collective-permute-start.2 = (bf16[4,24,384]{2,1,0:T(8,128)(2,1)}, bf16[4,24,384]{2,1,0:T(8,128)(2,1)S(1)}, u32[]{:S(2)}, u32[]{:S(2)}) collective-permute-start(bf16[4,24,384]{2,1,0:T(8,128)(2,1)} %get-tuple-element.80), channel_id=1, source_target_pairs={{0,12},{1,13},{2,14},{3,15},{4,8},{5,9},{6,10},{7,11},{8,4},{9,5},... | collective-permute-start | bytes 221192 | tf_op jit(solution)/shard_map/ppermute | solution.py:597
  7.7 6.0 %collective-permute-start = (bf16[4,24,384]{2,1,0:T(8,128)(2,1)}, bf16[4,24,384]{2,1,0:T(8,128)(2,1)S(1)}, u32[]{:S(2)}, u32[]{:S(2)}) collective-permute-start(bf16[4,24,384]{2,1,0:T(8,128)(2,1)} %get-tuple-element.80), channel_id=1, source_target_pairs={{0,8},{1,9},{2,10},{3,11},{4,12},{5,13},{6,14},{7,15},{8,0},{9,1},... | collective-permute-start | bytes 221192 | tf_op jit(solution)/shard_map/ppermute | solution.py:597
  14.6 9.3 %collective-permute-start.6 = (bf16[9,24,384]{2,1,0:T(8,128)(2,1)}, bf16[9,24,384]{2,1,0:T(8,128)(2,1)S(1)}, u32[]{:S(2)}, u32[]{:S(2)}) collective-permute-start(bf16[9,24,384]{2,1,0:T(8,128)(2,1)} %get-tuple-element.81), channel_id=1, source_target_pairs={{0,12},{1,13},{2,14},{3,15},{4,8},{5,9},{6,10},{7,11},{8,4},{9,5},... | collective-permute-start | bytes 497672 | tf_op jit(solution)/shard_map/ppermute | solution.py:597
  17.9 8.5 %collective-permute-start.5 = (bf16[9,24,384]{2,1,0:T(8,128)(2,1)}, bf16[9,24,384]{2,1,0:T(8,128)(2,1)S(1)}, u32[]{:S(2)}, u32[]{:S(2)}) collective-permute-start(bf16[9,24,384]{2,1,0:T(8,128)(2,1)} %get-tuple-element.81), channel_id=1, source_target_pairs={{0,4},{1,5},{2,6},{3,7},{4,0},{5,1},{6,2},{7,3},{8,12},{9,13},{10,... | collective-permute-start | bytes 497672 | tf_op jit(solution)/shard_map/ppermute | solution.py:597
  17.9 13.0 %collective-permute-start.3 = (bf16[9,24,384]{2,1,0:T(8,128)(2,1)}, bf16[9,24,384]{2,1,0:T(8,128)(2,1)S(1)}, u32[]{:S(2)}, u32[]{:S(2)}) collective-permute-start(bf16[9,24,384]{2,1,0:T(8,128)(2,1)} %get-tuple-element.81), channel_id=1, source_target_pairs={{0,8},{1,9},{2,10},{3,11},{4,12},{5,13},{6,14},{7,15},{8,0},{9,1},... | collective-permute-start | bytes 497672 | tf_op jit(solution)/shard_map/ppermute | solution.py:597
  19.1 6.8 %collective-permute-start.4 = (bf16[4,4,24,384]{3,2,1,0:T(8,128)(2,1)S(1)}, bf16[4,4,24,384]{3,2,1,0:T(8,128)(2,1)S(1)}, u32[]{:S(2)}, u32[]{:S(2)}) collective-permute-start(bf16[4,4,24,384]{3,2,1,0:T(8,128)(2,1)S(1)} %pad_maximum_fusion.2), channel_id=1, source_target_pairs={{0,2},{1,3},{2,0},{3,1},{4,6},{5,7},{6,4},{7,5},{8,10},{9,11},{10,... | collective-permute-start | bytes 884744 | tf_op jit(solution)/shard_map/ppermute | solution.py:597
  31.9 23.1 %collective-permute-start.11 = (bf16[12,24,384]{2,1,0:T(8,128)(2,1)S(1)}, bf16[12,24,384]{2,1,0:T(8,128)(2,1)S(1)}, u32[]{:S(2)}, u32[]{:S(2)}) collective-permute-start(bf16[12,24,384]{2,1,0:T(8,128)(2,1)S(1)} %copy-done.3), channel_id=1, source_target_pairs={{0,12},{1,13},{2,14},{3,15},{4,8},{5,9},{6,10},{7,11},{8,4},{9,5},... | collective-permute-start | bytes 663560 | tf_op jit(solution)/shard_map/ppermute | solution.py:597
  34.6 20.4 %collective-permute-start.10 = (bf16[12,24,384]{2,1,0:T(8,128)(2,1)S(1)}, bf16[12,24,384]{2,1,0:T(8,128)(2,1)S(1)}, u32[]{:S(2)}, u32[]{:S(2)}) collective-permute-start(bf16[12,24,384]{2,1,0:T(8,128)(2,1)S(1)} %copy-done.3), channel_id=1, source_target_pairs={{0,4},{1,5},{2,6},{3,7},{4,0},{5,1},{6,2},{7,3},{8,12},{9,13},{10,... | collective-permute-start | bytes 663560 | tf_op jit(solution)/shard_map/ppermute | solution.py:597
  34.6 20.4 %collective-permute-start.9 = (bf16[12,24,384]{2,1,0:T(8,128)(2,1)S(1)}, bf16[12,24,384]{2,1,0:T(8,128)(2,1)S(1)}, u32[]{:S(2)}, u32[]{:S(2)}) collective-permute-start(bf16[12,24,384]{2,1,0:T(8,128)(2,1)S(1)} %copy-done.3), channel_id=1, source_target_pairs={{0,8},{1,9},{2,10},{3,11},{4,12},{5,13},{6,14},{7,15},{8,0},{9,1},... | collective-permute-start | bytes 663560 | tf_op jit(solution)/shard_map/ppermute | solution.py:597
  36.4 18.6 %collective-permute-start.8 = (bf16[4,9,24,384]{3,2,1,0:T(8,128)(2,1)S(1)}, bf16[4,9,24,384]{3,2,1,0:T(8,128)(2,1)S(1)}, u32[]{:S(2)}, u32[]{:S(2)}) collective-permute-start(bf16[4,9,24,384]{3,2,1,0:T(8,128)(2,1)S(1)} %pad_maximum_fusion.1), channel_id=1, source_target_pairs={{0,2},{1,3},{2,0},{3,1},{4,6},{5,7},{6,4},{7,5},{8,10},{9,11},{10,... | collective-permute-start | bytes 1990664 | tf_op jit(solution)/shard_map/ppermute | solution.py:597
  55.5 21.9 %collective-permute-start.13 = (bf16[4,12,24,384]{3,2,1,0:T(8,128)(2,1)S(1)}, bf16[4,12,24,384]{3,2,1,0:T(8,128)(2,1)S(1)}, u32[]{:S(2)}, u32[]{:S(2)}) collective-permute-start(bf16[4,12,24,384]{3,2,1,0:T(8,128)(2,1)S(1)} %pad_maximum_fusion), channel_id=1, source_target_pairs={{0,2},{1,3},{2,0},{3,1},{4,6},{5,7},{6,4},{7,5},{8,10},{9,11},{10,... | collective-permute-start | bytes 2654216 | tf_op jit(solution)/shard_map/ppermute | solution.py:597
  158.7 26.4 %collective-permute-start.16 = (bf16[4,13,24,384]{3,2,1,0:T(8,128)(2,1)}, bf16[4,13,24,384]{3,2,1,0:T(8,128)(2,1)}, u32[]{:S(2)}, u32[]{:S(2)}) collective-permute-start(bf16[4,13,24,384]{3,2,1,0:T(8,128)(2,1)} %add_convert_fusion), channel_id=1, source_target_pairs={{0,2},{1,3},{2,0},{3,1},{4,6},{5,7},{6,4},{7,5},{8,10},{9,11},{10,... | collective-permute-start | bytes 2875400 | tf_op jit(solution)/shard_map/ppermute | solution.py:597
  184.9 32.1 %collective-permute-start.18 = (bf16[8,9,24,384]{3,2,1,0:T(8,128)(2,1)}, bf16[8,9,24,384]{3,2,1,0:T(8,128)(2,1)}, u32[]{:S(2)}, u32[]{:S(2)}) collective-permute-start(bf16[8,9,24,384]{3,2,1,0:T(8,128)(2,1)} %get-tuple-element.122), channel_id=1, source_target_pairs={{0,1},{1,0},{2,3},{3,2},{4,5},{5,4},{6,7},{7,6},{8,9},{9,8},{10,11... | collective-permute-start | bytes 3981320 | tf_op jit(solution)/shard_map/ppermute | solution.py:597
  187.0 30.0 %collective-permute-start.17 = (bf16[2,13,24,384]{3,2,1,0:T(8,128)(2,1)}, bf16[2,13,24,384]{3,2,1,0:T(8,128)(2,1)}, u32[]{:S(2)}, u32[]{:S(2)}) collective-permute-start(bf16[2,13,24,384]{3,2,1,0:T(8,128)(2,1)} %add_convert_fusion.2), channel_id=1, source_target_pairs={{0,4},{1,5},{2,6},{3,7},{4,0},{5,1},{6,2},{7,3},{8,12},{9,13},{10,... | collective-permute-start | bytes 1437704 | tf_op jit(solution)/shard_map/ppermute | solution.py:597
  217.0 7.8 %collective-permute-start.19 = (bf16[8,4,24,384]{3,2,1,0:T(8,128)(2,1)}, bf16[8,4,24,384]{3,2,1,0:T(8,128)(2,1)S(1)}, u32[]{:S(2)}, u32[]{:S(2)}) collective-permute-start(bf16[8,4,24,384]{3,2,1,0:T(8,128)(2,1)} %get-tuple-element.123), channel_id=1, source_target_pairs={{0,1},{1,0},{2,3},{3,2},{4,5},{5,4},{6,7},{7,6},{8,9},{9,8},{10,11... | collective-permute-start | bytes 1769480 | tf_op jit(solution)/shard_map/ppermute | solution.py:597
  218.9 17.8 %collective-permute-start.24 = (bf16[4,9,24,384]{3,2,1,0:T(8,128)(2,1)S(1)}, bf16[4,9,24,384]{3,2,1,0:T(8,128)(2,1)S(1)}, u32[]{:S(2)}, u32[]{:S(2)}) collective-permute-start(bf16[4,9,24,384]{3,2,1,0:T(8,128)(2,1)S(1)} %add_convert_fusion.1), channel_id=1, source_target_pairs={{0,2},{1,3},{2,0},{3,1},{4,6},{5,7},{6,4},{7,5},{8,10},{9,11},{10,... | collective-permute-start | bytes 1990664 | tf_op jit(solution)/shard_map/ppermute | solution.py:597
  221.8 14.2 %collective-permute-start.28 = (bf16[1,13,24,384]{3,2,1,0:T(8,128)(2,1)S(1)}, bf16[1,13,24,384]{3,2,1,0:T(8,128)(2,1)S(1)}, u32[]{:S(2)}, u32[]{:S(2)}) collective-permute-start(bf16[1,13,24,384]{3,2,1,0:T(8,128)(2,1)S(1)} %add_convert_fusion.6), channel_id=1, source_target_pairs={{0,8},{1,9},{2,10},{3,11},{4,12},{5,13},{6,14},{7,15},{8,0},{9,1},... | collective-permute-start | bytes 718856 | tf_op jit(solution)/shard_map/ppermute | solution.py:597
  224.9 17.5 %collective-permute-start.20 = (bf16[4,4,24,384]{3,2,1,0:T(8,128)(2,1)S(1)}, bf16[4,4,24,384]{3,2,1,0:T(8,128)(2,1)S(1)}, u32[]{:S(2)}, u32[]{:S(2)}) collective-permute-start(bf16[4,4,24,384]{3,2,1,0:T(8,128)(2,1)S(1)} %add_convert_fusion.4), channel_id=1, source_target_pairs={{0,2},{1,3},{2,0},{3,1},{4,6},{5,7},{6,4},{7,5},{8,10},{9,11},{10,... | collective-permute-start | bytes 884744 | tf_op jit(solution)/shard_map/ppermute | solution.py:597
  237.8 10.5 %collective-permute-start.25 = (bf16[2,9,24,384]{3,2,1,0:T(8,128)(2,1)S(1)}, bf16[2,9,24,384]{3,2,1,0:T(8,128)(2,1)S(1)}, u32[]{:S(2)}, u32[]{:S(2)}) collective-permute-start(bf16[2,9,24,384]{3,2,1,0:T(8,128)(2,1)S(1)} %add_convert_fusion.3), channel_id=1, source_target_pairs={{0,4},{1,5},{2,6},{3,7},{4,0},{5,1},{6,2},{7,3},{8,12},{9,13},{10,... | collective-permute-start | bytes 995336 | tf_op jit(solution)/shard_map/ppermute | solution.py:597
  240.1 22.1 %collective-permute-start.29 = (bf16[13,24,384]{2,1,0:T(8,128)(2,1)S(1)}, bf16[13,24,384]{2,1,0:T(8,128)(2,1)S(1)}, u32[]{:S(2)}, u32[]{:S(2)}) collective-permute-start(bf16[13,24,384]{2,1,0:T(8,128)(2,1)S(1)} %fusion.refs_4_), channel_id=1, source_target_pairs={{0,16},{16,0},{1,17},{17,1},{2,18},{18,2},{3,19},{19,3},{4,20},{20... | collective-permute-start | bytes 718856 | tf_op jit(solution)/shard_map/ppermute | solution.py:655
  242.4 9.7 %collective-permute-start.21 = (bf16[2,4,24,384]{3,2,1,0:T(8,128)(2,1)S(1)}, bf16[2,4,24,384]{3,2,1,0:T(8,128)(2,1)S(1)}, u32[]{:S(2)}, u32[]{:S(2)}) collective-permute-start(bf16[2,4,24,384]{3,2,1,0:T(8,128)(2,1)S(1)} %add_convert_fusion.9), channel_id=1, source_target_pairs={{0,4},{1,5},{2,6},{3,7},{4,0},{5,1},{6,2},{7,3},{8,12},{9,13},{10,... | collective-permute-start | bytes 442376 | tf_op jit(solution)/shard_map/ppermute | solution.py:597
  249.3 9.7 %collective-permute-start.26 = (bf16[1,9,24,384]{3,2,1,0:T(8,128)(2,1)S(1)}, bf16[1,9,24,384]{3,2,1,0:T(8,128)(2,1)S(1)}, u32[]{:S(2)}, u32[]{:S(2)}) collective-permute-start(bf16[1,9,24,384]{3,2,1,0:T(8,128)(2,1)S(1)} %add_convert_fusion.8), channel_id=1, source_target_pairs={{0,8},{1,9},{2,10},{3,11},{4,12},{5,13},{6,14},{7,15},{8,0},{9,1},... | collective-permute-start | bytes 497672 | tf_op jit(solution)/shard_map/ppermute | solution.py:597
  252.2 9.4 %collective-permute-start.22 = (bf16[1,4,24,384]{3,2,1,0:T(8,128)(2,1)S(1)}, bf16[1,4,24,384]{3,2,1,0:T(8,128)(2,1)S(1)}, u32[]{:S(2)}, u32[]{:S(2)}) collective-permute-start(bf16[1,4,24,384]{3,2,1,0:T(8,128)(2,1)S(1)} %add_convert_fusion.11), channel_id=1, source_target_pairs={{0,8},{1,9},{2,10},{3,11},{4,12},{5,13},{6,14},{7,15},{8,0},{9,1},... | collective-permute-start | bytes 221192 | tf_op jit(solution)/shard_map/ppermute | solution.py:597
  260.0 6.2 %collective-permute-start.27 = (bf16[9,24,384]{2,1,0:T(8,128)(2,1)S(1)}, bf16[9,24,384]{2,1,0:T(8,128)(2,1)S(1)}, u32[]{:S(2)}, u32[]{:S(2)}) collective-permute-start(bf16[9,24,384]{2,1,0:T(8,128)(2,1)S(1)} %fusion.1.refs_2_), channel_id=1, source_target_pairs={{0,16},{16,0},{1,17},{17,1},{2,18},{18,2},{3,19},{19,3},{4,20},{20... | collective-permute-start | bytes 497672 | tf_op jit(solution)/shard_map/ppermute | solution.py:655
  (24 other events, 175.3 us)

commit v4 on v3

--- a/solution.py
+++ b/solution.py
@@ -11,7 +11,7 @@
 HEADS = 6
 EPS = 1e-06
 NEG = -1e30
-VMEM_LIMIT = 60 * 2**20
+VMEM_LIMIT = 54 * 2**20
 
 
 def dot(a, b):
@@ -132,7 +132,7 @@
 
 def pack_kernel(*refs):
     smalls, (bias_up, w_qkv, w_proj, w_up, w_down) = refs[:8], refs[8:13]
-    out_a0, out_m0, out_l1, sq = refs[13:]
+    out_a0, out_l1, sq = refs[13:]
     part, width = out_a0.shape[1:]
     sq[...] = jnp.zeros_like(sq)
     for p, ref in enumerate(smalls):
@@ -144,7 +144,7 @@
     quart = w_up.shape[2] // width
     for layer in range(2):
         attn = out_a0 if layer == 0 else out_l1
-        rest, base = (out_m0, 0) if layer == 0 else (out_l1, 3)
+        rest, base = (out_a0, 4) if layer == 0 else (out_l1, 3)
         for k in range(3):
             attn[k] = w_qkv[layer, :, k * width : (k + 1) * width]
         rest[base] = w_proj[layer]
@@ -184,23 +184,20 @@
     low = lane < 64
     kpad = jnp.where(row >= seq, NEG, 0.0).astype(BF)
     ones = jnp.where(row >= seq, 0.0, 1.0).astype(BF)
-    qone0 = jnp.where(lane == 64, 1.0, 0.0).astype(BF)
-    qone1 = jnp.where(lane == 0, 1.0, 0.0).astype(BF)
-    valid = row < seq
+    first = lax.broadcasted_iota(jnp.int32, (1, 128), 1)
+    mine = [jnp.where(first < 64, 1.0, 0.0).astype(BF), jnp.where(first < 64, 0.0, 1.0).astype(BF)]
+    mark = [jnp.where(first == 64, 1.0, 0.0).astype(BF), jnp.where(first == 0, 1.0, 0.0).astype(BF)]
+    kpads = [kpad * mark[0], kpad * mark[1]]
     for g in range(images):
         aux = jnp.broadcast_to(rstd[g * rows : (g + 1) * rows], (rows, 128))
         for p in range(width // 128):
             q2 = m_ref[g, :, p * 128 : (p + 1) * 128] * jnp.asarray(0.125, BF)
             k2 = m_ref[g, :, width + p * 128 : width + (p + 1) * 128]
             v2 = m_ref[g, :, 2 * width + p * 128 : 2 * width + (p + 1) * 128]
-            v2 = jnp.where(valid, v2, jnp.zeros_like(v2))
-            vext = jnp.concatenate([v2, ones], 1)
+            vext = jnp.concatenate([v2 * ones, ones], 1)
             parts = []
             for half in range(2):
-                mine = low if half == 0 else ~low
-                qh = jnp.where(mine, q2, qone0 if half == 0 else qone1)
-                kh = jnp.where(mine, k2, kpad)
-                s = dot_nt(qh, kh)
+                s = dot_nt(q2 * mine[half] + mark[half], k2 * mine[half] + kpads[half])
                 mx = jnp.max(s, -1, keepdims=True)
                 pr = jnp.exp(s - mx).astype(BF)
                 oe = dot(pr, vext)
@@ -262,7 +259,7 @@
         dn2 = dn2 + dot_nt(dh, slabs(w, base + 1 + 2 * c, 2))
     rstd = jnp.concatenate([to_column(rs_ref[g], 0) for g in range(images)], 0)
     dx1 = gs[...] + norm_back(dn2 * vec[5:6, :], xhat, rstd)
-    dx1_ref[...] = dx1.reshape(images, rows, width)
+    dx1_ref[...] = dx1.reshape(images, rows, width).astype(dx1_ref.dtype)
     dy = dx1.astype(BF)
     dwp[...] += dot_tn(flat(o_ref[...]), dy)
     do_ref[...] = dot_nt(dy, slabs(w, base, 1)).astype(BF).reshape(images, rows, width)
@@ -278,31 +275,46 @@
     low = lane < 64
     last = rows - 16
     valid = lax.broadcasted_iota(jnp.int32, (16, rows), 0) < seq - last
-    none = jnp.zeros((rows, 128), BF)
-    for g in range(images):
-        lse = aux_ref[g]
-        for p in range(width // 128):
-            q2 = m_ref[g, :, p * 128 : (p + 1) * 128] * jnp.asarray(0.125, BF)
-            k2 = m_ref[g, :, width + p * 128 : width + (p + 1) * 128]
-            v2 = m_ref[g, :, 2 * width + p * 128 : 2 * width + (p + 1) * 128]
-            do2 = do_ref[g, :, p * 128 : (p + 1) * 128]
-            kt = (k2 * jnp.asarray(0.125, BF)).T
-            dks, dvs, dqs = [], [], []
-            for half in range(2):
-                h = 2 * p + half
-                kh = jnp.where(low, k2, none) if half == 0 else jnp.where(low, none, k2)
-                vh = jnp.where(low, v2, none) if half == 0 else jnp.where(low, none, v2)
-                st = dot_nt(kh, q2) - lse[h : h + 1, :]
-                pt = jnp.exp(jnp.concatenate([st[:last], jnp.where(valid, st[last:], NEG)], 0))
-                pd = pt * dot_nt(vh, do2)
-                dst = (pd - pt * colsum(pd)).astype(BF)
-                dvs.append(dot(pt.astype(BF), do2))
-                dks.append(dot(dst, q2))
-                dqs.append(dot(kt[half * 64 : half * 64 + 64], dst))
-            dq = jnp.concatenate(dqs, 0).T
-            dm_ref[g, :, p * 128 : (p + 1) * 128] = dq.astype(BF)
-            dm_ref[g, :, width + p * 128 : width + (p + 1) * 128] = jnp.where(low, dks[0], dks[1]).astype(BF)
-            dm_ref[g, :, 2 * width + p * 128 : 2 * width + (p + 1) * 128] = jnp.where(low, dvs[0], dvs[1]).astype(BF)
+    first = lax.broadcasted_iota(jnp.int32, (1, 128), 1)
+    mine = [jnp.where(first < 64, 1.0, 0.0).astype(BF), jnp.where(first < 64, 0.0, 1.0).astype(BF)]
+    def scores(g, p):
+        q2 = m_ref[g, :, p * 128 : (p + 1) * 128] * jnp.asarray(0.125, BF)
+        k2 = m_ref[g, :, width + p * 128 : width + (p + 1) * 128]
+        v2 = m_ref[g, :, 2 * width + p * 128 : 2 * width + (p + 1) * 128]
+        do2 = do_ref[g, :, p * 128 : (p + 1) * 128]
+        st = [dot_nt(k2 * mine[half], q2) for half in range(2)]
+        dp = [dot_nt(v2 * mine[half], do2) for half in range(2)]
+        return q2, k2, do2, st, dp
+
+    def weigh(g, p, got):
+        q2, k2, do2, st, dp = got
+        pts, dsts = [], []
+        for half in range(2):
+            h = 2 * p + half
+            sh = st[half] - aux_ref[g, h : h + 1, :]
+            pt = jnp.exp(jnp.concatenate([sh[:last], jnp.where(valid, sh[last:], NEG)], 0))
+            pd = pt * dp[half]
+            dsts.append((pd - pt * colsum(pd)).astype(BF))
+            pts.append(pt.astype(BF))
+        return q2, k2, do2, pts, dsts
+
+    def finish(g, p, got):
+        q2, k2, do2, pts, dsts = got
+        kt = (k2 * jnp.asarray(0.125, BF)).T
+        dvs = [dot(pts[half], do2) for half in range(2)]
+        dks = [dot(dsts[half], q2) for half in range(2)]
+        dqs = [dot(kt[half * 64 : half * 64 + 64], dsts[half]) for half in range(2)]
+        dm_ref[g, :, p * 128 : (p + 1) * 128] = jnp.concatenate(dqs, 0).T.astype(BF)
+        dm_ref[g, :, width + p * 128 : width + (p + 1) * 128] = jnp.where(low, dks[0], dks[1]).astype(BF)
+        dm_ref[g, :, 2 * width + p * 128 : 2 * width + (p + 1) * 128] = jnp.where(low, dvs[0], dvs[1]).astype(BF)
+
+    items = [(g, p) for g in range(images) for p in range(width // 128)]
+    ahead = scores(*items[0])
+    for t, item in enumerate(items):
+        got = weigh(*item, ahead)
+        if t + 1 < len(items):
+            ahead = scores(*items[t + 1])
+        finish(*item, got)
 
 
 def qkv_backward(seq, dx1_ref, dm_ref, xh_ref, aux_ref, vec, w, dx_ref, dwqkv, vec_s, dbm_s):
@@ -316,10 +328,10 @@
     vec_s[0:1, :] += colsum(dn1 * xhat)
     vec_s[1:2, :] += colsum(dn1)
     rstd = jnp.concatenate([to_column(aux_ref[g], 7) for g in range(images)], 0)
-    dx = flat(dx1_ref[...]) + norm_back(dn1 * vec[0:1, :], xhat, rstd)
+    dx = flat(dx1_ref[...]).astype(F32) + norm_back(dn1 * vec[0:1, :], xhat, rstd)
     dx = dx.reshape(images, rows, width)
     for g in range(images):
-        dx_ref[g] = dx[g, :seq]
+        dx_ref[g] = dx[g, :seq].astype(dx_ref.dtype)
 
 
 def small_slab(sm, vec_s, dbm_s, vec2, db1, part):
@@ -490,7 +502,7 @@
     quart = w_up.shape[2] // width
     return pl.pallas_call(
         pack_kernel,
-        out_shape=[sds((4, part, width), BF), sds((1 + 2 * quart, part, width), BF), sds((4 + 2 * quart, part, width), BF)],
+        out_shape=[sds((5 + 2 * quart, part, width), BF), sds((4 + 2 * quart, part, width), BF)],
         scratch_shapes=[pltpu.VMEM((128, 128), F32)],
         name="pack",
     )(*smalls, bias_up, w_qkv, w_proj, w_up, w_down)
@@ -516,7 +528,7 @@
     full = lambda r, c: pltpu.VMEM((r, c), F32)
     return call(
         functools.partial(top_kernel, seq), "top", per, [x, cot], [vec], wt,
-        [sds((images, seq, width), F32), sds((images, seq, width), F32)], slots(wt[0], wt[0].shape[1] + 1),
+        [sds((images, seq, width), F32), sds((images, seq, width), BF)], slots(wt[0], wt[0].shape[1] + 1),
         [full(n, width), full(n, width), cells(3 * width), cells(width), tall8, cells(width), cells(width), tall8,
          cells(ff), cells(ff), pltpu.VMEM((per, rows, width), F32), cells(width), cells(3 * width),
          full(width, 3 * width), full(width, width), full(width, ff), full(ff, width), full(8, width), full(8, width),
@@ -544,7 +556,7 @@
     rows, ff = a.shape[1:]
     return call(
         functools.partial(bm_kernel, seq), "bm", per, [gr, a, d, xh, rs, o], [vec], wm,
-        [sds((images, rows, width), F32), sds((images, rows, width), BF)],
+        [sds((images, rows, width), BF), sds((images, rows, width), BF)],
         slots(wm[0], wm[0].shape[1]) + [sds((8, width), F32), sds((1, ff), F32)],
         [pltpu.VMEM((per * rows, width), F32), pltpu.VMEM((width, width), F32), pltpu.VMEM((width, ff), F32),
          pltpu.VMEM((ff, width), F32)] + wscratch(wm[0]))
@@ -603,16 +615,16 @@
         return [x] + [swap(x, m) for m in masks[1:]]
 
     smalls = [norm1_gain, norm1_shift, query_bias, value_bias, proj_bias, norm2_gain, norm2_shift, fc2_bias]
-    a0, m0, l1 = run_pack(smalls, fc1_bias, qkv_weight, proj_weight, fc1_weight, fc2_weight)
-
-    a0 = jnp.stack(direct(a0))
-    m0 = direct(tie(m0, a0))
+    am, l1 = run_pack(smalls, fc1_bias, qkv_weight, proj_weight, fc1_weight, fc2_weight)
+
+    am = direct(am)
+    a0 = jnp.stack([y[:4] for y in am])
+    m0 = jnp.stack([y[4:] for y in am])
     a0x = swap(a0, 2)
+    l1 = direct(tie(l1, a0))
     a0 = jnp.concatenate([a0, a0x])
+    m0x = swap(tie(m0, a0x), 2)
     a0 = (a0, swap(a0, 1))
-    m0 = jnp.stack([m0[0]] + [tie(y, a0x) for y in m0[1:]])
-    m0x = swap(m0, 2)
-    l1 = direct(tie(l1, m0))
     mix, o, aux, xa, vec = run_fa(tie(tokens, m0, l1[0]), a0, ff, per)
     o, m0x, *l1 = group(o, m0x, *l1)
     m0 = jnp.concatenate([m0, m0x])
@@ -643,6 +655,23 @@
                 self.send = self.total(0, 1)[0].astype(BF)
             return self
 
+        def scatter(self):
+            self.rest = self.total(0, 1)[0]
+            masks = [0]
+            for b in upper:
+                masks = masks + [m ^ b for m in masks]
+            sends = [self.total(z, z + 1)[0].astype(BF) for z in range(1, len(masks))]
+            self.send = sends
+            self.flight = [swap(s, m) for s, m in zip(sends, masks[1:])]
+            return self
+
+        def collect(self):
+            total = self.rest
+            for f in self.flight:
+                total = total + f.astype(F32)
+            self.send = total.astype(BF)
+            return self
+
         def total(self, lo, hi):
             t = self.keep[lo:hi].astype(F32)
             for g in self.got:
@@ -670,25 +699,25 @@
 
     g1 = Sum(kp, sn).start().done().start()
     dx1, do, kp, sn, v2, db1 = run_bm(sent(grad, g1), act, der, xm, rs, o, vec, m0, per)
-    do = meet(do, g1)
-    g1.start()
+    do, sn, g1.flight = group(do, sn, g1.flight)
     gm0 = Sum(kp, sn).start()
-    tokens_grad, kp, sn = run_ba(seq, dx1, mix, sent(do, g1), xa, aux, vec, v2, db1, a0, per)
-    sn, g1.flight, gm0.flight = group(sn, g1.flight, gm0.flight)
+    g1.got.append(g1.flight)
+    g1.scatter()
+    gm0.done().start()
+    tokens_grad, kp, sn = run_ba(seq, dx1, mix, tie(do, *g1.send, gm0.send), xa, aux, vec, v2, db1, a0, per)
+    sn, gm0.flight, *g1.flight = group(sn, gm0.flight, *g1.flight)
     ga0 = Sum(kp, sn).start()
     gm0.done().start()
-    g1.done().start()
+    g1.collect()
     ga0.flight = tie(ga0.flight, gm0.send)
     ga0.done().start()
-    gm0.done().start()
-    g1.flight = tie(g1.flight, ga0.send)
-    g1.done()
+    g1.send = tie(g1.send, ga0.send)
     fin_1 = g1.replicas()
-    ga0.done().start()
     gm0.done().start()
     ga0.done().start()
     gm0.done()
     fin_m0 = gm0.replicas()
+    ga0.done().start()
     ga0.done()
     fin_a0 = ga0.replicas()
 

time: 271 us -> 248 us (0.915)
  Pallas kernels: 160 us -> 144 us
  waiting for transfers between devices: 48.8 us -> 60.1 us
  other arithmetic: 13.8 us -> 3.89 us
  starting transfers between devices: 36.8 us -> 30 us
    pallas_call x5, Pallas kernels: 156 us -> 139 us  [call(): pl.pallas_call(kern, grid=(blocked_in[0].shape[0] // per,), in_specs=in_s...]
    ppermute x27 -> x25, waiting for transfers between devices: 44.8 us -> 52.7 us  [swap(): return lax.ppermute(x, 'shard', xor_pairs(n, b))]
    ppermute x27 -> x25, starting transfers between devices: 32.9 us -> 26.4 us  [swap(): return lax.ppermute(x, 'shard', xor_pairs(n, b))]
    convert_element_type x9 -> x7, other arithmetic: 9.39 us -> 2.96 us  [done(): self.send = self.total(size // 2, size).astype(BF)]
    ppermute x3, waiting for transfers between devices: 3.97 us -> 7.44 us  [replicas(): other = lax.ppermute(mine, 'replica', xor_pairs(reps, b))]
    unnamed x48 -> x44, local copies, waits for them, and re-layouts: 8.66 us -> 5.94 us
  transfers between devices with their start and end apart: 30 -> 28, of which waited for: 18 -> 18; matrix products, arithmetic and copies ran while one was open for 4% -> 2% of each run, Pallas kernels for 32% -> 32%
where the time goes in v4:
time: 248 us; the launch traced here: 247 us
  Pallas kernels  144 us (58%)
  waiting for transfers between devices  60.1 us (24%)
  starting transfers between devices  30 us (12%)
  local copies, waits for them, and re-layouts  8.21 us (3%)
  other arithmetic  3.89 us (2%)
    pallas_call x5, Pallas kernels, call(): pl.pallas_call(kern, grid=(blocked_in[0].shape[0] // per,), in_specs=in_s...  139 us
    ppermute x25, waiting for transfers between devices, swap(): return lax.ppermute(x, 'shard', xor_pairs(n, b))  52.7 us
    ppermute x25, starting transfers between devices, swap(): return lax.ppermute(x, 'shard', xor_pairs(n, b))  26.4 us
    ppermute x3, waiting for transfers between devices, replicas(): other = lax.ppermute(mine, 'replica', xor_pairs(reps, b))  7.44 us
    unnamed x44, local copies, waits for them, and re-layouts  5.94 us
  transfers between devices with their start and end apart: 28, of which 18 were waited for; matrix products, arithmetic and copies ran while one was open for 2% of the time, Pallas kernels for 32%

profile of v4, /device:TPU:0, one launch (start us, length us, event | category | flops | bytes accessed | tf_op | source)
XLA Modules:
  0.0 247.1 jit_solution(18246657417686575256)
XLA Ops:
  0.7 2.0 pack.1
  2.6 5.0 %collective-permute-start.2 = (bf16[13,24,384]{2,1,0:T(8,128)(2,1)}, bf16[13,24,384]{2,1,0:T(8,128)(2,1)S(1)}, u32[]{:S(2)}, u32[]{:S(2)}) collective-permute-start(bf16[13,24,384]{2,1,0:T(8,128)(2,1)} %get-tuple-element.78), channel_id=1, source_target_pairs={{0,12},{1,13},{2,14},{3,15},{4,8},{5,9},{6,10},{7,11},{8,4},{9,5},... | collective-permute-start | bytes 718856 | tf_op jit(solution)/shard_map/ppermute | solution.py:609
  12.0 2.6 %collective-permute-done.2 = bf16[13,24,384]{2,1,0:T(8,128)(2,1)S(1)} collective-permute-done((bf16[13,24,384]{2,1,0:T(8,128)(2,1)}, bf16[13,24,384]{2,1,0:T(8,128)(2,1)S(1)}, u32[]{:S(2)}, u32[]{:S(2)}) %collective-permute-start.2) | collective-permute-done | bytes 239648 | tf_op jit(solution)/shard_map/ppermute | solution.py:609
  14.6 5.3 %collective-permute-done.1 = bf16[13,24,384]{2,1,0:T(8,128)(2,1)S(1)} collective-permute-done((bf16[13,24,384]{2,1,0:T(8,128)(2,1)}, bf16[13,24,384]{2,1,0:T(8,128)(2,1)S(1)}, u32[]{:S(2)}, u32[]{:S(2)}) %collective-permute-start.1) | collective-permute-done | bytes 239648 | tf_op jit(solution)/shard_map/ppermute | solution.py:609
  20.0 8.3 %collective-permute-done = bf16[13,24,384]{2,1,0:T(8,128)(2,1)S(1)} collective-permute-done((bf16[13,24,384]{2,1,0:T(8,128)(2,1)}, bf16[13,24,384]{2,1,0:T(8,128)(2,1)S(1)}, u32[]{:S(2)}, u32[]{:S(2)}) %collective-permute-start) | collective-permute-done | bytes 239648 | tf_op jit(solution)/shard_map/ppermute | solution.py:609
  28.3 2.5 %collective-permute-start.8 = (bf16[12,24,384]{2,1,0:T(8,128)(2,1)S(1)}, bf16[12,24,384]{2,1,0:T(8,128)(2,1)S(1)}, u32[]{:S(2)}, u32[]{:S(2)}) collective-permute-start(bf16[12,24,384]{2,1,0:T(8,128)(2,1)S(1)} %copy-done.3), channel_id=1, source_target_pairs={{0,12},{1,13},{2,14},{3,15},{4,8},{5,9},{6,10},{7,11},{8,4},{9,5},... | collective-permute-start | bytes 663560 | tf_op jit(solution)/shard_map/ppermute | solution.py:609
  30.9 1.9 collective-permute-start.6
  34.5 5.5 %collective-permute-done.3 = bf16[4,4,24,384]{3,2,1,0:T(8,128)(2,1)S(1)} collective-permute-done((bf16[4,4,24,384]{3,2,1,0:T(8,128)(2,1)S(1)}, bf16[4,4,24,384]{3,2,1,0:T(8,128)(2,1)S(1)}, u32[]{:S(2)}, u32[]{:S(2)}) %collective-permute-start.3) | collective-permute-done | bytes 294944 | tf_op jit(solution)/shard_map/ppermute | solution.py:609
  43.0 13.6 %fa.1 = (bf16[10,208,1152]{2,1,0:T(8,128)(2,1)}, bf16[10,208,384]{2,1,0:T(8,128)(2,1)}, f32[10,8,208]{2,1,0:T(8,128)}, bf16[10,208,384]{2,1,0:T(8,128)(2,1)}, f32[2,16,384]{2,1,0:T(8,128)}) custom-call(bf16[10,197,384]{2,1,0:T(8,128)(2,1)} %x_ref.2, bf16[8,4,24,384]{3,2,1,0:T(8,128)(2,1)} %copy-done.12, bf16[8,4,24,384]{3,2,1,0:T(8,128)(2,1)} %copy-done.15), custom_call_target="tpu_custom_call" | custom-call | flops 14949999616 | tf_op jit(solution)/shard_map/fa/pallas_call | solution.py:483
  62.2 17.6 %fm.1 = (f32[10,197,384]{2,1,0:T(8,128)}, bf16[10,208,1536]{2,1,0:T(8,128)(2,1)}, bf16[10,208,1536]{2,1,0:T(8,128)(2,1)}, bf16[10,208,384]{2,1,0:T(8,128)(2,1)}, f32[10,8,208]{2,1,0:T(8,128)}) custom-call(bf16[10,197,384]{2,1,0:T(8,128)(2,1)} %x_ref.2, bf16[10,208,384]{2,1,0:T(8,128)(2,1)} %get-tuple-element.84.o_ref, ...), custom_call_target="tpu_custom_call" | custom-call | flops 20700000256 | tf_op jit(solution)/shard_map/fm/pallas_call | solution.py:483
  80.3 3.7 %collective-permute-done.11.other = bf16[8,12,24,384]{3,2,1,0:T(8,128)(2,1)S(1)} collective-permute-done((bf16[8,12,24,384]{3,2,1,0:T(8,128)(2,1)S(1)}, bf16[8,12,24,384]{3,2,1,0:T(8,128)(2,1)S(1)}, u32[]{:S(2)}, u32[]{:S(2)}) %collective-permute-start.11) | collective-permute-done | bytes 1769504 | tf_op jit(solution)/shard_map/ppermute | solution.py:609
  85.2 60.8 %top.1 = (f32[10,197,384]{2,1,0:T(8,128)}, bf16[10,197,384]{2,1,0:T(8,128)(2,1)}, bf16[8,13,24,384]{3,2,1,0:T(8,128)(2,1)}, bf16[8,13,24,384]{3,2,1,0:T(8,128)(2,1)}) custom-call(f32[10,197,384]{2,1,0:T(8,128)} %get-tuple-element.62.x_ref, bf16[10,197,384]{2,1,0:T(8,128)(2,1)} %cot_ref.1, f32[2,16,384]{2,1,0:T(8,128)} %get-tuple-element.85.vec_ref, ...), custom_call_target="tpu_custom_call" | custom-call | flops 80499998720 | tf_op jit(solution)/shard_map/top/pallas_call | solution.py:483
  146.3 4.0 %collective-permute-done.12 = bf16[8,13,24,384]{3,2,1,0:T(8,128)(2,1)S(1)} collective-permute-done((bf16[8,13,24,384]{3,2,1,0:T(8,128)(2,1)}, bf16[8,13,24,384]{3,2,1,0:T(8,128)(2,1)S(1)}, u32[]{:S(2)}, u32[]{:S(2)}) %collective-permute-start.12) | collective-permute-done | bytes 1916960 | tf_op jit(solution)/shard_map/ppermute | solution.py:609
  153.2 26.0 %bm.1 = (bf16[10,208,384]{2,1,0:T(8,128)(2,1)}, bf16[10,208,384]{2,1,0:T(8,128)(2,1)}, bf16[8,9,24,384]{3,2,1,0:T(8,128)(2,1)}, bf16[8,9,24,384]{3,2,1,0:T(8,128...) custom-call(bf16[10,197,384]{2,1,0:T(8,128)(2,1)} %get-tuple-element.99.gr_ref, ...), custom_call_target="tpu_custom_call" | custom-call | flops 29899999232 | tf_op jit(solution)/shard_map/bm/pallas_call | solution.py:483
  179.6 2.3 collective-permute-start.18
  181.9 2.1 collective-permute-start.16
  184.8 21.3 %ba.1 = (f32[10,197,384]{2,1,0:T(8,128)}, bf16[8,4,24,384]{3,2,1,0:T(8,128)(2,1)}, bf16[8,4,24,384]{3,2,1,0:T(8,128)(2,1)}) custom-call(bf16[10,208,384]{2,1,0:T(8,128)(2,1)} %get-tuple-element.104.dx1_ref, bf16[10,208,1152]{2,1,0:T(8,128)(2,1)} %get-tuple-element.105.m_ref, bf16[10,208,384]{2,1,0:T(8,128)(2,1)} %get-tuple-element.112.do_ref, ...), custom_call_target="tpu_custom_call" | custom-call | flops 32199999488 | tf_op jit(solution)/shard_map/ba/pallas_call | solution.py:483
  206.4 2.1 collective-permute-done.19
  211.3 7.3 %collective-permute-done.20 = bf16[4,4,24,384]{3,2,1,0:T(8,128)(2,1)S(1)} collective-permute-done((bf16[4,4,24,384]{3,2,1,0:T(8,128)(2,1)S(1)}, bf16[4,4,24,384]{3,2,1,0:T(8,128)(2,1)S(1)}, u32[]{:S(2)}, u32[]{:S(2)}) %collective-permute-start.20) | collective-permute-done | bytes 294944 | tf_op jit(solution)/shard_map/ppermute | solution.py:609
  221.9 2.6 %collective-permute-done.21 = bf16[2,4,24,384]{3,2,1,0:T(8,128)(2,1)S(1)} collective-permute-done((bf16[2,4,24,384]{3,2,1,0:T(8,128)(2,1)S(1)}, bf16[2,4,24,384]{3,2,1,0:T(8,128)(2,1)S(1)}, u32[]{:S(2)}, u32[]{:S(2)}) %collective-permute-start.21) | collective-permute-done | bytes 147488 | tf_op jit(solution)/shard_map/ppermute | solution.py:609
  226.2 6.6 %collective-permute-done.25 = bf16[1,9,24,384]{3,2,1,0:T(8,128)(2,1)S(1)} collective-permute-done((bf16[1,9,24,384]{3,2,1,0:T(8,128)(2,1)S(1)}, bf16[1,9,24,384]{3,2,1,0:T(8,128)(2,1)S(1)}, u32[]{:S(2)}, u32[]{:S(2)}) %collective-permute-start.25) | collective-permute-done | bytes 165920 | tf_op jit(solution)/shard_map/ppermute | solution.py:609
  236.6 3.5 %collective-permute-done.26.refs_3_ = bf16[9,24,384]{2,1,0:T(8,128)(2,1)S(1)} collective-permute-done((bf16[9,24,384]{2,1,0:T(8,128)(2,1)S(1)}, bf16[9,24,384]{2,1,0:T(8,128)(2,1)S(1)}, u32[]{:S(2)}, u32[]{:S(2)}) %collective-permute-start.26) | collective-permute-done | bytes 165920 | tf_op jit(solution)/shard_map/ppermute | solution.py:684
  240.1 3.2 %collective-permute-done.27.refs_5_ = bf16[13,24,384]{2,1,0:T(8,128)(2,1)S(1)} collective-permute-done((bf16[13,24,384]{2,1,0:T(8,128)(2,1)S(1)}, bf16[13,24,384]{2,1,0:T(8,128)(2,1)S(1)}, u32[]{:S(2)}, u32[]{:S(2)}) %collective-permute-start.27) | collective-permute-done | bytes 239648 | tf_op jit(solution)/shard_map/ppermute | solution.py:684
  244.7 2.2 finish.1
  (108 shorter events, 33.8 us)
Async XLA Ops:
  2.6 12.0 %collective-permute-start.2 = (bf16[13,24,384]{2,1,0:T(8,128)(2,1)}, bf16[13,24,384]{2,1,0:T(8,128)(2,1)S(1)}, u32[]{:S(2)}, u32[]{:S(2)}) collective-permute-start(bf16[13,24,384]{2,1,0:T(8,128)(2,1)} %get-tuple-element.78), channel_id=1, source_target_pairs={{0,12},{1,13},{2,14},{3,15},{4,8},{5,9},{6,10},{7,11},{8,4},{9,5},... | collective-permute-start | bytes 718856 | tf_op jit(solution)/shard_map/ppermute | solution.py:609
  7.7 12.3 %collective-permute-start.1 = (bf16[13,24,384]{2,1,0:T(8,128)(2,1)}, bf16[13,24,384]{2,1,0:T(8,128)(2,1)S(1)}, u32[]{:S(2)}, u32[]{:S(2)}) collective-permute-start(bf16[13,24,384]{2,1,0:T(8,128)(2,1)} %get-tuple-element.78), channel_id=1, source_target_pairs={{0,4},{1,5},{2,6},{3,7},{4,0},{5,1},{6,2},{7,3},{8,12},{9,13},{10,... | collective-permute-start | bytes 718856 | tf_op jit(solution)/shard_map/ppermute | solution.py:609
  7.7 20.6 %collective-permute-start = (bf16[13,24,384]{2,1,0:T(8,128)(2,1)}, bf16[13,24,384]{2,1,0:T(8,128)(2,1)S(1)}, u32[]{:S(2)}, u32[]{:S(2)}) collective-permute-start(bf16[13,24,384]{2,1,0:T(8,128)(2,1)} %get-tuple-element.78), channel_id=1, source_target_pairs={{0,8},{1,9},{2,10},{3,11},{4,12},{5,13},{6,14},{7,15},{8,0},{9,1},... | collective-permute-start | bytes 718856 | tf_op jit(solution)/shard_map/ppermute | solution.py:609
  28.3 28.3 %collective-permute-start.8 = (bf16[12,24,384]{2,1,0:T(8,128)(2,1)S(1)}, bf16[12,24,384]{2,1,0:T(8,128)(2,1)S(1)}, u32[]{:S(2)}, u32[]{:S(2)}) collective-permute-start(bf16[12,24,384]{2,1,0:T(8,128)(2,1)S(1)} %copy-done.3), channel_id=1, source_target_pairs={{0,12},{1,13},{2,14},{3,15},{4,8},{5,9},{6,10},{7,11},{8,4},{9,5},... | collective-permute-start | bytes 663560 | tf_op jit(solution)/shard_map/ppermute | solution.py:609
  30.9 25.8 %collective-permute-start.7 = (bf16[12,24,384]{2,1,0:T(8,128)(2,1)S(1)}, bf16[12,24,384]{2,1,0:T(8,128)(2,1)S(1)}, u32[]{:S(2)}, u32[]{:S(2)}) collective-permute-start(bf16[12,24,384]{2,1,0:T(8,128)(2,1)S(1)} %copy-done.3), channel_id=1, source_target_pairs={{0,4},{1,5},{2,6},{3,7},{4,0},{5,1},{6,2},{7,3},{8,12},{9,13},{10,... | collective-permute-start | bytes 663560 | tf_op jit(solution)/shard_map/ppermute | solution.py:609
  30.9 25.8 %collective-permute-start.6 = (bf16[12,24,384]{2,1,0:T(8,128)(2,1)S(1)}, bf16[12,24,384]{2,1,0:T(8,128)(2,1)S(1)}, u32[]{:S(2)}, u32[]{:S(2)}) collective-permute-start(bf16[12,24,384]{2,1,0:T(8,128)(2,1)S(1)} %copy-done.3), channel_id=1, source_target_pairs={{0,8},{1,9},{2,10},{3,11},{4,12},{5,13},{6,14},{7,15},{8,0},{9,1},... | collective-permute-start | bytes 663560 | tf_op jit(solution)/shard_map/ppermute | solution.py:609
  32.8 7.2 %collective-permute-start.3 = (bf16[4,4,24,384]{3,2,1,0:T(8,128)(2,1)S(1)}, bf16[4,4,24,384]{3,2,1,0:T(8,128)(2,1)S(1)}, u32[]{:S(2)}, u32[]{:S(2)}) collective-permute-start(bf16[4,4,24,384]{3,2,1,0:T(8,128)(2,1)S(1)} %pad_maximum_fusion.2), channel_id=1, source_target_pairs={{0,2},{1,3},{2,0},{3,1},{4,6},{5,7},{6,4},{7,5},{8,10},{9,11},{10,... | collective-permute-start | bytes 884744 | tf_op jit(solution)/shard_map/ppermute | solution.py:609
  40.3 17.4 %collective-permute-start.5 = (bf16[4,9,24,384]{3,2,1,0:T(8,128)(2,1)S(1)}, bf16[4,9,24,384]{3,2,1,0:T(8,128)(2,1)S(1)}, u32[]{:S(2)}, u32[]{:S(2)}) collective-permute-start(bf16[4,9,24,384]{3,2,1,0:T(8,128)(2,1)S(1)} %pad_maximum_fusion.1), channel_id=1, source_target_pairs={{0,2},{1,3},{2,0},{3,1},{4,6},{5,7},{6,4},{7,5},{8,10},{9,11},{10,... | collective-permute-start | bytes 1990664 | tf_op jit(solution)/shard_map/ppermute | solution.py:609
  58.0 22.1 %collective-permute-start.10 = (bf16[4,12,24,384]{3,2,1,0:T(8,128)(2,1)S(1)}, bf16[4,12,24,384]{3,2,1,0:T(8,128)(2,1)S(1)}, u32[]{:S(2)}, u32[]{:S(2)}) collective-permute-start(bf16[4,12,24,384]{3,2,1,0:T(8,128)(2,1)S(1)} %pad_maximum_fusion), channel_id=1, source_target_pairs={{0,2},{1,3},{2,0},{3,1},{4,6},{5,7},{6,4},{7,5},{8,10},{9,11},{10,... | collective-permute-start | bytes 2654216 | tf_op jit(solution)/shard_map/ppermute | solution.py:609
  146.1 4.2 %collective-permute-start.12 = (bf16[8,13,24,384]{3,2,1,0:T(8,128)(2,1)}, bf16[8,13,24,384]{3,2,1,0:T(8,128)(2,1)S(1)}, u32[]{:S(2)}, u32[]{:S(2)}) collective-permute-start(bf16[8,13,24,384]{3,2,1,0:T(8,128)(2,1)} %get-tuple-element.98), channel_id=1, source_target_pairs={{0,1},{1,0},{2,3},{3,2},{4,5},{5,4},{6,7},{7,6},{8,9},{9,8},{10,11... | collective-permute-start | bytes 5750792 | tf_op jit(solution)/shard_map/ppermute | solution.py:609
  151.7 27.6 %collective-permute-start.13 = (bf16[4,13,24,384]{3,2,1,0:T(8,128)(2,1)S(1)}, bf16[4,13,24,384]{3,2,1,0:T(8,128)(2,1)S(1)}, u32[]{:S(2)}, u32[]{:S(2)}) collective-permute-start(bf16[4,13,24,384]{3,2,1,0:T(8,128)(2,1)S(1)} %add_convert_fusion), channel_id=1, source_target_pairs={{0,2},{1,3},{2,0},{3,1},{4,6},{5,7},{6,4},{7,5},{8,10},{9,11},{10,... | collective-permute-start | bytes 2875400 | tf_op jit(solution)/shard_map/ppermute | solution.py:609
  179.2 4.8 %collective-permute-start.14 = (bf16[8,9,24,384]{3,2,1,0:T(8,128)(2,1)}, bf16[8,9,24,384]{3,2,1,0:T(8,128)(2,1)S(1)}, u32[]{:S(2)}, u32[]{:S(2)}) collective-permute-start(bf16[8,9,24,384]{3,2,1,0:T(8,128)(2,1)} %get-tuple-element.111), channel_id=1, source_target_pairs={{0,1},{1,0},{2,3},{3,2},{4,5},{5,4},{6,7},{7,6},{8,9},{9,8},{10,11... | collective-permute-start | bytes 3981320 | tf_op jit(solution)/shard_map/ppermute | solution.py:609
  179.6 26.5 %collective-permute-start.18 = (bf16[13,24,384]{2,1,0:T(8,128)(2,1)S(1)}, bf16[13,24,384]{2,1,0:T(8,128)(2,1)S(1)}, u32[]{:S(2)}, u32[]{:S(2)}) collective-permute-start(bf16[13,24,384]{2,1,0:T(8,128)(2,1)S(1)} %get-tuple-element.140), channel_id=1, source_target_pairs={{0,12},{1,13},{2,14},{3,15},{4,8},{5,9},{6,10},{7,11},{8,4},{9,5},... | collective-permute-start | bytes 718856 | tf_op jit(solution)/shard_map/ppermute | solution.py:609
  181.9 24.2 %collective-permute-start.17 = (bf16[13,24,384]{2,1,0:T(8,128)(2,1)S(1)}, bf16[13,24,384]{2,1,0:T(8,128)(2,1)S(1)}, u32[]{:S(2)}, u32[]{:S(2)}) collective-permute-start(bf16[13,24,384]{2,1,0:T(8,128)(2,1)S(1)} %get-tuple-element.141), channel_id=1, source_target_pairs={{0,4},{1,5},{2,6},{3,7},{4,0},{5,1},{6,2},{7,3},{8,12},{9,13},{10,... | collective-permute-start | bytes 718856 | tf_op jit(solution)/shard_map/ppermute | solution.py:609
  181.9 24.2 %collective-permute-start.16 = (bf16[13,24,384]{2,1,0:T(8,128)(2,1)S(1)}, bf16[13,24,384]{2,1,0:T(8,128)(2,1)S(1)}, u32[]{:S(2)}, u32[]{:S(2)}) collective-permute-start(bf16[13,24,384]{2,1,0:T(8,128)(2,1)S(1)} %get-tuple-element.142), channel_id=1, source_target_pairs={{0,8},{1,9},{2,10},{3,11},{4,12},{5,13},{6,14},{7,15},{8,0},{9,1},... | collective-permute-start | bytes 718856 | tf_op jit(solution)/shard_map/ppermute | solution.py:609
  184.2 21.9 %collective-permute-start.15 = (bf16[4,9,24,384]{3,2,1,0:T(8,128)(2,1)S(1)}, bf16[4,9,24,384]{3,2,1,0:T(8,128)(2,1)S(1)}, u32[]{:S(2)}, u32[]{:S(2)}) collective-permute-start(bf16[4,9,24,384]{3,2,1,0:T(8,128)(2,1)S(1)} %add_convert_fusion.1), channel_id=1, source_target_pairs={{0,2},{1,3},{2,0},{3,1},{4,6},{5,7},{6,4},{7,5},{8,10},{9,11},{10,... | collective-permute-start | bytes 1990664 | tf_op jit(solution)/shard_map/ppermute | solution.py:609
  209.5 9.1 %collective-permute-start.20 = (bf16[4,4,24,384]{3,2,1,0:T(8,128)(2,1)S(1)}, bf16[4,4,24,384]{3,2,1,0:T(8,128)(2,1)S(1)}, u32[]{:S(2)}, u32[]{:S(2)}) collective-permute-start(bf16[4,4,24,384]{3,2,1,0:T(8,128)(2,1)S(1)} %add_convert_fusion.3), channel_id=1, source_target_pairs={{0,2},{1,3},{2,0},{3,1},{4,6},{5,7},{6,4},{7,5},{8,10},{9,11},{10,... | collective-permute-start | bytes 884744 | tf_op jit(solution)/shard_map/ppermute | solution.py:609
  211.1 9.6 %collective-permute-start.24 = (bf16[2,9,24,384]{3,2,1,0:T(8,128)(2,1)S(1)}, bf16[2,9,24,384]{3,2,1,0:T(8,128)(2,1)S(1)}, u32[]{:S(2)}, u32[]{:S(2)}) collective-permute-start(bf16[2,9,24,384]{3,2,1,0:T(8,128)(2,1)S(1)} %add_convert_fusion.2), channel_id=1, source_target_pairs={{0,4},{1,5},{2,6},{3,7},{4,0},{5,1},{6,2},{7,3},{8,12},{9,13},{10,... | collective-permute-start | bytes 995336 | tf_op jit(solution)/shard_map/ppermute | solution.py:609
  218.7 5.8 %collective-permute-start.21 = (bf16[2,4,24,384]{3,2,1,0:T(8,128)(2,1)S(1)}, bf16[2,4,24,384]{3,2,1,0:T(8,128)(2,1)S(1)}, u32[]{:S(2)}, u32[]{:S(2)}) collective-permute-start(bf16[2,4,24,384]{3,2,1,0:T(8,128)(2,1)S(1)} %add_convert_fusion.9), channel_id=1, source_target_pairs={{0,4},{1,5},{2,6},{3,7},{4,0},{5,1},{6,2},{7,3},{8,12},{9,13},{10,... | collective-permute-start | bytes 442376 | tf_op jit(solution)/shard_map/ppermute | solution.py:609
  220.7 12.0 %collective-permute-start.25 = (bf16[1,9,24,384]{3,2,1,0:T(8,128)(2,1)S(1)}, bf16[1,9,24,384]{3,2,1,0:T(8,128)(2,1)S(1)}, u32[]{:S(2)}, u32[]{:S(2)}) collective-permute-start(bf16[1,9,24,384]{3,2,1,0:T(8,128)(2,1)S(1)} %add_convert_fusion.8), channel_id=1, source_target_pairs={{0,8},{1,9},{2,10},{3,11},{4,12},{5,13},{6,14},{7,15},{8,0},{9,1},... | collective-permute-start | bytes 497672 | tf_op jit(solution)/shard_map/ppermute | solution.py:609
  224.5 10.4 %collective-permute-start.22 = (bf16[1,4,24,384]{3,2,1,0:T(8,128)(2,1)S(1)}, bf16[1,4,24,384]{3,2,1,0:T(8,128)(2,1)S(1)}, u32[]{:S(2)}, u32[]{:S(2)}) collective-permute-start(bf16[1,4,24,384]{3,2,1,0:T(8,128)(2,1)S(1)} %add_convert_fusion.11), channel_id=1, source_target_pairs={{0,8},{1,9},{2,10},{3,11},{4,12},{5,13},{6,14},{7,15},{8,0},{9,1},... | collective-permute-start | bytes 221192 | tf_op jit(solution)/shard_map/ppermute | solution.py:609
  232.9 7.2 %collective-permute-start.26 = (bf16[9,24,384]{2,1,0:T(8,128)(2,1)S(1)}, bf16[9,24,384]{2,1,0:T(8,128)(2,1)S(1)}, u32[]{:S(2)}, u32[]{:S(2)}) collective-permute-start(bf16[9,24,384]{2,1,0:T(8,128)(2,1)S(1)} %fusion.6.refs_2_), channel_id=1, source_target_pairs={{0,16},{16,0},{1,17},{17,1},{2,18},{18,2},{3,19},{19,3},{4,20},{20... | collective-permute-start | bytes 497672 | tf_op jit(solution)/shard_map/ppermute | solution.py:684
  234.4 8.8 %collective-permute-start.27 = (bf16[13,24,384]{2,1,0:T(8,128)(2,1)S(1)}, bf16[13,24,384]{2,1,0:T(8,128)(2,1)S(1)}, u32[]{:S(2)}, u32[]{:S(2)}) collective-permute-start(bf16[13,24,384]{2,1,0:T(8,128)(2,1)S(1)} %fusion.2.refs_4_), channel_id=1, source_target_pairs={{0,16},{16,0},{1,17},{17,1},{2,18},{18,2},{3,19},{19,3},{4,20},{20... | collective-permute-start | bytes 718856 | tf_op jit(solution)/shard_map/ppermute | solution.py:684
  235.0 9.0 %collective-permute-start.23 = (bf16[4,24,384]{2,1,0:T(8,128)(2,1)S(1)}, bf16[4,24,384]{2,1,0:T(8,128)(2,1)S(1)}, u32[]{:S(2)}, u32[]{:S(2)}) collective-permute-start(bf16[4,24,384]{2,1,0:T(8,128)(2,1)S(1)} %fusion.7.refs_0_), channel_id=1, source_target_pairs={{0,16},{16,0},{1,17},{17,1},{2,18},{18,2},{3,19},{19,3},{4,20},{20... | collective-permute-start | bytes 221192 | tf_op jit(solution)/shard_map/ppermute | solution.py:684
  (20 other events, 140.5 us)

commit v5 on v4

--- a/solution.py
+++ b/solution.py
@@ -392,18 +392,42 @@
         store_slots(keep, send, mlp_pieces(dwp, dw1, dw2, w.shape[2]))
 
 
-def ba_kernel(seq, dx1_ref, m_ref, do_ref, xh_ref, aux_ref, vec_ref, vec2, db1, own, other,
-              dx_ref, keep, send, dm_s, dwqkv, vec_s, dbm_s, w, sems, sm):
-    first_step(lambda: start_weights(own, other, w, sems), lambda: zero(dwqkv, vec_s, dbm_s))
-    attn_backward(seq, m_ref, do_ref, aux_ref, dm_s)
+def ba_kernel(seq, m_ref, do_ref, xh_ref, aux_ref, vec_ref, vec2, db1, own, other,
+              dm_ref, keep, send, dwqkv, dbm_s, w, sems, sm):
+    first_step(lambda: start_weights(own, other, w, sems), lambda: zero(dwqkv, dbm_s))
+    attn_backward(seq, m_ref, do_ref, aux_ref, dm_ref)
+    dm = flat(dm_ref[...])
+    dbm_s[...] += colsum(dm.astype(F32))
+    dwqkv[...] += dot_tn(flat(xh_ref[...]), dm)
     first_step(lambda: wait_weights(own, other, w, sems))
-    qkv_backward(seq, dx1_ref, dm_s, xh_ref, aux_ref, vec_ref.at[0], w, dx_ref, dwqkv, vec_s, dbm_s)
 
     @last_step
     def _():
         part = w.shape[2]
-        small_slab(sm, vec_s, dbm_s, vec2, db1, part)
+        width = sm.shape[0]
+        prod = dwqkv[...]
+        full = slabs(w, 0, 3).astype(F32)
+        gain = jnp.sum(full * prod, 1, keepdims=True)
+        shift = jnp.sum(full * dbm_s[...], 1, keepdims=True)
+        params = vec_ref[0, 0:8, :]
+        dwqkv[...] = to_column(params, 0) * prod + to_column(params, 1) * dbm_s[...]
+        small_slab(sm, jnp.zeros((8, width), F32), dbm_s, vec2, db1, part)
+        sm[:, 0:1] = gain
+        sm[:, 1:2] = shift
         store_slots(keep, send, attn_pieces(dwqkv, sm, part))
+
+
+def bx_kernel(seq, dx1_ref, dm_ref, xh_ref, aux_ref, vec_ref, own, other, *rest):
+    dx_ref, w, sems = rest[-3:]
+    vec = vec_ref.at[0]
+    images, rows, width = xh_ref.shape
+    first_step(lambda: start_weights(own, other, w, sems), lambda: wait_weights(own, other, w, sems))
+    dn1 = dot_nt(flat(dm_ref[...]), slabs(w, 0, 3))
+    rstd = jnp.concatenate([to_column(aux_ref[g], 7) for g in range(images)], 0)
+    dx = flat(dx1_ref[...]).astype(F32) + norm_back(dn1 * vec[0:1, :], flat(xh_ref[...]).astype(F32), rstd)
+    dx = dx.reshape(images, rows, width)
+    for g in range(images):
+        dx_ref[g] = dx[g, :seq]
 
 
 def top_kernel(seq, x_ref, cot_ref, vec_ref, own, other, out_ref, dx_ref, keep, send,
@@ -474,7 +498,7 @@
     return jax.ShapeDtypeStruct(shape, dt)
 
 
-COST = {"fa": 13, "fm": 18, "bm": 26, "ba": 28, "top": 70}
+COST = {"fa": 13, "fm": 18, "bm": 26, "ba": 20, "top": 70}
 
 
 def call(kern, name, per, blocked_in, whole_in, any_in, blocked_out, whole_out, scratch):
@@ -562,13 +586,37 @@
          pltpu.VMEM((ff, width), F32)] + wscratch(wm[0]))
 
 
-def run_ba(seq, dx1, m, do, xh, aux, vec, vec2, db1, wa, per):
+def run_ba(seq, m, do, xh, aux, vec, vec2, db1, wa, per):
+    images, rows, width = do.shape
+    return call(
+        functools.partial(ba_kernel, seq), "ba", per, [m, do, xh, aux], [vec, vec2, db1], wa,
+        [sds((images, rows, 3 * width), BF)], slots(wa[0], 4),
+        [pltpu.VMEM((width, 3 * width), F32), pltpu.VMEM((1, 3 * width), F32)]
+        + wscratch(wa[0]) + [pltpu.VMEM((width, width), F32)])
+
+
+def run_bx(seq, dx1, dm, xh, aux, vec, wa, per, first, count, prev=None):
     images, rows, width = dx1.shape
-    return call(
-        functools.partial(ba_kernel, seq), "ba", per, [dx1, m, do, xh, aux], [vec, vec2, db1], wa,
-        [sds((images, seq, width), F32)], slots(wa[0], 4),
-        [pltpu.VMEM((per, rows, 3 * width), BF), pltpu.VMEM((width, 3 * width), F32), pltpu.VMEM((8, width), F32),
-         pltpu.VMEM((1, 3 * width), F32)] + wscratch(wa[0]) + [pltpu.VMEM((width, width), F32)])
+    base = first // per
+
+    def at(shape):
+        nd = len(shape)
+        return pl.BlockSpec((per,) + shape[1:], lambda i: (i + base,) + (0,) * (nd - 1))
+
+    more = [] if prev is None else [prev]
+    out = sds((images, seq, width), F32)
+    return pl.pallas_call(
+        functools.partial(bx_kernel, seq),
+        grid=(count // per,),
+        in_specs=[at(a.shape) for a in (dx1, dm, xh, aux)] + [whole(vec)] + [anyspec() for _ in [*wa, *more]],
+        out_specs=at(out.shape),
+        out_shape=out,
+        input_output_aliases={7: 0} if more else {},
+        scratch_shapes=wscratch(wa[0]),
+        compiler_params=pltpu.CompilerParams(vmem_limit_bytes=VMEM_LIMIT),
+        name="bx",
+        cost_estimate=pl.CostEstimate(flops=count * 1_150_000_000, bytes_accessed=0, transcendentals=0),
+    )(dx1, dm, xh, aux, vec, *wa, *more)
 
 
 def run_finish(a0, m0, l1, ff):
@@ -704,20 +752,24 @@
     g1.got.append(g1.flight)
     g1.scatter()
     gm0.done().start()
-    tokens_grad, kp, sn = run_ba(seq, dx1, mix, tie(do, *g1.send, gm0.send), xa, aux, vec, v2, db1, a0, per)
+    dm, kp, sn = run_ba(seq, mix, tie(do, *g1.send, gm0.send), xa, aux, vec, v2, db1, a0, per)
     sn, gm0.flight, *g1.flight = group(sn, gm0.flight, *g1.flight)
     ga0 = Sum(kp, sn).start()
     gm0.done().start()
     g1.collect()
     ga0.flight = tie(ga0.flight, gm0.send)
     ga0.done().start()
-    g1.send = tie(g1.send, ga0.send)
+    first = images // (2 * per) * per
+    part_grad = run_bx(seq, dx1, tie(dm, ga0.send, gm0.send), xa, aux, vec, a0, per, 0, first)
+    part_grad, ga0.flight, gm0.flight, g1.send = group(part_grad, ga0.flight, gm0.flight, g1.send)
+    ga0.done().start()
+    gm0.done().start()
     fin_1 = g1.replicas()
-    gm0.done().start()
+    tokens_grad = run_bx(seq, dx1, dm, xa, aux, vec, a0, per, first, images - first, tie(part_grad, ga0.send, gm0.send))
+    tokens_grad, ga0.flight, gm0.flight = group(tokens_grad, ga0.flight, gm0.flight)
     ga0.done().start()
     gm0.done()
     fin_m0 = gm0.replicas()
-    ga0.done().start()
     ga0.done()
     fin_a0 = ga0.replicas()
 

time: 248 us -> 242 us (0.976)
  waiting for transfers between devices: 60.1 us -> 41.1 us
  Pallas kernels: 144 us -> 153 us
    ppermute x25, waiting for transfers between devices: 52.7 us -> 38.7 us  [swap(): return lax.ppermute(x, 'shard', xor_pairs(n, b))]
    pallas_call x0 -> x2, Pallas kernels: none -> 13 us  [run_bx(): pl.pallas_call(functools.partial(bx_kernel, seq), grid=(count // per,), i...]
    ppermute x3, waiting for transfers between devices: 7.44 us -> 2.41 us  [replicas(): other = lax.ppermute(mine, 'replica', xor_pairs(reps, b))]
    pallas_call x5, Pallas kernels: 139 us -> 136 us  [call(): pl.pallas_call(kern, grid=(blocked_in[0].shape[0] // per,), in_specs=in_s...]
    unnamed x44 -> x50, local copies, waits for them, and re-layouts: 5.94 us -> 7.31 us
  transfers between devices with their start and end apart: 28 -> 28, of which waited for: 18 -> 16; matrix products, arithmetic and copies ran while one was open for 2% -> 3% of each run, Pallas kernels for 32% -> 36%
where the time goes in v5:
time: 242 us; the launch traced here: 241 us
  Pallas kernels  153 us (63%)
  waiting for transfers between devices  41.1 us (17%)
  starting transfers between devices  31.7 us (13%)
  local copies, waits for them, and re-layouts  9.59 us (4%)
  other arithmetic  4.86 us (2%)
    pallas_call x5, Pallas kernels, call(): pl.pallas_call(kern, grid=(blocked_in[0].shape[0] // per,), in_specs=in_s...  136 us
    ppermute x25, waiting for transfers between devices, swap(): return lax.ppermute(x, 'shard', xor_pairs(n, b))  38.7 us
    ppermute x25, starting transfers between devices, swap(): return lax.ppermute(x, 'shard', xor_pairs(n, b))  27.6 us
    pallas_call x2, Pallas kernels, run_bx(): pl.pallas_call(functools.partial(bx_kernel, seq), grid=(count // per,), i...  13 us
    unnamed x50, local copies, waits for them, and re-layouts  7.31 us
  transfers between devices with their start and end apart: 28, of which 16 were waited for; matrix products, arithmetic and copies ran while one was open for 3% of the time, Pallas kernels for 36%

profile of v5, /device:TPU:0, one launch (start us, length us, event | category | flops | bytes accessed | tf_op | source)
XLA Modules:
  0.0 241.5 jit_solution(11110357389260500855)
XLA Ops:
  0.7 2.0 pack.1
  2.6 5.0 %collective-permute-start.2 = (bf16[13,24,384]{2,1,0:T(8,128)(2,1)}, bf16[13,24,384]{2,1,0:T(8,128)(2,1)S(1)}, u32[]{:S(2)}, u32[]{:S(2)}) collective-permute-start(bf16[13,24,384]{2,1,0:T(8,128)(2,1)} %get-tuple-element.86), channel_id=1, source_target_pairs={{0,12},{1,13},{2,14},{3,15},{4,8},{5,9},{6,10},{7,11},{8,4},{9,5},... | collective-permute-start | bytes 718856 | tf_op jit(solution)/shard_map/ppermute | solution.py:657
  12.0 2.6 %collective-permute-done.2 = bf16[13,24,384]{2,1,0:T(8,128)(2,1)S(1)} collective-permute-done((bf16[13,24,384]{2,1,0:T(8,128)(2,1)}, bf16[13,24,384]{2,1,0:T(8,128)(2,1)S(1)}, u32[]{:S(2)}, u32[]{:S(2)}) %collective-permute-start.2) | collective-permute-done | bytes 239648 | tf_op jit(solution)/shard_map/ppermute | solution.py:657
  14.6 5.3 %collective-permute-done.1 = bf16[13,24,384]{2,1,0:T(8,128)(2,1)S(1)} collective-permute-done((bf16[13,24,384]{2,1,0:T(8,128)(2,1)}, bf16[13,24,384]{2,1,0:T(8,128)(2,1)S(1)}, u32[]{:S(2)}, u32[]{:S(2)}) %collective-permute-start.1) | collective-permute-done | bytes 239648 | tf_op jit(solution)/shard_map/ppermute | solution.py:657
  20.0 8.3 %collective-permute-done = bf16[13,24,384]{2,1,0:T(8,128)(2,1)S(1)} collective-permute-done((bf16[13,24,384]{2,1,0:T(8,128)(2,1)}, bf16[13,24,384]{2,1,0:T(8,128)(2,1)S(1)}, u32[]{:S(2)}, u32[]{:S(2)}) %collective-permute-start) | collective-permute-done | bytes 239648 | tf_op jit(solution)/shard_map/ppermute | solution.py:657
  28.3 2.5 %collective-permute-start.8 = (bf16[12,24,384]{2,1,0:T(8,128)(2,1)S(1)}, bf16[12,24,384]{2,1,0:T(8,128)(2,1)S(1)}, u32[]{:S(2)}, u32[]{:S(2)}) collective-permute-start(bf16[12,24,384]{2,1,0:T(8,128)(2,1)S(1)} %copy-done.3), channel_id=1, source_target_pairs={{0,12},{1,13},{2,14},{3,15},{4,8},{5,9},{6,10},{7,11},{8,4},{9,5},... | collective-permute-start | bytes 663560 | tf_op jit(solution)/shard_map/ppermute | solution.py:657
  30.9 1.9 collective-permute-start.6
  34.5 5.5 %collective-permute-done.3 = bf16[4,4,24,384]{3,2,1,0:T(8,128)(2,1)S(1)} collective-permute-done((bf16[4,4,24,384]{3,2,1,0:T(8,128)(2,1)S(1)}, bf16[4,4,24,384]{3,2,1,0:T(8,128)(2,1)S(1)}, u32[]{:S(2)}, u32[]{:S(2)}) %collective-permute-start.3) | collective-permute-done | bytes 294944 | tf_op jit(solution)/shard_map/ppermute | solution.py:657
  43.0 13.6 %fa.1 = (bf16[10,208,1152]{2,1,0:T(8,128)(2,1)}, bf16[10,208,384]{2,1,0:T(8,128)(2,1)}, f32[10,8,208]{2,1,0:T(8,128)}, bf16[10,208,384]{2,1,0:T(8,128)(2,1)}, f32[2,16,384]{2,1,0:T(8,128)}) custom-call(bf16[10,197,384]{2,1,0:T(8,128)(2,1)} %x_ref.2, bf16[8,4,24,384]{3,2,1,0:T(8,128)(2,1)} %copy-done.15, bf16[8,4,24,384]{3,2,1,0:T(8,128)(2,1)} %copy-done.18), custom_call_target="tpu_custom_call" | custom-call | flops 14949999616 | tf_op jit(solution)/shard_map/fa/pallas_call | solution.py:507
  62.2 17.6 %fm.1 = (f32[10,197,384]{2,1,0:T(8,128)}, bf16[10,208,1536]{2,1,0:T(8,128)(2,1)}, bf16[10,208,1536]{2,1,0:T(8,128)(2,1)}, bf16[10,208,384]{2,1,0:T(8,128)(2,1)}, f32[10,8,208]{2,1,0:T(8,128)}) custom-call(bf16[10,197,384]{2,1,0:T(8,128)(2,1)} %x_ref.2, bf16[10,208,384]{2,1,0:T(8,128)(2,1)} %get-tuple-element.92.o_ref, ...), custom_call_target="tpu_custom_call" | custom-call | flops 20700000256 | tf_op jit(solution)/shard_map/fm/pallas_call | solution.py:507
  80.3 3.7 %collective-permute-done.11.other = bf16[8,12,24,384]{3,2,1,0:T(8,128)(2,1)S(1)} collective-permute-done((bf16[8,12,24,384]{3,2,1,0:T(8,128)(2,1)S(1)}, bf16[8,12,24,384]{3,2,1,0:T(8,128)(2,1)S(1)}, u32[]{:S(2)}, u32[]{:S(2)}) %collective-permute-start.11) | collective-permute-done | bytes 1769504 | tf_op jit(solution)/shard_map/ppermute | solution.py:657
  85.3 60.8 %top.1 = (f32[10,197,384]{2,1,0:T(8,128)}, bf16[10,197,384]{2,1,0:T(8,128)(2,1)}, bf16[8,13,24,384]{3,2,1,0:T(8,128)(2,1)}, bf16[8,13,24,384]{3,2,1,0:T(8,128)(2,1)}) custom-call(f32[10,197,384]{2,1,0:T(8,128)} %get-tuple-element.70.x_ref, bf16[10,197,384]{2,1,0:T(8,128)(2,1)} %cot_ref.1, f32[2,16,384]{2,1,0:T(8,128)} %get-tuple-element.93.vec_ref, ...), custom_call_target="tpu_custom_call" | custom-call | flops 80499998720 | tf_op jit(solution)/shard_map/top/pallas_call | solution.py:507
  146.2 4.0 %collective-permute-done.12 = bf16[8,13,24,384]{3,2,1,0:T(8,128)(2,1)S(1)} collective-permute-done((bf16[8,13,24,384]{3,2,1,0:T(8,128)(2,1)}, bf16[8,13,24,384]{3,2,1,0:T(8,128)(2,1)S(1)}, u32[]{:S(2)}, u32[]{:S(2)}) %collective-permute-start.12) | collective-permute-done | bytes 1916960 | tf_op jit(solution)/shard_map/ppermute | solution.py:657
  153.2 25.9 %bm.1 = (bf16[10,208,384]{2,1,0:T(8,128)(2,1)}, bf16[10,208,384]{2,1,0:T(8,128)(2,1)}, bf16[8,9,24,384]{3,2,1,0:T(8,128)(2,1)}, bf16[8,9,24,384]{3,2,1,0:T(8,128...) custom-call(bf16[10,197,384]{2,1,0:T(8,128)(2,1)} %get-tuple-element.107.gr_ref, ...), custom_call_target="tpu_custom_call" | custom-call | flops 29899999232 | tf_op jit(solution)/shard_map/bm/pallas_call | solution.py:507
  180.3 2.3 collective-permute-start.18
  182.6 2.1 collective-permute-start.16
  185.5 17.9 %ba.1 = (bf16[10,208,1152]{2,1,0:T(8,128)(2,1)}, bf16[8,4,24,384]{3,2,1,0:T(8,128)(2,1)}, bf16[8,4,24,384]{3,2,1,0:T(8,128)(2,1)}) custom-call(bf16[10,208,1152]{2,1,0:T(8,128)(2,1)} %get-tuple-element.113.m_ref, bf16[10,208,384]{2,1,0:T(8,128)(2,1)} %get-tuple-element.120.do_ref, bf16[10,208,384]{2,1,0:T(8,128)(2,1)} %get-tuple-element.121.xh_ref, ...), custom_call_target="tpu_custom_call" | custom-call | flops 23000000512 | tf_op jit(solution)/shard_map/ba/pallas_call | solution.py:507
  208.0 5.7 %bx.2.rest_0_ = f32[10,197,384]{2,1,0:T(8,128)} custom-call(bf16[10,208,384]{2,1,0:T(8,128)(2,1)} %get-tuple-element.112.dx1_ref, bf16[10,208,1152]{2,1,0:T(8,128)(2,1)} %get-tuple-element.131.dm_ref, bf16[10,208,384]{2,1,0:T(8,128)(2,1)} %get-tuple-element.121.xh_ref, f32[10,8,208]{2,1,0:T(8,128)} %get-tuple-element.122.aux_ref, ...), custom_call_target="tpu_custom_call" | custom-call | flops 4600000000 | tf_op jit(solution)/shard_map/bx/pallas_call | solution.py:608
  220.7 7.2 %bx.3 = f32[10,197,384]{2,1,0:T(8,128)} custom-call(bf16[10,208,384]{2,1,0:T(8,128)(2,1)} %get-tuple-element.112.dx1_ref, bf16[10,208,1152]{2,1,0:T(8,128)(2,1)} %get-tuple-element.131.dm_ref, bf16[10,208,384]{2,1,0:T(8,128)(2,1)} %get-tuple-element.121.xh_ref, f32[10,8,208]{2,1,0:T(8,128)} %get-tuple-element.122.aux_ref, ...), custom_call_target="tpu_custom_call", output_to_operand_aliasing={{}: (7, {})} | custom-call | flops 6899999744 | tf_op jit(solution)/shard_map/bx/pallas_call | solution.py:608
  228.0 1.6 collective-permute-start.24
  230.3 3.0 %collective-permute-done.24 = bf16[1,4,24,384]{3,2,1,0:T(8,128)(2,1)S(1)} collective-permute-done((bf16[1,4,24,384]{3,2,1,0:T(8,128)(2,1)S(1)}, bf16[1,4,24,384]{3,2,1,0:T(8,128)(2,1)S(1)}, u32[]{:S(2)}, u32[]{:S(2)}) %collective-permute-start.24) | collective-permute-done | bytes 73760 | tf_op jit(solution)/shard_map/ppermute | solution.py:657
  233.4 2.0 collective-permute-start.25
  235.4 2.4 collective-permute-done.25.refs_1_
  239.1 2.2 finish.1
  (116 shorter events, 34.9 us)
Async XLA Ops:
  2.6 12.0 %collective-permute-start.2 = (bf16[13,24,384]{2,1,0:T(8,128)(2,1)}, bf16[13,24,384]{2,1,0:T(8,128)(2,1)S(1)}, u32[]{:S(2)}, u32[]{:S(2)}) collective-permute-start(bf16[13,24,384]{2,1,0:T(8,128)(2,1)} %get-tuple-element.86), channel_id=1, source_target_pairs={{0,12},{1,13},{2,14},{3,15},{4,8},{5,9},{6,10},{7,11},{8,4},{9,5},... | collective-permute-start | bytes 718856 | tf_op jit(solution)/shard_map/ppermute | solution.py:657
  7.7 12.3 %collective-permute-start.1 = (bf16[13,24,384]{2,1,0:T(8,128)(2,1)}, bf16[13,24,384]{2,1,0:T(8,128)(2,1)S(1)}, u32[]{:S(2)}, u32[]{:S(2)}) collective-permute-start(bf16[13,24,384]{2,1,0:T(8,128)(2,1)} %get-tuple-element.86), channel_id=1, source_target_pairs={{0,4},{1,5},{2,6},{3,7},{4,0},{5,1},{6,2},{7,3},{8,12},{9,13},{10,... | collective-permute-start | bytes 718856 | tf_op jit(solution)/shard_map/ppermute | solution.py:657
  7.7 20.6 %collective-permute-start = (bf16[13,24,384]{2,1,0:T(8,128)(2,1)}, bf16[13,24,384]{2,1,0:T(8,128)(2,1)S(1)}, u32[]{:S(2)}, u32[]{:S(2)}) collective-permute-start(bf16[13,24,384]{2,1,0:T(8,128)(2,1)} %get-tuple-element.86), channel_id=1, source_target_pairs={{0,8},{1,9},{2,10},{3,11},{4,12},{5,13},{6,14},{7,15},{8,0},{9,1},... | collective-permute-start | bytes 718856 | tf_op jit(solution)/shard_map/ppermute | solution.py:657
  28.3 28.3 %collective-permute-start.8 = (bf16[12,24,384]{2,1,0:T(8,128)(2,1)S(1)}, bf16[12,24,384]{2,1,0:T(8,128)(2,1)S(1)}, u32[]{:S(2)}, u32[]{:S(2)}) collective-permute-start(bf16[12,24,384]{2,1,0:T(8,128)(2,1)S(1)} %copy-done.3), channel_id=1, source_target_pairs={{0,12},{1,13},{2,14},{3,15},{4,8},{5,9},{6,10},{7,11},{8,4},{9,5},... | collective-permute-start | bytes 663560 | tf_op jit(solution)/shard_map/ppermute | solution.py:657
  30.9 25.8 %collective-permute-start.7 = (bf16[12,24,384]{2,1,0:T(8,128)(2,1)S(1)}, bf16[12,24,384]{2,1,0:T(8,128)(2,1)S(1)}, u32[]{:S(2)}, u32[]{:S(2)}) collective-permute-start(bf16[12,24,384]{2,1,0:T(8,128)(2,1)S(1)} %copy-done.3), channel_id=1, source_target_pairs={{0,4},{1,5},{2,6},{3,7},{4,0},{5,1},{6,2},{7,3},{8,12},{9,13},{10,... | collective-permute-start | bytes 663560 | tf_op jit(solution)/shard_map/ppermute | solution.py:657
  30.9 25.8 %collective-permute-start.6 = (bf16[12,24,384]{2,1,0:T(8,128)(2,1)S(1)}, bf16[12,24,384]{2,1,0:T(8,128)(2,1)S(1)}, u32[]{:S(2)}, u32[]{:S(2)}) collective-permute-start(bf16[12,24,384]{2,1,0:T(8,128)(2,1)S(1)} %copy-done.3), channel_id=1, source_target_pairs={{0,8},{1,9},{2,10},{3,11},{4,12},{5,13},{6,14},{7,15},{8,0},{9,1},... | collective-permute-start | bytes 663560 | tf_op jit(solution)/shard_map/ppermute | solution.py:657
  32.8 7.2 %collective-permute-start.3 = (bf16[4,4,24,384]{3,2,1,0:T(8,128)(2,1)S(1)}, bf16[4,4,24,384]{3,2,1,0:T(8,128)(2,1)S(1)}, u32[]{:S(2)}, u32[]{:S(2)}) collective-permute-start(bf16[4,4,24,384]{3,2,1,0:T(8,128)(2,1)S(1)} %pad_maximum_fusion.2), channel_id=1, source_target_pairs={{0,2},{1,3},{2,0},{3,1},{4,6},{5,7},{6,4},{7,5},{8,10},{9,11},{10,... | collective-permute-start | bytes 884744 | tf_op jit(solution)/shard_map/ppermute | solution.py:657
  40.3 17.4 %collective-permute-start.5 = (bf16[4,9,24,384]{3,2,1,0:T(8,128)(2,1)S(1)}, bf16[4,9,24,384]{3,2,1,0:T(8,128)(2,1)S(1)}, u32[]{:S(2)}, u32[]{:S(2)}) collective-permute-start(bf16[4,9,24,384]{3,2,1,0:T(8,128)(2,1)S(1)} %pad_maximum_fusion.1), channel_id=1, source_target_pairs={{0,2},{1,3},{2,0},{3,1},{4,6},{5,7},{6,4},{7,5},{8,10},{9,11},{10,... | collective-permute-start | bytes 1990664 | tf_op jit(solution)/shard_map/ppermute | solution.py:657
  58.0 22.1 %collective-permute-start.10 = (bf16[4,12,24,384]{3,2,1,0:T(8,128)(2,1)S(1)}, bf16[4,12,24,384]{3,2,1,0:T(8,128)(2,1)S(1)}, u32[]{:S(2)}, u32[]{:S(2)}) collective-permute-start(bf16[4,12,24,384]{3,2,1,0:T(8,128)(2,1)S(1)} %pad_maximum_fusion), channel_id=1, source_target_pairs={{0,2},{1,3},{2,0},{3,1},{4,6},{5,7},{6,4},{7,5},{8,10},{9,11},{10,... | collective-permute-start | bytes 2654216 | tf_op jit(solution)/shard_map/ppermute | solution.py:657
  146.0 4.2 %collective-permute-start.12 = (bf16[8,13,24,384]{3,2,1,0:T(8,128)(2,1)}, bf16[8,13,24,384]{3,2,1,0:T(8,128)(2,1)S(1)}, u32[]{:S(2)}, u32[]{:S(2)}) collective-permute-start(bf16[8,13,24,384]{3,2,1,0:T(8,128)(2,1)} %get-tuple-element.106), channel_id=1, source_target_pairs={{0,1},{1,0},{2,3},{3,2},{4,5},{5,4},{6,7},{7,6},{8,9},{9,8},{10,11... | collective-permute-start | bytes 5750792 | tf_op jit(solution)/shard_map/ppermute | solution.py:657
  151.7 27.5 %collective-permute-start.13 = (bf16[4,13,24,384]{3,2,1,0:T(8,128)(2,1)S(1)}, bf16[4,13,24,384]{3,2,1,0:T(8,128)(2,1)S(1)}, u32[]{:S(2)}, u32[]{:S(2)}) collective-permute-start(bf16[4,13,24,384]{3,2,1,0:T(8,128)(2,1)S(1)} %add_convert_fusion), channel_id=1, source_target_pairs={{0,2},{1,3},{2,0},{3,1},{4,6},{5,7},{6,4},{7,5},{8,10},{9,11},{10,... | collective-permute-start | bytes 2875400 | tf_op jit(solution)/shard_map/ppermute | solution.py:657
  179.2 5.5 %collective-permute-start.14 = (bf16[8,9,24,384]{3,2,1,0:T(8,128)(2,1)}, bf16[8,9,24,384]{3,2,1,0:T(8,128)(2,1)S(1)}, u32[]{:S(2)}, u32[]{:S(2)}) collective-permute-start(bf16[8,9,24,384]{3,2,1,0:T(8,128)(2,1)} %get-tuple-element.119), channel_id=1, source_target_pairs={{0,1},{1,0},{2,3},{3,2},{4,5},{5,4},{6,7},{7,6},{8,9},{9,8},{10,11... | collective-permute-start | bytes 3981320 | tf_op jit(solution)/shard_map/ppermute | solution.py:657
  180.3 23.1 %collective-permute-start.18 = (bf16[13,24,384]{2,1,0:T(8,128)(2,1)}, bf16[13,24,384]{2,1,0:T(8,128)(2,1)S(1)}, u32[]{:S(2)}, u32[]{:S(2)}) collective-permute-start(bf16[13,24,384]{2,1,0:T(8,128)(2,1)} %get-tuple-element.156), channel_id=1, source_target_pairs={{0,12},{1,13},{2,14},{3,15},{4,8},{5,9},{6,10},{7,11},{8,4},{9,5},... | collective-permute-start | bytes 718856 | tf_op jit(solution)/shard_map/ppermute | solution.py:657
  182.6 20.8 %collective-permute-start.17 = (bf16[13,24,384]{2,1,0:T(8,128)(2,1)}, bf16[13,24,384]{2,1,0:T(8,128)(2,1)S(1)}, u32[]{:S(2)}, u32[]{:S(2)}) collective-permute-start(bf16[13,24,384]{2,1,0:T(8,128)(2,1)} %get-tuple-element.157), channel_id=1, source_target_pairs={{0,4},{1,5},{2,6},{3,7},{4,0},{5,1},{6,2},{7,3},{8,12},{9,13},{10,... | collective-permute-start | bytes 718856 | tf_op jit(solution)/shard_map/ppermute | solution.py:657
  182.6 21.3 %collective-permute-start.16 = (bf16[13,24,384]{2,1,0:T(8,128)(2,1)}, bf16[13,24,384]{2,1,0:T(8,128)(2,1)S(1)}, u32[]{:S(2)}, u32[]{:S(2)}) collective-permute-start(bf16[13,24,384]{2,1,0:T(8,128)(2,1)} %get-tuple-element.158), channel_id=1, source_target_pairs={{0,8},{1,9},{2,10},{3,11},{4,12},{5,13},{6,14},{7,15},{8,0},{9,1},... | collective-permute-start | bytes 718856 | tf_op jit(solution)/shard_map/ppermute | solution.py:657
  184.9 19.1 %collective-permute-start.15 = (bf16[4,9,24,384]{3,2,1,0:T(8,128)(2,1)S(1)}, bf16[4,9,24,384]{3,2,1,0:T(8,128)(2,1)S(1)}, u32[]{:S(2)}, u32[]{:S(2)}) collective-permute-start(bf16[4,9,24,384]{3,2,1,0:T(8,128)(2,1)S(1)} %add_convert_fusion.1), channel_id=1, source_target_pairs={{0,2},{1,3},{2,0},{3,1},{4,6},{5,7},{6,4},{7,5},{8,10},{9,11},{10,... | collective-permute-start | bytes 1990664 | tf_op jit(solution)/shard_map/ppermute | solution.py:657
  204.7 10.3 %collective-permute-start.21 = (bf16[2,9,24,384]{3,2,1,0:T(8,128)(2,1)S(1)}, bf16[2,9,24,384]{3,2,1,0:T(8,128)(2,1)S(1)}, u32[]{:S(2)}, u32[]{:S(2)}) collective-permute-start(bf16[2,9,24,384]{3,2,1,0:T(8,128)(2,1)S(1)} %add_convert_fusion.2), channel_id=1, source_target_pairs={{0,4},{1,5},{2,6},{3,7},{4,0},{5,1},{6,2},{7,3},{8,12},{9,13},{10,... | collective-permute-start | bytes 995336 | tf_op jit(solution)/shard_map/ppermute | solution.py:657
  206.9 9.1 %collective-permute-start.20 = (bf16[4,4,24,384]{3,2,1,0:T(8,128)(2,1)S(1)}, bf16[4,4,24,384]{3,2,1,0:T(8,128)(2,1)S(1)}, u32[]{:S(2)}, u32[]{:S(2)}) collective-permute-start(bf16[4,4,24,384]{3,2,1,0:T(8,128)(2,1)S(1)} %add_convert_fusion.3), channel_id=1, source_target_pairs={{0,2},{1,3},{2,0},{3,1},{4,6},{5,7},{6,4},{7,5},{8,10},{9,11},{10,... | collective-permute-start | bytes 884744 | tf_op jit(solution)/shard_map/ppermute | solution.py:657
  216.1 11.8 %collective-permute-start.22 = (bf16[2,4,24,384]{3,2,1,0:T(8,128)(2,1)S(1)}, bf16[2,4,24,384]{3,2,1,0:T(8,128)(2,1)S(1)}, u32[]{:S(2)}, u32[]{:S(2)}) collective-permute-start(bf16[2,4,24,384]{3,2,1,0:T(8,128)(2,1)S(1)} %add_convert_fusion.9), channel_id=1, source_target_pairs={{0,4},{1,5},{2,6},{3,7},{4,0},{5,1},{6,2},{7,3},{8,12},{9,13},{10,... | collective-permute-start | bytes 442376 | tf_op jit(solution)/shard_map/ppermute | solution.py:657
  217.7 10.2 %collective-permute-start.23 = (bf16[1,9,24,384]{3,2,1,0:T(8,128)(2,1)S(1)}, bf16[1,9,24,384]{3,2,1,0:T(8,128)(2,1)S(1)}, u32[]{:S(2)}, u32[]{:S(2)}) collective-permute-start(bf16[1,9,24,384]{3,2,1,0:T(8,128)(2,1)S(1)} %add_convert_fusion.8), channel_id=1, source_target_pairs={{0,8},{1,9},{2,10},{3,11},{4,12},{5,13},{6,14},{7,15},{8,0},{9,1},... | collective-permute-start | bytes 497672 | tf_op jit(solution)/shard_map/ppermute | solution.py:657
  219.1 16.2 %collective-permute-start.27 = (bf16[13,24,384]{2,1,0:T(8,128)(2,1)S(1)}, bf16[13,24,384]{2,1,0:T(8,128)(2,1)S(1)}, u32[]{:S(2)}, u32[]{:S(2)}) collective-permute-start(bf16[13,24,384]{2,1,0:T(8,128)(2,1)S(1)} %fusion.2.refs_4_), channel_id=1, source_target_pairs={{0,16},{16,0},{1,17},{17,1},{2,18},{18,2},{3,19},{19,3},{4,20},{20... | collective-permute-start | bytes 718856 | tf_op jit(solution)/shard_map/ppermute | solution.py:732
  228.0 5.3 %collective-permute-start.24 = (bf16[1,4,24,384]{3,2,1,0:T(8,128)(2,1)S(1)}, bf16[1,4,24,384]{3,2,1,0:T(8,128)(2,1)S(1)}, u32[]{:S(2)}, u32[]{:S(2)}) collective-permute-start(bf16[1,4,24,384]{3,2,1,0:T(8,128)(2,1)S(1)} %add_convert_fusion.11), channel_id=1, source_target_pairs={{0,8},{1,9},{2,10},{3,11},{4,12},{5,13},{6,14},{7,15},{8,0},{9,1},... | collective-permute-start | bytes 221192 | tf_op jit(solution)/shard_map/ppermute | solution.py:657
  229.7 8.0 %collective-permute-start.26 = (bf16[9,24,384]{2,1,0:T(8,128)(2,1)S(1)}, bf16[9,24,384]{2,1,0:T(8,128)(2,1)S(1)}, u32[]{:S(2)}, u32[]{:S(2)}) collective-permute-start(bf16[9,24,384]{2,1,0:T(8,128)(2,1)S(1)} %fusion.6.refs_2_), channel_id=1, source_target_pairs={{0,16},{16,0},{1,17},{17,1},{2,18},{18,2},{3,19},{19,3},{4,20},{20... | collective-permute-start | bytes 497672 | tf_op jit(solution)/shard_map/ppermute | solution.py:732
  233.4 4.4 %collective-permute-start.25 = (bf16[4,24,384]{2,1,0:T(8,128)(2,1)S(1)}, bf16[4,24,384]{2,1,0:T(8,128)(2,1)S(1)}, u32[]{:S(2)}, u32[]{:S(2)}) collective-permute-start(bf16[4,24,384]{2,1,0:T(8,128)(2,1)S(1)} %fusion.7.refs_0_), channel_id=1, source_target_pairs={{0,16},{16,0},{1,17},{17,1},{2,18},{18,2},{3,19},{19,3},{4,20},{20... | collective-permute-start | bytes 221192 | tf_op jit(solution)/shard_map/ppermute | solution.py:732
  (23 other events, 114.7 us)

commit v6 on v5

--- a/solution.py
+++ b/solution.py
@@ -613,7 +613,7 @@
         out_shape=out,
         input_output_aliases={7: 0} if more else {},
         scratch_shapes=wscratch(wa[0]),
-        compiler_params=pltpu.CompilerParams(vmem_limit_bytes=VMEM_LIMIT),
+        compiler_params=pltpu.CompilerParams(vmem_limit_bytes=32 * 2**20),
         name="bx",
         cost_estimate=pl.CostEstimate(flops=count * 1_150_000_000, bytes_accessed=0, transcendentals=0),
     )(dx1, dm, xh, aux, vec, *wa, *more)
@@ -626,6 +626,7 @@
         out_shape=[sds((2, part, 3 * width), F32), sds((2, part, width), F32), sds((2, part, ff), F32),
                    sds((2, ff // width * part, width), F32), sds((2, ff // width * part), F32)]
         + [sds((2, part), F32)] * 8,
+        compiler_params=pltpu.CompilerParams(vmem_limit_bytes=24 * 2**20),
         name="finish",
     )(*a0, *m0, *l1)
 

time: 242 us -> 239 us (0.988)
  Pallas kernels: 153 us -> 148 us
    pallas_call x2, Pallas kernels: 13 us -> 9.56 us  [run_bx(): pl.pallas_call(functools.partial(bx_kernel, seq), grid=(count // per,), i...]
    unnamed x50 -> x46, local copies, waits for them, and re-layouts: 7.31 us -> 7.68 us
  transfers between devices with their start and end apart: 28 -> 28, of which waited for: 16 -> 17; matrix products, arithmetic and copies ran while one was open for 3% -> 3% of each run, Pallas kernels for 36% -> 36%
where the time goes in v6:
time: 239 us; the launch traced here: 238 us
  Pallas kernels  148 us (62%)
  waiting for transfers between devices  42.5 us (18%)
  starting transfers between devices  30.8 us (13%)
  local copies, waits for them, and re-layouts  9.95 us (4%)
  other arithmetic  5.01 us (2%)
    pallas_call x5, Pallas kernels, call(): pl.pallas_call(kern, grid=(blocked_in[0].shape[0] // per,), in_specs=in_s...  136 us
    ppermute x25, waiting for transfers between devices, swap(): return lax.ppermute(x, 'shard', xor_pairs(n, b))  39.7 us
    ppermute x25, starting transfers between devices, swap(): return lax.ppermute(x, 'shard', xor_pairs(n, b))  26.1 us
    pallas_call x2, Pallas kernels, run_bx(): pl.pallas_call(functools.partial(bx_kernel, seq), grid=(count // per,), i...  9.56 us
    unnamed x46, local copies, waits for them, and re-layouts  7.68 us
  transfers between devices with their start and end apart: 28, of which 17 were waited for; matrix products, arithmetic and copies ran while one was open for 3% of the time, Pallas kernels for 36%

profile of v6, /device:TPU:0, one launch (start us, length us, event | category | flops | bytes accessed | tf_op | source)
XLA Modules:
  0.0 238.1 jit_solution(16953153442373370760)
XLA Ops:
  0.7 2.0 pack.1
  2.6 5.0 %collective-permute-start.2 = (bf16[13,24,384]{2,1,0:T(8,128)(2,1)}, bf16[13,24,384]{2,1,0:T(8,128)(2,1)S(1)}, u32[]{:S(2)}, u32[]{:S(2)}) collective-permute-start(bf16[13,24,384]{2,1,0:T(8,128)(2,1)} %get-tuple-element.86), channel_id=1, source_target_pairs={{0,12},{1,13},{2,14},{3,15},{4,8},{5,9},{6,10},{7,11},{8,4},{9,5},... | collective-permute-start | bytes 718856 | tf_op jit(solution)/shard_map/ppermute | solution.py:658
  12.0 2.6 %collective-permute-done.2 = bf16[13,24,384]{2,1,0:T(8,128)(2,1)S(1)} collective-permute-done((bf16[13,24,384]{2,1,0:T(8,128)(2,1)}, bf16[13,24,384]{2,1,0:T(8,128)(2,1)S(1)}, u32[]{:S(2)}, u32[]{:S(2)}) %collective-permute-start.2) | collective-permute-done | bytes 239648 | tf_op jit(solution)/shard_map/ppermute | solution.py:658
  14.6 5.3 %collective-permute-done.1 = bf16[13,24,384]{2,1,0:T(8,128)(2,1)S(1)} collective-permute-done((bf16[13,24,384]{2,1,0:T(8,128)(2,1)}, bf16[13,24,384]{2,1,0:T(8,128)(2,1)S(1)}, u32[]{:S(2)}, u32[]{:S(2)}) %collective-permute-start.1) | collective-permute-done | bytes 239648 | tf_op jit(solution)/shard_map/ppermute | solution.py:658
  20.0 8.3 %collective-permute-done = bf16[13,24,384]{2,1,0:T(8,128)(2,1)S(1)} collective-permute-done((bf16[13,24,384]{2,1,0:T(8,128)(2,1)}, bf16[13,24,384]{2,1,0:T(8,128)(2,1)S(1)}, u32[]{:S(2)}, u32[]{:S(2)}) %collective-permute-start) | collective-permute-done | bytes 239648 | tf_op jit(solution)/shard_map/ppermute | solution.py:658
  28.3 2.5 %collective-permute-start.8 = (bf16[12,24,384]{2,1,0:T(8,128)(2,1)S(1)}, bf16[12,24,384]{2,1,0:T(8,128)(2,1)S(1)}, u32[]{:S(2)}, u32[]{:S(2)}) collective-permute-start(bf16[12,24,384]{2,1,0:T(8,128)(2,1)S(1)} %copy-done.11), channel_id=1, source_target_pairs={{0,12},{1,13},{2,14},{3,15},{4,8},{5,9},{6,10},{7,11},{8,4},{9,5},... | collective-permute-start | bytes 663560 | tf_op jit(solution)/shard_map/ppermute | solution.py:658
  30.9 1.9 collective-permute-start.6
  34.5 5.5 %collective-permute-done.3 = bf16[4,4,24,384]{3,2,1,0:T(8,128)(2,1)S(1)} collective-permute-done((bf16[4,4,24,384]{3,2,1,0:T(8,128)(2,1)S(1)}, bf16[4,4,24,384]{3,2,1,0:T(8,128)(2,1)S(1)}, u32[]{:S(2)}, u32[]{:S(2)}) %collective-permute-start.3) | collective-permute-done | bytes 294944 | tf_op jit(solution)/shard_map/ppermute | solution.py:658
  43.0 13.6 %fa.1 = (bf16[10,208,1152]{2,1,0:T(8,128)(2,1)}, bf16[10,208,384]{2,1,0:T(8,128)(2,1)}, f32[10,8,208]{2,1,0:T(8,128)}, bf16[10,208,384]{2,1,0:T(8,128)(2,1)}, f32[2,16,384]{2,1,0:T(8,128)}) custom-call(bf16[10,197,384]{2,1,0:T(8,128)(2,1)} %x_ref.2, bf16[8,4,24,384]{3,2,1,0:T(8,128)(2,1)} %copy-done, bf16[8,4,24,384]{3,2,1,0:T(8,128)(2,1)} %copy-done.2), custom_call_target="tpu_custom_call" | custom-call | flops 14949999616 | tf_op jit(solution)/shard_map/fa/pallas_call | solution.py:507
  62.1 17.6 %fm.1 = (f32[10,197,384]{2,1,0:T(8,128)}, bf16[10,208,1536]{2,1,0:T(8,128)(2,1)}, bf16[10,208,1536]{2,1,0:T(8,128)(2,1)}, bf16[10,208,384]{2,1,0:T(8,128)(2,1)}, f32[10,8,208]{2,1,0:T(8,128)}) custom-call(bf16[10,197,384]{2,1,0:T(8,128)(2,1)} %x_ref.2, bf16[10,208,384]{2,1,0:T(8,128)(2,1)} %get-tuple-element.92.o_ref, ...), custom_call_target="tpu_custom_call" | custom-call | flops 20700000256 | tf_op jit(solution)/shard_map/fm/pallas_call | solution.py:507
  80.3 3.7 %collective-permute-done.11.other = bf16[8,12,24,384]{3,2,1,0:T(8,128)(2,1)S(1)} collective-permute-done((bf16[8,12,24,384]{3,2,1,0:T(8,128)(2,1)S(1)}, bf16[8,12,24,384]{3,2,1,0:T(8,128)(2,1)S(1)}, u32[]{:S(2)}, u32[]{:S(2)}) %collective-permute-start.11) | collective-permute-done | bytes 1769504 | tf_op jit(solution)/shard_map/ppermute | solution.py:658
  85.2 60.8 %top.1 = (f32[10,197,384]{2,1,0:T(8,128)}, bf16[10,197,384]{2,1,0:T(8,128)(2,1)}, bf16[8,13,24,384]{3,2,1,0:T(8,128)(2,1)}, bf16[8,13,24,384]{3,2,1,0:T(8,128)(2,1)}) custom-call(f32[10,197,384]{2,1,0:T(8,128)} %get-tuple-element.70.x_ref, bf16[10,197,384]{2,1,0:T(8,128)(2,1)} %cot_ref.1, f32[2,16,384]{2,1,0:T(8,128)} %get-tuple-element.93.vec_ref, ...), custom_call_target="tpu_custom_call" | custom-call | flops 80499998720 | tf_op jit(solution)/shard_map/top/pallas_call | solution.py:507
  146.2 4.0 %collective-permute-done.12 = bf16[8,13,24,384]{3,2,1,0:T(8,128)(2,1)S(1)} collective-permute-done((bf16[8,13,24,384]{3,2,1,0:T(8,128)(2,1)}, bf16[8,13,24,384]{3,2,1,0:T(8,128)(2,1)S(1)}, u32[]{:S(2)}, u32[]{:S(2)}) %collective-permute-start.12) | collective-permute-done | bytes 1916960 | tf_op jit(solution)/shard_map/ppermute | solution.py:658
  153.2 25.9 %bm.1 = (bf16[10,208,384]{2,1,0:T(8,128)(2,1)}, bf16[10,208,384]{2,1,0:T(8,128)(2,1)}, bf16[8,9,24,384]{3,2,1,0:T(8,128)(2,1)}, bf16[8,9,24,384]{3,2,1,0:T(8,128...) custom-call(bf16[10,197,384]{2,1,0:T(8,128)(2,1)} %get-tuple-element.107.gr_ref, ...), custom_call_target="tpu_custom_call" | custom-call | flops 29899999232 | tf_op jit(solution)/shard_map/bm/pallas_call | solution.py:507
  180.3 2.3 collective-permute-start.18
  182.6 2.1 collective-permute-start.16
  185.5 18.0 %ba.1 = (bf16[10,208,1152]{2,1,0:T(8,128)(2,1)}, bf16[8,4,24,384]{3,2,1,0:T(8,128)(2,1)}, bf16[8,4,24,384]{3,2,1,0:T(8,128)(2,1)}) custom-call(bf16[10,208,1152]{2,1,0:T(8,128)(2,1)} %get-tuple-element.113.m_ref, bf16[10,208,384]{2,1,0:T(8,128)(2,1)} %get-tuple-element.120.do_ref, bf16[10,208,384]{2,1,0:T(8,128)(2,1)} %get-tuple-element.121.xh_ref, ...), custom_call_target="tpu_custom_call" | custom-call | flops 23000000512 | tf_op jit(solution)/shard_map/ba/pallas_call | solution.py:507
  207.5 2.3 copy-done.4
  209.9 4.3 %bx.2.rest_0_ = f32[10,197,384]{2,1,0:T(8,128)} custom-call(bf16[10,208,384]{2,1,0:T(8,128)(2,1)S(1)} %copy-done.6, bf16[10,208,1152]{2,1,0:T(8,128)(2,1)S(1)} %copy-done.4, bf16[10,208,384]{2,1,0:T(8,128)(2,1)S(1)} %copy-done.5, f32[10,8,208]{2,1,0:T(8,128)S(1)} %copy-done.7, f32[2,16,384]{2,1,0:T(8,128)S(1)} %copy-done.8, ...), custom_call_target="tpu_custom_call" | custom-call | flops 4600000000 | tf_op jit(solution)/shard_map/bx/pallas_call | solution.py:608
  220.1 5.2 %bx.3 = f32[10,197,384]{2,1,0:T(8,128)} custom-call(bf16[10,208,384]{2,1,0:T(8,128)(2,1)S(1)} %copy-done.6, bf16[10,208,1152]{2,1,0:T(8,128)(2,1)S(1)} %copy-done.4, bf16[10,208,384]{2,1,0:T(8,128)(2,1)S(1)} %copy-done.5, f32[10,8,208]{2,1,0:T(8,128)S(1)} %copy-done.7, f32[2,16,384]{2,1,0:T(8,128)S(1)} %copy-done.8, ...), custom_call_target="tpu_custom_call", output_to_operand_aliasing={{}: (7, {})} | custom-call | flops 6899999744 | tf_op jit(solution)/shard_map/bx/pallas_call | solution.py:608
  225.3 1.7 collective-permute-done.23
  227.3 1.7 collective-permute-start.26
  228.9 3.6 %collective-permute-done.24 = bf16[1,4,24,384]{3,2,1,0:T(8,128)(2,1)S(1)} collective-permute-done((bf16[1,4,24,384]{3,2,1,0:T(8,128)(2,1)S(1)}, bf16[1,4,24,384]{3,2,1,0:T(8,128)(2,1)S(1)}, u32[]{:S(2)}, u32[]{:S(2)}) %collective-permute-start.24) | collective-permute-done | bytes 73760 | tf_op jit(solution)/shard_map/ppermute | solution.py:658
  234.1 2.8 %collective-permute-done.25.refs_1_ = bf16[4,24,384]{2,1,0:T(8,128)(2,1)S(1)} collective-permute-done((bf16[4,24,384]{2,1,0:T(8,128)(2,1)S(1)}, bf16[4,24,384]{2,1,0:T(8,128)(2,1)S(1)}, u32[]{:S(2)}, u32[]{:S(2)}) %collective-permute-start.25) | collective-permute-done | bytes 73760 | tf_op jit(solution)/shard_map/ppermute | solution.py:733
  (112 shorter events, 34.0 us)
Async XLA Ops:
  2.6 12.0 %collective-permute-start.2 = (bf16[13,24,384]{2,1,0:T(8,128)(2,1)}, bf16[13,24,384]{2,1,0:T(8,128)(2,1)S(1)}, u32[]{:S(2)}, u32[]{:S(2)}) collective-permute-start(bf16[13,24,384]{2,1,0:T(8,128)(2,1)} %get-tuple-element.86), channel_id=1, source_target_pairs={{0,12},{1,13},{2,14},{3,15},{4,8},{5,9},{6,10},{7,11},{8,4},{9,5},... | collective-permute-start | bytes 718856 | tf_op jit(solution)/shard_map/ppermute | solution.py:658
  7.7 12.3 %collective-permute-start.1 = (bf16[13,24,384]{2,1,0:T(8,128)(2,1)}, bf16[13,24,384]{2,1,0:T(8,128)(2,1)S(1)}, u32[]{:S(2)}, u32[]{:S(2)}) collective-permute-start(bf16[13,24,384]{2,1,0:T(8,128)(2,1)} %get-tuple-element.86), channel_id=1, source_target_pairs={{0,4},{1,5},{2,6},{3,7},{4,0},{5,1},{6,2},{7,3},{8,12},{9,13},{10,... | collective-permute-start | bytes 718856 | tf_op jit(solution)/shard_map/ppermute | solution.py:658
  7.7 20.6 %collective-permute-start = (bf16[13,24,384]{2,1,0:T(8,128)(2,1)}, bf16[13,24,384]{2,1,0:T(8,128)(2,1)S(1)}, u32[]{:S(2)}, u32[]{:S(2)}) collective-permute-start(bf16[13,24,384]{2,1,0:T(8,128)(2,1)} %get-tuple-element.86), channel_id=1, source_target_pairs={{0,8},{1,9},{2,10},{3,11},{4,12},{5,13},{6,14},{7,15},{8,0},{9,1},... | collective-permute-start | bytes 718856 | tf_op jit(solution)/shard_map/ppermute | solution.py:658
  28.3 28.3 %collective-permute-start.8 = (bf16[12,24,384]{2,1,0:T(8,128)(2,1)S(1)}, bf16[12,24,384]{2,1,0:T(8,128)(2,1)S(1)}, u32[]{:S(2)}, u32[]{:S(2)}) collective-permute-start(bf16[12,24,384]{2,1,0:T(8,128)(2,1)S(1)} %copy-done.11), channel_id=1, source_target_pairs={{0,12},{1,13},{2,14},{3,15},{4,8},{5,9},{6,10},{7,11},{8,4},{9,5},... | collective-permute-start | bytes 663560 | tf_op jit(solution)/shard_map/ppermute | solution.py:658
  30.9 25.8 %collective-permute-start.7 = (bf16[12,24,384]{2,1,0:T(8,128)(2,1)S(1)}, bf16[12,24,384]{2,1,0:T(8,128)(2,1)S(1)}, u32[]{:S(2)}, u32[]{:S(2)}) collective-permute-start(bf16[12,24,384]{2,1,0:T(8,128)(2,1)S(1)} %copy-done.11), channel_id=1, source_target_pairs={{0,4},{1,5},{2,6},{3,7},{4,0},{5,1},{6,2},{7,3},{8,12},{9,13},{10,... | collective-permute-start | bytes 663560 | tf_op jit(solution)/shard_map/ppermute | solution.py:658
  30.9 25.8 %collective-permute-start.6 = (bf16[12,24,384]{2,1,0:T(8,128)(2,1)S(1)}, bf16[12,24,384]{2,1,0:T(8,128)(2,1)S(1)}, u32[]{:S(2)}, u32[]{:S(2)}) collective-permute-start(bf16[12,24,384]{2,1,0:T(8,128)(2,1)S(1)} %copy-done.11), channel_id=1, source_target_pairs={{0,8},{1,9},{2,10},{3,11},{4,12},{5,13},{6,14},{7,15},{8,0},{9,1},... | collective-permute-start | bytes 663560 | tf_op jit(solution)/shard_map/ppermute | solution.py:658
  32.8 7.2 %collective-permute-start.3 = (bf16[4,4,24,384]{3,2,1,0:T(8,128)(2,1)S(1)}, bf16[4,4,24,384]{3,2,1,0:T(8,128)(2,1)S(1)}, u32[]{:S(2)}, u32[]{:S(2)}) collective-permute-start(bf16[4,4,24,384]{3,2,1,0:T(8,128)(2,1)S(1)} %pad_maximum_fusion.2), channel_id=1, source_target_pairs={{0,2},{1,3},{2,0},{3,1},{4,6},{5,7},{6,4},{7,5},{8,10},{9,11},{10,... | collective-permute-start | bytes 884744 | tf_op jit(solution)/shard_map/ppermute | solution.py:658
  40.3 17.4 %collective-permute-start.5 = (bf16[4,9,24,384]{3,2,1,0:T(8,128)(2,1)S(1)}, bf16[4,9,24,384]{3,2,1,0:T(8,128)(2,1)S(1)}, u32[]{:S(2)}, u32[]{:S(2)}) collective-permute-start(bf16[4,9,24,384]{3,2,1,0:T(8,128)(2,1)S(1)} %pad_maximum_fusion.1), channel_id=1, source_target_pairs={{0,2},{1,3},{2,0},{3,1},{4,6},{5,7},{6,4},{7,5},{8,10},{9,11},{10,... | collective-permute-start | bytes 1990664 | tf_op jit(solution)/shard_map/ppermute | solution.py:658
  58.0 22.1 %collective-permute-start.10 = (bf16[4,12,24,384]{3,2,1,0:T(8,128)(2,1)S(1)}, bf16[4,12,24,384]{3,2,1,0:T(8,128)(2,1)S(1)}, u32[]{:S(2)}, u32[]{:S(2)}) collective-permute-start(bf16[4,12,24,384]{3,2,1,0:T(8,128)(2,1)S(1)} %pad_maximum_fusion), channel_id=1, source_target_pairs={{0,2},{1,3},{2,0},{3,1},{4,6},{5,7},{6,4},{7,5},{8,10},{9,11},{10,... | collective-permute-start | bytes 2654216 | tf_op jit(solution)/shard_map/ppermute | solution.py:658
  146.0 4.2 %collective-permute-start.12 = (bf16[8,13,24,384]{3,2,1,0:T(8,128)(2,1)}, bf16[8,13,24,384]{3,2,1,0:T(8,128)(2,1)S(1)}, u32[]{:S(2)}, u32[]{:S(2)}) collective-permute-start(bf16[8,13,24,384]{3,2,1,0:T(8,128)(2,1)} %get-tuple-element.106), channel_id=1, source_target_pairs={{0,1},{1,0},{2,3},{3,2},{4,5},{5,4},{6,7},{7,6},{8,9},{9,8},{10,11... | collective-permute-start | bytes 5750792 | tf_op jit(solution)/shard_map/ppermute | solution.py:658
  151.6 27.5 %collective-permute-start.13 = (bf16[4,13,24,384]{3,2,1,0:T(8,128)(2,1)S(1)}, bf16[4,13,24,384]{3,2,1,0:T(8,128)(2,1)S(1)}, u32[]{:S(2)}, u32[]{:S(2)}) collective-permute-start(bf16[4,13,24,384]{3,2,1,0:T(8,128)(2,1)S(1)} %add_convert_fusion), channel_id=1, source_target_pairs={{0,2},{1,3},{2,0},{3,1},{4,6},{5,7},{6,4},{7,5},{8,10},{9,11},{10,... | collective-permute-start | bytes 2875400 | tf_op jit(solution)/shard_map/ppermute | solution.py:658
  179.2 5.5 %collective-permute-start.14 = (bf16[8,9,24,384]{3,2,1,0:T(8,128)(2,1)}, bf16[8,9,24,384]{3,2,1,0:T(8,128)(2,1)S(1)}, u32[]{:S(2)}, u32[]{:S(2)}) collective-permute-start(bf16[8,9,24,384]{3,2,1,0:T(8,128)(2,1)} %get-tuple-element.119), channel_id=1, source_target_pairs={{0,1},{1,0},{2,3},{3,2},{4,5},{5,4},{6,7},{7,6},{8,9},{9,8},{10,11... | collective-permute-start | bytes 3981320 | tf_op jit(solution)/shard_map/ppermute | solution.py:658
  180.3 23.2 %collective-permute-start.18 = (bf16[13,24,384]{2,1,0:T(8,128)(2,1)}, bf16[13,24,384]{2,1,0:T(8,128)(2,1)}, u32[]{:S(2)}, u32[]{:S(2)}) collective-permute-start(bf16[13,24,384]{2,1,0:T(8,128)(2,1)} %get-tuple-element.156), channel_id=1, source_target_pairs={{0,12},{1,13},{2,14},{3,15},{4,8},{5,9},{6,10},{7,11},{8,4},{9,5},... | collective-permute-start | bytes 718856 | tf_op jit(solution)/shard_map/ppermute | solution.py:658
  182.6 20.9 %collective-permute-start.17 = (bf16[13,24,384]{2,1,0:T(8,128)(2,1)}, bf16[13,24,384]{2,1,0:T(8,128)(2,1)}, u32[]{:S(2)}, u32[]{:S(2)}) collective-permute-start(bf16[13,24,384]{2,1,0:T(8,128)(2,1)} %get-tuple-element.157), channel_id=1, source_target_pairs={{0,4},{1,5},{2,6},{3,7},{4,0},{5,1},{6,2},{7,3},{8,12},{9,13},{10,... | collective-permute-start | bytes 718856 | tf_op jit(solution)/shard_map/ppermute | solution.py:658
  182.6 21.4 %collective-permute-start.16 = (bf16[13,24,384]{2,1,0:T(8,128)(2,1)}, bf16[13,24,384]{2,1,0:T(8,128)(2,1)}, u32[]{:S(2)}, u32[]{:S(2)}) collective-permute-start(bf16[13,24,384]{2,1,0:T(8,128)(2,1)} %get-tuple-element.158), channel_id=1, source_target_pairs={{0,8},{1,9},{2,10},{3,11},{4,12},{5,13},{6,14},{7,15},{8,0},{9,1},... | collective-permute-start | bytes 718856 | tf_op jit(solution)/shard_map/ppermute | solution.py:658
  184.9 19.1 %collective-permute-start.15 = (bf16[4,9,24,384]{3,2,1,0:T(8,128)(2,1)S(1)}, bf16[4,9,24,384]{3,2,1,0:T(8,128)(2,1)S(1)}, u32[]{:S(2)}, u32[]{:S(2)}) collective-permute-start(bf16[4,9,24,384]{3,2,1,0:T(8,128)(2,1)S(1)} %add_convert_fusion.1), channel_id=1, source_target_pairs={{0,2},{1,3},{2,0},{3,1},{4,6},{5,7},{6,4},{7,5},{8,10},{9,11},{10,... | collective-permute-start | bytes 1990664 | tf_op jit(solution)/shard_map/ppermute | solution.py:658
  204.2 10.3 %collective-permute-start.21 = (bf16[2,9,24,384]{3,2,1,0:T(8,128)(2,1)S(1)}, bf16[2,9,24,384]{3,2,1,0:T(8,128)(2,1)S(1)}, u32[]{:S(2)}, u32[]{:S(2)}) collective-permute-start(bf16[2,9,24,384]{3,2,1,0:T(8,128)(2,1)S(1)} %add_convert_fusion.2), channel_id=1, source_target_pairs={{0,4},{1,5},{2,6},{3,7},{4,0},{5,1},{6,2},{7,3},{8,12},{9,13},{10,... | collective-permute-start | bytes 995336 | tf_op jit(solution)/shard_map/ppermute | solution.py:658
  206.3 9.1 %collective-permute-start.20 = (bf16[4,4,24,384]{3,2,1,0:T(8,128)(2,1)S(1)}, bf16[4,4,24,384]{3,2,1,0:T(8,128)(2,1)S(1)}, u32[]{:S(2)}, u32[]{:S(2)}) collective-permute-start(bf16[4,4,24,384]{3,2,1,0:T(8,128)(2,1)S(1)} %add_convert_fusion.3), channel_id=1, source_target_pairs={{0,2},{1,3},{2,0},{3,1},{4,6},{5,7},{6,4},{7,5},{8,10},{9,11},{10,... | collective-permute-start | bytes 884744 | tf_op jit(solution)/shard_map/ppermute | solution.py:658
  215.5 9.8 %collective-permute-start.22 = (bf16[2,4,24,384]{3,2,1,0:T(8,128)(2,1)S(1)}, bf16[2,4,24,384]{3,2,1,0:T(8,128)(2,1)S(1)}, u32[]{:S(2)}, u32[]{:S(2)}) collective-permute-start(bf16[2,4,24,384]{3,2,1,0:T(8,128)(2,1)S(1)} %add_convert_fusion.9), channel_id=1, source_target_pairs={{0,4},{1,5},{2,6},{3,7},{4,0},{5,1},{6,2},{7,3},{8,12},{9,13},{10,... | collective-permute-start | bytes 442376 | tf_op jit(solution)/shard_map/ppermute | solution.py:658
  217.2 9.8 %collective-permute-start.23 = (bf16[1,9,24,384]{3,2,1,0:T(8,128)(2,1)S(1)}, bf16[1,9,24,384]{3,2,1,0:T(8,128)(2,1)S(1)}, u32[]{:S(2)}, u32[]{:S(2)}) collective-permute-start(bf16[1,9,24,384]{3,2,1,0:T(8,128)(2,1)S(1)} %add_convert_fusion.8), channel_id=1, source_target_pairs={{0,8},{1,9},{2,10},{3,11},{4,12},{5,13},{6,14},{7,15},{8,0},{9,1},... | collective-permute-start | bytes 497672 | tf_op jit(solution)/shard_map/ppermute | solution.py:658
  218.6 15.6 %collective-permute-start.27 = (bf16[13,24,384]{2,1,0:T(8,128)(2,1)S(1)}, bf16[13,24,384]{2,1,0:T(8,128)(2,1)S(1)}, u32[]{:S(2)}, u32[]{:S(2)}) collective-permute-start(bf16[13,24,384]{2,1,0:T(8,128)(2,1)S(1)} %fusion.2.refs_4_), channel_id=1, source_target_pairs={{0,16},{16,0},{1,17},{17,1},{2,18},{18,2},{3,19},{19,3},{4,20},{20... | collective-permute-start | bytes 718856 | tf_op jit(solution)/shard_map/ppermute | solution.py:733
  227.1 5.4 %collective-permute-start.24 = (bf16[1,4,24,384]{3,2,1,0:T(8,128)(2,1)S(1)}, bf16[1,4,24,384]{3,2,1,0:T(8,128)(2,1)S(1)}, u32[]{:S(2)}, u32[]{:S(2)}) collective-permute-start(bf16[1,4,24,384]{3,2,1,0:T(8,128)(2,1)S(1)} %add_convert_fusion.11), channel_id=1, source_target_pairs={{0,8},{1,9},{2,10},{3,11},{4,12},{5,13},{6,14},{7,15},{8,0},{9,1},... | collective-permute-start | bytes 221192 | tf_op jit(solution)/shard_map/ppermute | solution.py:658
  227.3 9.7 %collective-permute-start.26 = (bf16[9,24,384]{2,1,0:T(8,128)(2,1)S(1)}, bf16[9,24,384]{2,1,0:T(8,128)(2,1)S(1)}, u32[]{:S(2)}, u32[]{:S(2)}) collective-permute-start(bf16[9,24,384]{2,1,0:T(8,128)(2,1)S(1)} %fusion.6.refs_2_), channel_id=1, source_target_pairs={{0,16},{16,0},{1,17},{17,1},{2,18},{18,2},{3,19},{19,3},{4,20},{20... | collective-permute-start | bytes 497672 | tf_op jit(solution)/shard_map/ppermute | solution.py:733
  232.5 4.4 %collective-permute-start.25 = (bf16[4,24,384]{2,1,0:T(8,128)(2,1)S(1)}, bf16[4,24,384]{2,1,0:T(8,128)(2,1)S(1)}, u32[]{:S(2)}, u32[]{:S(2)}) collective-permute-start(bf16[4,24,384]{2,1,0:T(8,128)(2,1)S(1)} %fusion.7.refs_0_), channel_id=1, source_target_pairs={{0,16},{16,0},{1,17},{17,1},{2,18},{18,2},{3,19},{19,3},{4,20},{20... | collective-permute-start | bytes 221192 | tf_op jit(solution)/shard_map/ppermute | solution.py:733
  (21 other events, 123.3 us)
